TPU v7x, 32 devices: a whole 2x2x4 slice. The times are simulated.
32 devices in a mesh: rep: 4 (over x, core), fsdp: 8 (over z, y).
Axes of the slice: x: 2, y: 2, z: 4, core: 2. Of those that a mesh axis runs over, the one named last changes fastest.
Arguments:
- hidden_in: bfloat16 [4096, 2048], P(('rep', 'fsdp')), may hold values from -6 to 6
- layer_input: bfloat16 [4096, 256], P(('rep', 'fsdp')), may hold values from -6 to 6
- out_grad: bfloat16 [4096, 2048], P(('rep', 'fsdp')), may hold values from -6 to 6
- seg_lengths: int32 [4, 13], P('rep'), may hold values from 1 to 409, 1024 in all within a row
- seg_parents: int32 [4, 13], P('rep'), may hold values from 0 to 11, as said below
- attn_norm: bfloat16 [2048], P('fsdp'), may hold values from 0.25 to 1.75
- q_proj: bfloat16 [2048, 2048], P('fsdp'), may hold values from -0.125 to 0.125
- k_proj: bfloat16 [2048, 512], P('fsdp'), may hold values from -0.125 to 0.125
- v_proj: bfloat16 [2048, 512], P('fsdp'), may hold values from -0.125 to 0.125
- q_norm: bfloat16 [256], P('fsdp'), may hold values from 0.25 to 1.75
- k_norm: bfloat16 [256], P('fsdp'), may hold values from 0.25 to 1.75
- o_proj: bfloat16 [2048, 2048], P('fsdp'), may hold values from -0.125 to 0.125
- attn_post_norm: bfloat16 [2048], P('fsdp'), may hold values from 0.25 to 1.75
- laurel_left: bfloat16 [2048, 64], P('fsdp'), may hold values from -0.125 to 0.125
- laurel_right: bfloat16 [2048, 64], P('fsdp'), may hold values from -0.75 to 0.75
- laurel_norm: bfloat16 [2048], P('fsdp'), may hold values from 0.25 to 1.75
- ffw_norm: bfloat16 [2048], P('fsdp'), may hold values from 0.25 to 1.75
- gate_proj: bfloat16 [8192, 2048], P('fsdp'), may hold values from -0.125 to 0.125
- up_proj: bfloat16 [8192, 2048], P('fsdp'), may hold values from -0.125 to 0.125
- down_proj: bfloat16 [8192, 2048], P('fsdp'), may hold values from -0.0625 to 0.0625
- ffw_post_norm: bfloat16 [2048], P('fsdp'), may hold values from 0.25 to 1.75
- pl_gate: bfloat16 [2048, 256], P('fsdp'), may hold values from -0.125 to 0.125
- pl_proj: bfloat16 [256, 2048], P('fsdp'), may hold values from -0.375 to 0.375
- pl_post_norm: bfloat16 [2048], P('fsdp'), may hold values from 0.25 to 1.75
Outputs:
- layer_out: bfloat16 [4096, 2048], P(('rep', 'fsdp'))
- input_grad: bfloat16 [4096, 2048], P(('rep', 'fsdp'))
- layer_input_grad: bfloat16 [4096, 256], P(('rep', 'fsdp'))
- attn_norm_grad: float32 [2048], P('fsdp')
- q_proj_grad: float32 [2048, 2048], P('fsdp')
- k_proj_grad: float32 [2048, 512], P('fsdp')
- v_proj_grad: float32 [2048, 512], P('fsdp')
- q_norm_grad: float32 [256], P('fsdp')
- k_norm_grad: float32 [256], P('fsdp')
- o_proj_grad: float32 [2048, 2048], P('fsdp')
- attn_post_norm_grad: float32 [2048], P('fsdp')
- laurel_left_grad: float32 [2048, 64], P('fsdp')
- laurel_right_grad: float32 [2048, 64], P('fsdp')
- laurel_norm_grad: float32 [2048], P('fsdp')
- ffw_norm_grad: float32 [2048], P('fsdp')
- gate_proj_grad: float32 [8192, 2048], P('fsdp')
- up_proj_grad: float32 [8192, 2048], P('fsdp')
- down_proj_grad: float32 [8192, 2048], P('fsdp')
- ffw_post_norm_grad: float32 [2048], P('fsdp')
- pl_gate_grad: float32 [2048, 256], P('fsdp')
- pl_proj_grad: float32 [256, 2048], P('fsdp')
- pl_post_norm_grad: float32 [2048], P('fsdp')
Inputs may be any that keep to these rules, and one draw needn't show every extreme that they name: Row r describes the tree of replica group r: segment s covers the next seg_lengths[r, s] of that group's 1024 tokens, in order; each row sums to 1024. seg_parents[r, 0] is 0 and marks the root; for s >= 1, seg_parents[r, s] is a segment below s.
All inputs are finite; a program needn't handle non-finite values.
Results may differ from a plain program's by a relative error of at most 0.025.
Values may be sent and summed in bfloat16 or wider, within the bound.
A program may use at most 704 MiB of HBM per device.

v0:
```python
import math

import jax
import jax.numpy as jnp
from jax import lax
from jax.sharding import PartitionSpec as P

HEADS = 8
KV_HEADS = 2
HEAD_DIM = 256


EPS = 1e-06
ROPE_BASE = 1000000.0
HALF_ROOT = 0.7071067811865476
MASKED = -1e30


def norm_rows(value, gain):
    return value * lax.rsqrt(jnp.mean(value * value, axis=-1, keepdims=True) + EPS) * gain


def norm_back(value, gain, grad):
    unused, pull = jax.vjp(norm_rows, value, gain)
    return pull(grad)


def rotate(value, position):
    half = value.shape[-1] // 2
    freqs = jnp.exp(
        jnp.arange(half, dtype=jnp.float32) * (-2.0 * math.log(ROPE_BASE) / value.shape[-1])
    )
    angle = position[:, None] * freqs[None, :]
    cosine = jnp.cos(angle)[:, None, :]
    sine = jnp.sin(angle)[:, None, :]
    first_half = value[..., :half]
    second_half = value[..., half:]
    return jnp.concatenate(
        [first_half * cosine - second_half * sine, second_half * cosine + first_half * sine],
        axis=-1,
    )


def tree_tables(lengths, parents, total):
    count = lengths.shape[0]
    labels = jnp.arange(count, dtype=jnp.int32)
    ends = jnp.cumsum(lengths)
    starts = ends - lengths
    tokens = jnp.arange(total, dtype=jnp.int32)
    segment = jnp.sum((ends[None, :] <= tokens[:, None]).astype(jnp.int32), axis=1)
    parent_hot = ((parents[:, None] == labels[None, :]) & (labels[:, None] > 0)).astype(jnp.int32)
    identity = (labels[:, None] == labels[None, :]).astype(jnp.int32)
    ancestors = lax.fori_loop(
        0, count, lambda step, held: jnp.minimum(1, identity + jnp.dot(parent_hot, held)), identity
    )
    offset = jnp.dot(ancestors - identity, lengths) - starts
    member = (segment[:, None] == labels[None, :]).astype(jnp.int32)
    reach = jnp.dot(member, ancestors)
    position = jnp.dot(member, offset) + tokens
    return (tokens, member, reach, position)


def outer(left, right):
    return lax.dot_general(
        left, right, (((0,), (0,)), ((), ())), preferred_element_type=jnp.float32
    )


def mul_t(left, right):
    return lax.dot_general(
        left, right, (((1,), (1,)), ((), ())), preferred_element_type=jnp.float32
    )


def gelu_mix(first, second):
    return jax.nn.gelu(first, approximate=True) * second


def mix_back(first, second, grad):
    unused, pull = jax.vjp(gelu_mix, first, second)
    return pull(grad)


def per_device(
    hidden_in,
    layer_input,
    out_grad,
    seg_lengths,
    seg_parents,
    attn_norm,
    q_proj,
    k_proj,
    v_proj,
    q_norm,
    k_norm,
    o_proj,
    attn_post_norm,
    laurel_left,
    laurel_right,
    laurel_norm,
    ffw_norm,
    gate_proj,
    up_proj,
    down_proj,
    ffw_post_norm,
    pl_gate,
    pl_proj,
    pl_post_norm,
):
    shards = lax.axis_size("fsdp")
    rank_index = lax.axis_index("fsdp")
    rows = hidden_in.shape[0]
    total = rows * shards
    groups = HEADS // KV_HEADS
    scale = HEAD_DIM ** (-0.5)
    tokens, member, reach, position = tree_tables(seg_lengths[0], seg_parents[0], total)
    first_row = rank_index * rows
    my_tokens = first_row + jnp.arange(rows, dtype=jnp.int32)
    my_reach = lax.dynamic_slice_in_dim(reach, first_row, rows, 0)
    my_depth = lax.dynamic_slice_in_dim(position, first_row, rows, 0).astype(jnp.float32)
    seen = (jnp.dot(my_reach, member.T) > 0) & (tokens[None, :] <= my_tokens[:, None])
    (
        full_anorm,
        full_q,
        full_k,
        full_v,
        full_qnorm,
        full_knorm,
        full_o,
        full_apost,
        full_left,
        full_right,
        full_lnorm,
        full_fnorm,
        full_fpost,
        full_plgate,
        full_plproj,
        full_plpost,
    ) = (
        lax.all_gather(attn_norm, "fsdp", axis=0, tiled=True),
        lax.all_gather(q_proj, "fsdp", axis=0, tiled=True),
        lax.all_gather(k_proj, "fsdp", axis=0, tiled=True),
        lax.all_gather(v_proj, "fsdp", axis=0, tiled=True),
        lax.all_gather(q_norm, "fsdp", axis=0, tiled=True),
        lax.all_gather(k_norm, "fsdp", axis=0, tiled=True),
        lax.all_gather(o_proj, "fsdp", axis=0, tiled=True),
        lax.all_gather(attn_post_norm, "fsdp", axis=0, tiled=True),
        lax.all_gather(laurel_left, "fsdp", axis=0, tiled=True),
        lax.all_gather(laurel_right, "fsdp", axis=0, tiled=True),
        lax.all_gather(laurel_norm, "fsdp", axis=0, tiled=True),
        lax.all_gather(ffw_norm, "fsdp", axis=0, tiled=True),
        lax.all_gather(ffw_post_norm, "fsdp", axis=0, tiled=True),
        lax.all_gather(pl_gate, "fsdp", axis=0, tiled=True),
        lax.all_gather(pl_proj, "fsdp", axis=0, tiled=True),
        lax.all_gather(pl_post_norm, "fsdp", axis=0, tiled=True),
    )
    gain_anorm = full_anorm.astype(jnp.float32)
    gain_qnorm = full_qnorm.astype(jnp.float32)
    gain_knorm = full_knorm.astype(jnp.float32)
    gain_apost = full_apost.astype(jnp.float32)
    gain_lnorm = full_lnorm.astype(jnp.float32)
    gain_fnorm = full_fnorm.astype(jnp.float32)
    gain_fpost = full_fpost.astype(jnp.float32)
    gain_plpost = full_plpost.astype(jnp.float32)
    source = hidden_in.astype(jnp.float32)
    extra = layer_input.astype(jnp.float32)
    normed = norm_rows(source, gain_anorm)
    normed_low = normed.astype(jnp.bfloat16)
    q_raw = jnp.dot(normed_low, full_q, preferred_element_type=jnp.float32)
    k_raw = jnp.dot(normed_low, full_k, preferred_element_type=jnp.float32)
    v_raw = jnp.dot(normed_low, full_v, preferred_element_type=jnp.float32)

    def head_path(raw, gain):
        return rotate(norm_rows(raw.reshape(rows, -1, HEAD_DIM), gain), my_depth)

    q_low = head_path(q_raw, gain_qnorm).astype(jnp.bfloat16)
    k_low = head_path(k_raw, gain_knorm).reshape(rows, -1).astype(jnp.bfloat16)
    v_low = v_raw.astype(jnp.bfloat16)
    keys_all, values_all = (
        lax.all_gather(k_low, "fsdp", axis=0, tiled=True),
        lax.all_gather(v_low, "fsdp", axis=0, tiled=True),
    )
    keys_heads = keys_all.reshape(total, KV_HEADS, HEAD_DIM)
    values_heads = values_all.reshape(total, KV_HEADS, HEAD_DIM)
    query_groups = q_low.reshape(rows, KV_HEADS, groups, HEAD_DIM)
    mixed_list = []
    log_list = []
    for head in range(KV_HEADS):
        scores = (
            jnp.einsum(
                "tgd,nd->gtn",
                query_groups[:, head],
                keys_heads[:, head],
                preferred_element_type=jnp.float32,
            )
            * scale
        )
        scores = jnp.where(seen[None], scores, MASKED)
        top = jnp.max(scores, axis=-1, keepdims=True)
        expo = jnp.exp(scores - top)
        sums = jnp.sum(expo, axis=-1, keepdims=True)
        weights = (expo / sums).astype(jnp.bfloat16)
        mixed_list.append(
            jnp.einsum(
                "gtn,nd->tgd", weights, values_heads[:, head], preferred_element_type=jnp.float32
            )
        )
        log_list.append(top[..., 0] + jnp.log(sums[..., 0]))
    attended = jnp.stack(mixed_list, axis=1)
    log_sums = jnp.stack(log_list, axis=0)
    attended_low = attended.reshape(rows, -1).astype(jnp.bfloat16)
    branch = jnp.dot(attended_low, full_o, preferred_element_type=jnp.float32)
    left_low = jnp.dot(normed_low, full_left, preferred_element_type=jnp.float32).astype(
        jnp.bfloat16
    )
    low_rank = mul_t(left_low, full_right)
    first_sum = (
        source + norm_rows(branch, gain_apost) + normed + norm_rows(low_rank, gain_lnorm)
    ) * HALF_ROOT
    ffw_low = norm_rows(first_sum, gain_fnorm).astype(jnp.bfloat16)
    full_gate, full_up, full_down = (
        lax.all_gather(gate_proj, "fsdp", axis=0, tiled=True),
        lax.all_gather(up_proj, "fsdp", axis=0, tiled=True),
        lax.all_gather(down_proj, "fsdp", axis=0, tiled=True),
    )
    gate_val = mul_t(ffw_low, full_gate)
    up_val = mul_t(ffw_low, full_up)
    inner_low = gelu_mix(gate_val, up_val).astype(jnp.bfloat16)
    ffw_out = jnp.dot(inner_low, full_down, preferred_element_type=jnp.float32)
    second_sum = first_sum + norm_rows(ffw_out, gain_fpost)
    second_low = second_sum.astype(jnp.bfloat16)
    pl_pre = jnp.dot(second_low, full_plgate, preferred_element_type=jnp.float32)
    pl_mix = gelu_mix(pl_pre, extra).astype(jnp.bfloat16)
    pl_out = jnp.dot(pl_mix, full_plproj, preferred_element_type=jnp.float32)
    result = second_sum + norm_rows(pl_out, gain_plpost)
    seed = out_grad.astype(jnp.float32)
    d_plout, grad_plpost = norm_back(pl_out, gain_plpost, seed)
    d_plout_low = d_plout.astype(jnp.bfloat16)
    grad_plproj = outer(pl_mix, d_plout_low)
    d_mix = mul_t(d_plout_low, full_plproj)
    d_pre, d_extra = mix_back(pl_pre, extra, d_mix)
    d_pre_low = d_pre.astype(jnp.bfloat16)
    grad_plgate = outer(second_low, d_pre_low)
    d_second = seed + mul_t(d_pre_low, full_plgate)
    d_ffwout, grad_fpost = norm_back(ffw_out, gain_fpost, d_second)
    d_ffw_low = d_ffwout.astype(jnp.bfloat16)
    d_inner = mul_t(d_ffw_low, full_down)
    d_gate, d_up = mix_back(gate_val, up_val, d_inner)
    d_gate_low = d_gate.astype(jnp.bfloat16)
    d_up_low = d_up.astype(jnp.bfloat16)
    d_ffwin = jnp.dot(d_gate_low, full_gate, preferred_element_type=jnp.float32) + jnp.dot(
        d_up_low, full_up, preferred_element_type=jnp.float32
    )
    width = ffw_low.shape[1]
    gate_part = outer(d_gate_low, ffw_low)
    up_part = outer(d_up_low, ffw_low)
    down_part = outer(inner_low, d_ffw_low)
    stacked = lax.psum_scatter(
        jnp.concatenate([gate_part, up_part, down_part], axis=1).astype(jnp.bfloat16),
        "fsdp",
        scatter_dimension=0,
        tiled=True,
    ).astype(jnp.float32)
    grad_gate = stacked[:, :width]
    grad_up = stacked[:, width : 2 * width]
    grad_down = stacked[:, 2 * width :]
    d_first_part, grad_fnorm = norm_back(first_sum, gain_fnorm, d_ffwin)
    d_first = d_second + d_first_part
    d_scaled = d_first * HALF_ROOT
    d_branch, grad_apost = norm_back(branch, gain_apost, d_scaled)
    d_branch_low = d_branch.astype(jnp.bfloat16)
    d_lowrank, grad_lnorm = norm_back(low_rank, gain_lnorm, d_scaled)
    d_lowrank_low = d_lowrank.astype(jnp.bfloat16)
    grad_o = outer(attended_low, d_branch_low)
    d_att_low = mul_t(d_branch_low, full_o).astype(jnp.bfloat16)
    grad_right = outer(d_lowrank_low, left_low)
    d_left_low = jnp.dot(d_lowrank_low, full_right, preferred_element_type=jnp.float32).astype(
        jnp.bfloat16
    )
    grad_left = outer(normed_low, d_left_low)
    d_att_heads = d_att_low.reshape(rows, KV_HEADS, groups, HEAD_DIM)
    delta = jnp.sum(d_att_heads.astype(jnp.float32) * attended, axis=-1).transpose(1, 2, 0)
    block = 512
    count = total // block
    key_blocks = keys_heads.reshape(count, block, KV_HEADS, HEAD_DIM)
    value_blocks = values_heads.reshape(count, block, KV_HEADS, HEAD_DIM)
    seen_blocks = seen.reshape(rows, count, block).transpose(1, 0, 2)

    def key_step(d_query, item):
        keys, values, shown = item
        scores = (
            jnp.einsum("tkgd,nkd->kgtn", query_groups, keys, preferred_element_type=jnp.float32)
            * scale
        )
        scores = jnp.where(shown[None, None], scores, MASKED)
        probs = jnp.exp(scores - log_sums[..., None])
        d_probs = jnp.einsum(
            "tkgd,nkd->kgtn", d_att_heads, values, preferred_element_type=jnp.float32
        )
        d_scores = (probs * (d_probs - delta[..., None]) * scale).astype(jnp.bfloat16)
        d_query = d_query + jnp.einsum(
            "kgtn,nkd->tkgd", d_scores, keys, preferred_element_type=jnp.float32
        )
        d_keys = jnp.einsum(
            "kgtn,tkgd->nkd", d_scores, query_groups, preferred_element_type=jnp.float32
        )
        d_values = jnp.einsum(
            "kgtn,tkgd->nkd",
            probs.astype(jnp.bfloat16),
            d_att_heads,
            preferred_element_type=jnp.float32,
        )
        return (d_query, (d_keys, d_values))

    zero_query = jnp.zeros((rows, KV_HEADS, groups, HEAD_DIM), jnp.float32)
    d_query, (d_key_blocks, d_value_blocks) = lax.scan(
        key_step, zero_query, (key_blocks, value_blocks, seen_blocks)
    )
    my_dkeys, my_dvalues = (
        lax.psum_scatter(
            d_key_blocks.reshape(total, -1).astype(jnp.bfloat16),
            "fsdp",
            scatter_dimension=0,
            tiled=True,
        ).astype(jnp.float32),
        lax.psum_scatter(
            d_value_blocks.reshape(total, -1).astype(jnp.bfloat16),
            "fsdp",
            scatter_dimension=0,
            tiled=True,
        ).astype(jnp.float32),
    )
    unused_q, q_pull = jax.vjp(head_path, q_raw, gain_qnorm)
    d_qraw, grad_qnorm = q_pull(d_query.reshape(rows, HEADS, HEAD_DIM))
    unused_k, k_pull = jax.vjp(head_path, k_raw, gain_knorm)
    d_kraw, grad_knorm = k_pull(my_dkeys.reshape(rows, KV_HEADS, HEAD_DIM))
    d_q_low = d_qraw.astype(jnp.bfloat16)
    d_k_low = d_kraw.astype(jnp.bfloat16)
    d_v_low = my_dvalues.astype(jnp.bfloat16)
    grad_q = outer(normed_low, d_q_low)
    grad_k = outer(normed_low, d_k_low)
    grad_v = outer(normed_low, d_v_low)
    d_normed = (
        d_scaled
        + mul_t(d_q_low, full_q)
        + mul_t(d_k_low, full_k)
        + mul_t(d_v_low, full_v)
        + mul_t(d_left_low, full_left)
    )
    d_source_part, grad_anorm = norm_back(source, gain_anorm, d_normed)
    d_source = d_scaled + d_source_part
    shard_grads = (
        lax.psum_scatter(
            grad_anorm.astype(jnp.bfloat16), "fsdp", scatter_dimension=0, tiled=True
        ).astype(jnp.float32),
        lax.psum_scatter(
            grad_q.astype(jnp.bfloat16), "fsdp", scatter_dimension=0, tiled=True
        ).astype(jnp.float32),
        lax.psum_scatter(
            grad_k.astype(jnp.bfloat16), "fsdp", scatter_dimension=0, tiled=True
        ).astype(jnp.float32),
        lax.psum_scatter(
            grad_v.astype(jnp.bfloat16), "fsdp", scatter_dimension=0, tiled=True
        ).astype(jnp.float32),
        lax.psum_scatter(
            grad_qnorm.astype(jnp.bfloat16), "fsdp", scatter_dimension=0, tiled=True
        ).astype(jnp.float32),
        lax.psum_scatter(
            grad_knorm.astype(jnp.bfloat16), "fsdp", scatter_dimension=0, tiled=True
        ).astype(jnp.float32),
        lax.psum_scatter(
            grad_o.astype(jnp.bfloat16), "fsdp", scatter_dimension=0, tiled=True
        ).astype(jnp.float32),
        lax.psum_scatter(
            grad_apost.astype(jnp.bfloat16), "fsdp", scatter_dimension=0, tiled=True
        ).astype(jnp.float32),
        lax.psum_scatter(
            grad_left.astype(jnp.bfloat16), "fsdp", scatter_dimension=0, tiled=True
        ).astype(jnp.float32),
        lax.psum_scatter(
            grad_right.astype(jnp.bfloat16), "fsdp", scatter_dimension=0, tiled=True
        ).astype(jnp.float32),
        lax.psum_scatter(
            grad_lnorm.astype(jnp.bfloat16), "fsdp", scatter_dimension=0, tiled=True
        ).astype(jnp.float32),
        lax.psum_scatter(
            grad_fnorm.astype(jnp.bfloat16), "fsdp", scatter_dimension=0, tiled=True
        ).astype(jnp.float32),
        lax.psum_scatter(
            grad_fpost.astype(jnp.bfloat16), "fsdp", scatter_dimension=0, tiled=True
        ).astype(jnp.float32),
        lax.psum_scatter(
            grad_plgate.astype(jnp.bfloat16), "fsdp", scatter_dimension=0, tiled=True
        ).astype(jnp.float32),
        lax.psum_scatter(
            grad_plproj.astype(jnp.bfloat16), "fsdp", scatter_dimension=0, tiled=True
        ).astype(jnp.float32),
        lax.psum_scatter(
            grad_plpost.astype(jnp.bfloat16), "fsdp", scatter_dimension=0, tiled=True
        ).astype(jnp.float32),
    )
    (
        sum_anorm,
        sum_q,
        sum_k,
        sum_v,
        sum_qnorm,
        sum_knorm,
        sum_o,
        sum_apost,
        sum_left,
        sum_right,
        sum_lnorm,
        sum_fnorm,
        sum_fpost,
        sum_plgate,
        sum_plproj,
        sum_plpost,
        sum_gate,
        sum_up,
        sum_down,
    ) = (
        lax.psum(shard_grads[0].astype(jnp.bfloat16), "rep").astype(jnp.float32),
        lax.psum(shard_grads[1].astype(jnp.bfloat16), "rep").astype(jnp.float32),
        lax.psum(shard_grads[2].astype(jnp.bfloat16), "rep").astype(jnp.float32),
        lax.psum(shard_grads[3].astype(jnp.bfloat16), "rep").astype(jnp.float32),
        lax.psum(shard_grads[4].astype(jnp.bfloat16), "rep").astype(jnp.float32),
        lax.psum(shard_grads[5].astype(jnp.bfloat16), "rep").astype(jnp.float32),
        lax.psum(shard_grads[6].astype(jnp.bfloat16), "rep").astype(jnp.float32),
        lax.psum(shard_grads[7].astype(jnp.bfloat16), "rep").astype(jnp.float32),
        lax.psum(shard_grads[8].astype(jnp.bfloat16), "rep").astype(jnp.float32),
        lax.psum(shard_grads[9].astype(jnp.bfloat16), "rep").astype(jnp.float32),
        lax.psum(shard_grads[10].astype(jnp.bfloat16), "rep").astype(jnp.float32),
        lax.psum(shard_grads[11].astype(jnp.bfloat16), "rep").astype(jnp.float32),
        lax.psum(shard_grads[12].astype(jnp.bfloat16), "rep").astype(jnp.float32),
        lax.psum(shard_grads[13].astype(jnp.bfloat16), "rep").astype(jnp.float32),
        lax.psum(shard_grads[14].astype(jnp.bfloat16), "rep").astype(jnp.float32),
        lax.psum(shard_grads[15].astype(jnp.bfloat16), "rep").astype(jnp.float32),
        lax.psum(grad_gate.astype(jnp.bfloat16), "rep").astype(jnp.float32),
        lax.psum(grad_up.astype(jnp.bfloat16), "rep").astype(jnp.float32),
        lax.psum(grad_down.astype(jnp.bfloat16), "rep").astype(jnp.float32),
    )
    return (
        result.astype(jnp.bfloat16),
        d_source.astype(jnp.bfloat16),
        d_extra.astype(jnp.bfloat16),
        sum_anorm,
        sum_q,
        sum_k,
        sum_v,
        sum_qnorm,
        sum_knorm,
        sum_o,
        sum_apost,
        sum_left,
        sum_right,
        sum_lnorm,
        sum_fnorm,
        sum_gate,
        sum_up,
        sum_down,
        sum_fpost,
        sum_plgate,
        sum_plproj,
        sum_plpost,
    )


def solution(mesh):
    placed = (
        P(("rep", "fsdp"), None),
        P(("rep", "fsdp"), None),
        P(("rep", "fsdp"), None),
        P("rep", None),
        P("rep", None),
        P("fsdp"),
        P("fsdp", None),
        P("fsdp", None),
        P("fsdp", None),
        P("fsdp"),
        P("fsdp"),
        P("fsdp", None),
        P("fsdp"),
        P("fsdp", None),
        P("fsdp", None),
        P("fsdp"),
        P("fsdp"),
        P("fsdp", None),
        P("fsdp", None),
        P("fsdp", None),
        P("fsdp"),
        P("fsdp", None),
        P("fsdp", None),
        P("fsdp"),
    )
    return jax.shard_map(
        per_device,
        mesh=mesh,
        in_specs=placed,
        out_specs=(
            P(("rep", "fsdp"), None),
            P(("rep", "fsdp"), None),
            P(("rep", "fsdp"), None),
            P("fsdp"),
            P("fsdp", None),
            P("fsdp", None),
            P("fsdp", None),
            P("fsdp"),
            P("fsdp"),
            P("fsdp", None),
            P("fsdp"),
            P("fsdp", None),
            P("fsdp", None),
            P("fsdp"),
            P("fsdp"),
            P("fsdp", None),
            P("fsdp", None),
            P("fsdp", None),
            P("fsdp"),
            P("fsdp", None),
            P("fsdp", None),
            P("fsdp"),
        ),
        check_vma=False,
    )
```

profile of v0, /device:TPU:0, one launch (start us, length us, event | category | flops | bytes accessed | tf_op | source)
XLA Modules:
  0.0 5272.3 jit_solution(13606260073701760084)
XLA Ops:
  24.9 23.4 all-reduce.15
  73.0 39.4 all-gather.18.cloned.1.call-done
  120.8 18.1 all-gather.5
  155.5 17.9 all-gather.3
  173.5 16.6 all-gather.2
  190.1 18.0 all-gather.1
  209.1 32.0 all_gather.73
  241.6 32.5 all_gather.74
  283.8 41.3 all-gather.26.cloned.1.call-done
  335.5 115.0 %all-gather.28.cloned.1.call-done = bf16[2048,2048]{1,0:T(8,128)(2,1)} async-done(((bf16[256,2048]{1,0:T(8,128)(2,1)}), bf16[2048,2048]{1,0:T(8,128)(2,1)}) %all-gather.28.cloned.1.call-update) | async-done | bytes 8388624 | tf_op jit(solution)/shard_map/all_gather | solution.py:146
  456.5 631.5 %all-gather.30.cloned.1.call-done = bf16[8192,2048]{1,0:T(8,128)(2,1)} async-done(((bf16[1024,2048]{1,0:T(8,128)(2,1)}), bf16[8192,2048]{1,0:T(8,128)(2,1)}) %all-gather.30.cloned.1.call-update) | async-done | bytes 33554448 | tf_op jit(solution)/shard_map/all_gather | solution.py:222
  1088.0 18.5 fusion.121
  1106.5 620.8 %all-gather.32.cloned.1.call-done = bf16[8192,2048]{1,0:T(8,128)(2,1)} async-done(((bf16[1024,2048]{1,0:T(8,128)(2,1)}), bf16[8192,2048]{1,0:T(8,128)(2,1)}) %all-gather.32.cloned.1.call-update) | async-done | bytes 33554448 | tf_op jit(solution)/shard_map/all_gather | solution.py:223
  1727.2 20.6 multiply_convert_fusion.1
  1747.9 618.7 %all-gather.34.cloned.1.call-done = bf16[8192,2048]{1,0:T(8,128)(2,1)} async-done(((bf16[1024,2048]{1,0:T(8,128)(2,1)}), bf16[8192,2048]{1,0:T(8,128)(2,1)}) %all-gather.34.cloned.1.call-update) | async-done | bytes 33554448 | tf_op jit(solution)/shard_map/all_gather | solution.py:224
  2382.4 26.2 all-gather.36.cloned.1.call-done
  2410.5 39.2 all-gather.38.cloned.1.call-done
  2457.1 20.8 multiply_convert_fusion
  2477.9 16.8 fusion.122
  2494.7 17.4 multiply_reduce_fusion.1
  2595.0 67.8 %pad_maximum_fusion = bf16[8192,6144]{0,1:T(8,128)(2,1)} fusion(bf16[8192,2048]{0,1:T(8,128)(2,1)} %convolution_convert_fusion, bf16[8192,2048]{0,1:T(8,128)(2,1)} %convolution_convert_fusion.1, bf16[8192,2048]{0,1:T(8,128)(2,1)} %convolution_convert_fusion.2), kind=kLoop, calls=%fused_computation.33 | loop fusion | flops 301989888 | bytes 201326592 | tf_op jit(solution)/shard_map/concatenate | solution.py:259
  2707.6 35.3 all-reduce.14
  2747.6 54.2 %reduce-scatter.24.cloned.1.call-done = bf16[256,64]{0,1:T(8,128)(2,1)} async-done(((bf16[2048,64]{0,1:T(8,128)(2,1)}), bf16[256,64]{0,1:T(8,128)(2,1)}) %reduce-scatter.24.cloned.1.call-update) | async-done | bytes 32784 | tf_op jit(solution)/shard_map/reduce_scatter | solution.py:377
  2801.8 1540.9 %reduce-scatter.28.cloned.1.call-done = bf16[1024,6144]{0,1:T(8,128)(2,1)} async-done(((bf16[8192,6144]{0,1:T(8,128)(2,1)}), bf16[1024,6144]{0,1:T(8,128)(2,1)}) %reduce-scatter.28.cloned.1.call-update) | async-done | bytes 12582928 | tf_op jit(solution)/shard_map/reduce_scatter | solution.py:258
  4351.9 57.1 %reduce-scatter.30.cloned.1.call-done = bf16[256,256]{1,0:T(8,128)(2,1)} async-done(((bf16[2048,256]{1,0:T(8,128)(2,1)}), bf16[256,256]{1,0:T(8,128)(2,1)}) %reduce-scatter.30.cloned.1.call-update) | async-done | bytes 131088 | tf_op jit(solution)/shard_map/reduce_scatter | solution.py:392
  4409.0 65.6 %reduce-scatter.32.cloned.1.call-done = bf16[32,2048]{1,0:T(8,128)(2,1)} async-done(((bf16[256,2048]{1,0:T(8,128)(2,1)}), bf16[32,2048]{1,0:T(8,128)(2,1)}) %reduce-scatter.32.cloned.1.call-update) | async-done | bytes 131088 | tf_op jit(solution)/shard_map/reduce_scatter | solution.py:395
  4474.6 71.5 %reduce-scatter.20.cloned.1.call-done = bf16[256,512]{1,0:T(8,128)(2,1)} async-done(((bf16[2048,512]{1,0:T(8,128)(2,1)}), bf16[256,512]{1,0:T(8,128)(2,1)}) %reduce-scatter.20.cloned.1.call-update) | async-done | bytes 262160 | tf_op jit(solution)/shard_map/reduce_scatter | solution.py:362
  4546.1 71.2 %reduce-scatter.18.cloned.1.call-done = bf16[256,512]{1,0:T(8,128)(2,1)} async-done(((bf16[2048,512]{1,0:T(8,128)(2,1)}), bf16[256,512]{1,0:T(8,128)(2,1)}) %reduce-scatter.18.cloned.1.call-update) | async-done | bytes 262160 | tf_op jit(solution)/shard_map/reduce_scatter | solution.py:359
  4617.3 152.7 %reduce-scatter.16.cloned.1.call-done = bf16[256,2048]{1,0:T(8,128)(2,1)} async-done(((bf16[2048,2048]{1,0:T(8,128)(2,1)}), bf16[256,2048]{1,0:T(8,128)(2,1)}) %reduce-scatter.16.cloned.1.call-update) | async-done | bytes 1048592 | tf_op jit(solution)/shard_map/reduce_scatter | solution.py:356
  4770.0 152.2 %reduce-scatter.22.cloned.1.call-done = bf16[256,2048]{1,0:T(8,128)(2,1)} async-done(((bf16[2048,2048]{1,0:T(8,128)(2,1)}), bf16[256,2048]{1,0:T(8,128)(2,1)}) %reduce-scatter.22.cloned.1.call-update) | async-done | bytes 1048592 | tf_op jit(solution)/shard_map/reduce_scatter | solution.py:371
  4924.1 32.8 all-reduce.21.cloned.1.call-done
  4969.3 263.3 %all-reduce.23.cloned.1.call-done = (bf16[1024,2048]{0,1:T(8,128)(2,1)}, bf16[1024,2048]{0,1:T(8,128)(2,1)}, bf16[1024,2048]{0,1:T(8,128)(2,1)}, bf16[256,2048]{...) async-done(((bf16[1024,2048]{0,1:T(8,128)(2,1)}, ...) | async-done | bytes 15466512 | tf_op jit(solution)/shard_map/psum | solution.py:439
  (469 shorter events, 326.8 us)
Async XLA Ops:
  7.2 61.3 %all-gather.22.cloned.1.call-start = ((), (), s32[]{:S(2)}) async-start(), calls=%async_computation.13 | async-start | bytes 2359296 | tf_op jit(solution)/shard_map/all_gather | solution.py:142
  7.9 104.5 %all-gather.18.cloned.1.call-start = ((), (), s32[]{:S(2)}) async-start(), calls=%async_computation.11 | async-start | bytes 2359296 | tf_op jit(solution)/shard_map/all_gather | solution.py:143
  8.7 266.7 %all-gather.24.cloned.1.call-start = ((), (), s32[]{:S(2)}) async-start(), calls=%async_computation.14 | async-start | bytes 1179648 | tf_op jit(solution)/shard_map/all_gather | solution.py:180
  65.5 389.9 %copy-start.45 = (f32[8,1,256]{2,1,0:T(1,128)}, f32[8,1,256]{2,1,0:T(1,128)S(1)}, u32[]{:S(2)}) copy-start(f32[8,1,256]{2,1,0:T(1,128)S(1)} %convert_element_type.386) | copy-start | bytes 24580
  68.2 387.2 %copy-start.71 = (f32[128]{0:T(128)}, f32[128]{0:T(128)S(1)}, u32[]{:S(2)}) copy-start(f32[128]{0:T(128)S(1)} %fusion.90) | copy-start | bytes 1540
  68.5 262.3 %copy-start.41 = (f32[128,128]{1,0:T(8,128)}, f32[128,128]{1,0:T(8,128)S(1)}, u32[]{:S(2)}) copy-start(f32[128,128]{1,0:T(8,128)S(1)} %get-tuple-element.455) | copy-start | bytes 196612
  68.5 262.3 %copy-start.43 = (f32[128,128]{1,0:T(8,128)}, f32[128,128]{1,0:T(8,128)S(1)}, u32[]{:S(2)}) copy-start(f32[128,128]{1,0:T(8,128)S(1)} %get-tuple-element.456) | copy-start | bytes 196612
  73.0 206.4 %all-gather.20.cloned.1.call-start = ((), (), s32[]{:S(2)}) async-start(), calls=%async_computation.12 | async-start | bytes 1179648 | tf_op jit(solution)/shard_map/all_gather | solution.py:181
  115.2 209.9 %all-gather.26.cloned.1.call-start = ((), (), s32[]{:S(2)}) async-start(), calls=%async_computation.15 | async-start | bytes 9437184 | tf_op jit(solution)/shard_map/all_gather | solution.py:141
  115.8 334.7 %all-gather.28.cloned.1.call-start = ((), (), s32[]{:S(2)}) async-start(), calls=%async_computation.16 | async-start | bytes 9437184 | tf_op jit(solution)/shard_map/all_gather | solution.py:146
  116.4 971.6 %all-gather.30.cloned.1.call-start = ((), (), s32[]{:S(2)}) async-start(), calls=%async_computation.17 | async-start | bytes 37748736 | tf_op jit(solution)/shard_map/all_gather | solution.py:222
  117.2 1610.0 %all-gather.32.cloned.1.call-start = ((), (), s32[]{:S(2)}) async-start(), calls=%async_computation.18 | async-start | bytes 37748736 | tf_op jit(solution)/shard_map/all_gather | solution.py:223
  118.0 123.6 %copy-start.76 = (bf16[256,64]{0,1:T(8,128)(2,1)S(1)}, bf16[256,64]{0,1:T(8,128)(2,1)}, u32[]{:S(2)}) copy-start(bf16[256,64]{0,1:T(8,128)(2,1)} %param.42) | copy-start | bytes 98308
  118.0 2248.5 %all-gather.34.cloned.1.call-start = ((), (), s32[]{:S(2)}) async-start(), calls=%async_computation.19 | async-start | bytes 37748736 | tf_op jit(solution)/shard_map/all_gather | solution.py:224
  118.7 2289.9 %all-gather.36.cloned.1.call-start = ((), (), s32[]{:S(2)}) async-start(), calls=%async_computation.20 | async-start | bytes 1179648 | tf_op jit(solution)/shard_map/all_gather | solution.py:153
  119.3 2330.4 %all-gather.38.cloned.1.call-start = ((), (), s32[]{:S(2)}) async-start(), calls=%async_computation.21 | async-start | bytes 1179648 | tf_op jit(solution)/shard_map/all_gather | solution.py:154
  120.0 2547.2 %reduce-scatter.14.cloned.1.call-start = ((), (), s32[]{:S(2)}) async-start(), calls=%async_computation.23 | async-start | bytes 1179648 | tf_op jit(solution)/shard_map/reduce_scatter | solution.py:326
  120.7 209.9 %copy-start.82 = (f32[256]{0:T(256)}, f32[256]{0:T(256)S(1)}, u32[]{:S(2)}) copy-start(f32[256]{0:T(256)S(1)} %convert_element_type.313) | copy-start | bytes 3076
  335.5 119.8 %copy-start.21 = (bf16[128,2,4,256]{0,3,2,1:T(8,128)(2,1)}, bf16[128,2,4,256]{0,3,2,1:T(8,128)(2,1)S(1)}, u32[]{:S(2)}) copy-start(bf16[128,2,4,256]{0,3,2,1:T(8,128)(2,1)S(1)} %fusion.57) | copy-start | bytes 1572868
  456.5 1270.8 %copy-start.14 = (bf16[128,2048]{1,0:T(8,128)(2,1)}, bf16[128,2048]{1,0:T(8,128)(2,1)S(1)}, u32[]{:S(2)}) copy-start(bf16[128,2048]{1,0:T(8,128)(2,1)S(1)} %multiply_convert_fusion.2) | copy-start | bytes 1572868
  2543.4 129.2 %reduce-scatter.12.cloned.1.call-start = ((), (), s32[]{:S(2)}) async-start(), calls=%async_computation.22 | async-start | bytes 1179648 | tf_op jit(solution)/shard_map/reduce_scatter | solution.py:320
  2561.3 186.3 %reduce-scatter.26.cloned.1.call-start = ((), (), s32[]{:S(2)}) async-start(), calls=%async_computation.29 | async-start | bytes 294912 | tf_op jit(solution)/shard_map/reduce_scatter | solution.py:380
  2577.9 223.9 %reduce-scatter.24.cloned.1.call-start = ((), (), s32[]{:S(2)}) async-start(), calls=%async_computation.28 | async-start | bytes 294912 | tf_op jit(solution)/shard_map/reduce_scatter | solution.py:377
  2594.9 1747.8 %reduce-scatter.28.cloned.1.call-start = ((), (), s32[]{:S(2)}) async-start(), calls=%async_computation.30 | async-start | bytes 113246208 | tf_op jit(solution)/shard_map/reduce_scatter | solution.py:258
  2662.9 1746.1 %reduce-scatter.30.cloned.1.call-start = ((), (), s32[]{:S(2)}) async-start(), calls=%async_computation.31 | async-start | bytes 1179648 | tf_op jit(solution)/shard_map/reduce_scatter | solution.py:392
  2665.6 1809.0 %reduce-scatter.32.cloned.1.call-start = ((), (), s32[]{:S(2)}) async-start(), calls=%async_computation.32 | async-start | bytes 1179648 | tf_op jit(solution)/shard_map/reduce_scatter | solution.py:395
  2667.2 1878.9 %reduce-scatter.20.cloned.1.call-start = ((), (), s32[]{:S(2)}) async-start(), calls=%async_computation.26 | async-start | bytes 2359296 | tf_op jit(solution)/shard_map/reduce_scatter | solution.py:362
  2670.3 1947.0 %reduce-scatter.18.cloned.1.call-start = ((), (), s32[]{:S(2)}) async-start(), calls=%async_computation.25 | async-start | bytes 2359296 | tf_op jit(solution)/shard_map/reduce_scatter | solution.py:359
  2677.2 2092.9 %reduce-scatter.16.cloned.1.call-start = ((), (), s32[]{:S(2)}) async-start(), calls=%async_computation.24 | async-start | bytes 9437184 | tf_op jit(solution)/shard_map/reduce_scatter | solution.py:356
  2689.7 2232.6 %reduce-scatter.22.cloned.1.call-start = ((), (), s32[]{:S(2)}) async-start(), calls=%async_computation.27 | async-start | bytes 9437184 | tf_op jit(solution)/shard_map/reduce_scatter | solution.py:371
  2696.6 2260.3 %all-reduce.21.cloned.1.call-start = ((), (), s32[]{:S(2)}) async-start(), calls=%async_computation.33 | async-start | bytes 139264 | tf_op jit(solution)/shard_map/psum | solution.py:423
  2801.8 2430.8 %all-reduce.23.cloned.1.call-start = ((), (), s32[]{:S(2)}) async-start(), calls=%async_computation.34 | async-start | bytes 30932992 | tf_op jit(solution)/shard_map/psum | solution.py:439
  (92 other events, 1033.4 us)
Sparse Core Ops, SparseCore 0:
  10.2 52.3 all-gather.21
  64.6 47.7 all-gather.17
  115.1 38.2 all-gather.23
  155.9 39.0 all-gather.19
  197.0 128.1 all-gather.25
  327.1 123.3 all-gather.27
  452.0 635.8 all-gather.29
  1089.5 637.6 all-gather.31
  1728.8 637.6 all-gather.33
  2368.5 40.1 all-gather.35
  2410.8 38.8 all-gather.37
  2543.5 62.2 reduce-scatter.13
  2610.2 62.4 reduce-scatter.11
  2676.4 60.7 reduce-scatter.25
  2741.0 60.7 reduce-scatter.23
  2805.5 1537.2 reduce-scatter.27
  4346.4 62.5 reduce-scatter.29
  4412.2 62.3 reduce-scatter.31
  4479.1 66.9 reduce-scatter.19
  4550.4 66.8 reduce-scatter.17
  4622.0 148.0 reduce-scatter.15
  4774.2 147.9 reduce-scatter.21
  4927.3 29.5 all-reduce.20
  4960.7 271.7 all-reduce.22
where the time goes:
time: 5280 us; the launch traced here: 5270 us
  waiting for transfers between devices  4600 us (87%)
  matrix products  238 us (5%)
  blocking collectives  227 us (4%)
  other arithmetic  110 us (2%)
  local copies, waits for them, and re-layouts  75.1 us (1%)
    reduce_scatter x1, waiting for transfers between devices, per_device(): lax.psum_scatter(jnp.concatenate([gate_part, up_part, down_part], axis=1)...  1540 us
    all_gather x1, waiting for transfers between devices, per_device(): lax.all_gather(gate_proj, 'fsdp', axis=0, tiled=True)  631 us
    all_gather x1, waiting for transfers between devices, per_device(): lax.all_gather(up_proj, 'fsdp', axis=0, tiled=True)  621 us
    all_gather x1, waiting for transfers between devices, per_device(): lax.all_gather(down_proj, 'fsdp', axis=0, tiled=True)  619 us
    psum x1, waiting for transfers between devices, per_device(): lax.psum(grad_gate.astype(jnp.bfloat16), 'rep').astype(jnp.float32)  263 us
    reduce_scatter x1, waiting for transfers between devices, per_device(): lax.psum_scatter(grad_q.astype(jnp.bfloat16), 'fsdp', scatter_dimension=0...  153 us
    reduce_scatter x1, waiting for transfers between devices, per_device(): lax.psum_scatter(grad_o.astype(jnp.bfloat16), 'fsdp', scatter_dimension=0...  152 us
    all_gather x1, waiting for transfers between devices, per_device(): lax.all_gather(o_proj, 'fsdp', axis=0, tiled=True)  115 us
  transfers between devices with their start and end apart: 24, of which 19 were waited for; matrix products, arithmetic and copies ran while one was open for 6% of the time, Pallas kernels for 0%

commit v1 on v0

--- a/solution.py
+++ b/solution.py
@@ -1,8 +1,11 @@
+import functools
 import math
 
 import jax
 import jax.numpy as jnp
 from jax import lax
+from jax.experimental import pallas as pl
+from jax.experimental.pallas import tpu as pltpu
 from jax.sharding import PartitionSpec as P
 
 HEADS = 8
@@ -81,7 +84,415 @@
     return pull(grad)
 
 
-def per_device(
+MESH = pl.DeviceIdType.MESH
+VMEM_BYTES = 48 << 20
+
+
+def ring_place(index):
+    side = lax.rem(index, 2)
+    return index // 2 + side * (HEADS - 1 - 2 * (index // 2))
+
+
+def ring_index(place):
+    back = place // (HEADS // 2)
+    return (1 - back) * 2 * place + back * (2 * HEADS - 1 - 2 * place)
+
+
+def ring_ends(place):
+    after = {"fsdp": ring_index(lax.rem(place + 1, HEADS))}
+    before = {"fsdp": ring_index(lax.rem(place + HEADS - 1, HEADS))}
+    return (after, before)
+
+
+def greet(others):
+    barrier = pltpu.get_barrier_semaphore()
+    for other in others:
+        pl.semaphore_signal(barrier, inc=1, device_id=other, device_id_type=MESH)
+    pl.semaphore_wait(barrier, len(others))
+
+
+def span(start, size):
+    return pl.ds(pl.multiple_of(start, size), size)
+
+
+def gather_kernel(subs, own_ref, all_ref, local_sem, send_sem, recv_sem):
+    rows = own_ref.shape[0]
+    part = rows // (2 * subs)
+    index = lax.axis_index("fsdp")
+    place = ring_place(index)
+    ends = ring_ends(place)
+    greet(ends)
+    local = pltpu.make_async_copy(own_ref, all_ref.at[span(index * rows, rows)], local_sem)
+    local.start()
+    copies = []
+    lanes = 2 * subs
+    for step in range(HEADS - 1):
+        for lane in range(lanes):
+            way = lane % 2
+            owner = ring_index(lax.rem(place + (step if way else HEADS - step), HEADS))
+            offset = lane * part
+            there = all_ref.at[span(owner * rows + offset, part)]
+            number = step * lanes + lane
+            if step:
+                copies[number - lanes].wait_recv()
+            copy = pltpu.make_async_remote_copy(
+                there if step else own_ref.at[pl.ds(offset, part)],
+                there,
+                send_sem.at[number],
+                recv_sem.at[number],
+                device_id=ends[way],
+                device_id_type=MESH,
+            )
+            copy.start()
+            copies.append(copy)
+    for number, copy in enumerate(copies):
+        if number >= (HEADS - 2) * lanes:
+            copy.wait_recv()
+        copy.wait_send()
+    local.wait()
+
+
+def ring_gather(own, number, subs=2):
+    steps = (HEADS - 1) * 2 * subs
+    return pl.pallas_call(
+        functools.partial(gather_kernel, subs),
+        out_shape=jax.ShapeDtypeStruct((own.shape[0] * HEADS, own.shape[1]), own.dtype),
+        in_specs=[pl.BlockSpec(memory_space=pl.ANY)],
+        out_specs=pl.BlockSpec(memory_space=pl.ANY),
+        scratch_shapes=[
+            pltpu.SemaphoreType.DMA,
+            pltpu.SemaphoreType.DMA((steps,)),
+            pltpu.SemaphoreType.DMA((steps,)),
+        ],
+        compiler_params=pltpu.CompilerParams(collective_id=number, has_side_effects=True),
+    )(own)
+
+
+def scatter_kernel(subs, part_ref, sum_ref, held, send_sem, recv_sem):
+    rows = sum_ref.shape[0]
+    part = rows // (2 * subs)
+    index = lax.axis_index("fsdp")
+    place = ring_place(index)
+    ends = ring_ends(place)
+    greet(ends)
+    copies = []
+    lanes = 2 * subs
+    for step in range(HEADS - 1):
+        for lane in range(lanes):
+            way = lane % 2
+            owner = ring_index(lax.rem(place + (step + 1 if way else HEADS - 1 - step), HEADS))
+            mine = span(owner * rows + lane * part, part)
+            number = step * lanes + lane
+            if step:
+                copies[number - lanes].wait_recv()
+                source = held.at[number - lanes]
+                source[...] = (
+                    source[...].astype(jnp.float32) + part_ref[mine, :].astype(jnp.float32)
+                ).astype(jnp.bfloat16)
+            else:
+                source = part_ref.at[mine]
+            copy = pltpu.make_async_remote_copy(
+                source,
+                held.at[number],
+                send_sem.at[number],
+                recv_sem.at[number],
+                device_id=ends[way],
+                device_id_type=MESH,
+            )
+            copy.start()
+            copies.append(copy)
+    for lane in range(lanes):
+        number = (HEADS - 2) * lanes + lane
+        copies[number].wait_recv()
+        mine = span(index * rows + lane * part, part)
+        sum_ref[pl.ds(lane * part, part), :] = held[number].astype(jnp.float32) + part_ref[
+            mine, :
+        ].astype(jnp.float32)
+    for copy in copies:
+        copy.wait_send()
+
+
+def ring_scatter(parts, number, subs=2):
+    rows = parts.shape[0] // HEADS
+    steps = (HEADS - 1) * 2 * subs
+    return pl.pallas_call(
+        functools.partial(scatter_kernel, subs),
+        out_shape=jax.ShapeDtypeStruct((rows, parts.shape[1]), jnp.float32),
+        in_specs=[pl.BlockSpec(memory_space=pltpu.VMEM)],
+        out_specs=pl.BlockSpec(memory_space=pltpu.VMEM),
+        scratch_shapes=[
+            pltpu.VMEM((steps, rows // (2 * subs), parts.shape[1]), jnp.bfloat16),
+            pltpu.SemaphoreType.DMA((steps,)),
+            pltpu.SemaphoreType.DMA((steps,)),
+        ],
+        compiler_params=pltpu.CompilerParams(
+            collective_id=number, has_side_effects=True, vmem_limit_bytes=VMEM_BYTES
+        ),
+    )(parts)
+
+
+def swap_kernel(own_ref, all_ref, local_sem, send_sem, recv_sem):
+    rows = own_ref.shape[0] // HEADS
+    index = lax.axis_index("fsdp")
+    others = [lax.rem(index + step, HEADS) for step in range(1, HEADS)]
+    greet([{"fsdp": other} for other in others])
+    mine = span(index * rows, rows)
+    copies = []
+    for step, other in enumerate(others):
+        copy = pltpu.make_async_remote_copy(
+            own_ref.at[span(other * rows, rows)],
+            all_ref.at[mine],
+            send_sem.at[step],
+            recv_sem.at[step],
+            device_id={"fsdp": other},
+            device_id_type=MESH,
+        )
+        copy.start()
+        copies.append(copy)
+    local = pltpu.make_async_copy(own_ref.at[mine], all_ref.at[mine], local_sem)
+    local.start()
+    for copy in copies:
+        copy.wait()
+    local.wait()
+
+
+def swap_blocks(own, number):
+    return pl.pallas_call(
+        swap_kernel,
+        out_shape=jax.ShapeDtypeStruct(own.shape, own.dtype),
+        in_specs=[pl.BlockSpec(memory_space=pl.ANY)],
+        out_specs=pl.BlockSpec(memory_space=pl.ANY),
+        scratch_shapes=[
+            pltpu.SemaphoreType.DMA,
+            pltpu.SemaphoreType.DMA((HEADS - 1,)),
+            pltpu.SemaphoreType.DMA((HEADS - 1,)),
+        ],
+        compiler_params=pltpu.CompilerParams(collective_id=number, has_side_effects=True),
+    )(own)
+
+
+def dot(left, right):
+    return jnp.dot(left, right, preferred_element_type=jnp.float32)
+
+
+def low(value):
+    return value.astype(jnp.bfloat16)
+
+
+def head_plan(
+    hidden_in,
+    layer_input,
+    out_grad,
+    seg_lengths,
+    seg_parents,
+    attn_norm,
+    q_proj,
+    k_proj,
+    v_proj,
+    q_norm,
+    k_norm,
+    o_proj,
+    attn_post_norm,
+    laurel_left,
+    laurel_right,
+    laurel_norm,
+    ffw_norm,
+    gate_proj,
+    up_proj,
+    down_proj,
+    ffw_post_norm,
+    pl_gate,
+    pl_proj,
+    pl_post_norm,
+):
+    index = lax.axis_index("fsdp")
+    rows, width = hidden_in.shape
+    shard = width // HEADS
+    total = rows * HEADS
+    groups = HEADS // KV_HEADS
+    scale = HEAD_DIM ** (-0.5)
+    rank = laurel_left.shape[1]
+    per_layer = pl_gate.shape[1]
+    key_head = index // groups
+
+    gains = (attn_norm, attn_post_norm, laurel_norm, ffw_norm, ffw_post_norm, pl_post_norm)
+    packed = jnp.concatenate(gains + (q_norm, k_norm))
+    pad = -packed.shape[0] % (32 * 128)
+    packed = jnp.pad(packed, (0, pad)).reshape(-1, 128)
+    all_gains = ring_gather(packed, 0, 1).reshape(HEADS, -1).astype(jnp.float32)
+    wide_gains = [all_gains[:, i * shard : (i + 1) * shard].reshape(-1) for i in range(len(gains))]
+    gain_anorm, gain_apost, gain_lnorm, gain_fnorm, gain_fpost, gain_plpost = wide_gains
+    at = len(gains) * shard
+    piece = HEAD_DIM // HEADS
+    gain_qnorm = all_gains[:, at : at + piece].reshape(-1)
+    gain_knorm = all_gains[:, at + piece : at + 2 * piece].reshape(-1)
+
+    hidden_all = ring_gather(hidden_in, 1)
+    q_blocks = q_proj.reshape(shard, HEADS, HEAD_DIM).transpose(1, 0, 2).reshape(-1, HEAD_DIM)
+    q_head = swap_blocks(q_blocks, 2)
+    kv_all = ring_gather(jnp.concatenate([k_proj, v_proj], axis=1), 3)
+    small_all = ring_gather(jnp.concatenate([pl_gate, laurel_left, laurel_right], axis=1), 4)
+    full_plproj = ring_gather(pl_proj, 5, 1)
+    k_head = lax.dynamic_slice_in_dim(kv_all, key_head * HEAD_DIM, HEAD_DIM, 1)
+    v_head = lax.dynamic_slice_in_dim(kv_all, (KV_HEADS + key_head) * HEAD_DIM, HEAD_DIM, 1)
+    full_plgate = small_all[:, :per_layer]
+    full_left = small_all[:, per_layer : per_layer + rank]
+    full_right = small_all[:, per_layer + rank :]
+
+    tokens, member, reach, position = tree_tables(seg_lengths[0], seg_parents[0], total)
+    depth = position.astype(jnp.float32)
+    seen = (jnp.dot(reach, member.T) > 0) & (tokens[None, :] <= tokens[:, None])
+
+    normed_all = low(norm_rows(hidden_all.astype(jnp.float32), gain_anorm))
+    q_raw = dot(normed_all, q_head)
+    k_raw = dot(normed_all, k_head)
+    v_low = low(dot(normed_all, v_head))
+
+    def head_path(raw, gain):
+        return rotate(norm_rows(raw, gain)[:, None, :], depth)[:, 0, :]
+
+    q_low = low(head_path(q_raw, gain_qnorm))
+    k_low = low(head_path(k_raw, gain_knorm))
+    scores = jnp.where(seen, mul_t(q_low, k_low) * scale, MASKED)
+    top = jnp.max(scores, axis=-1, keepdims=True)
+    expo = jnp.exp(scores - top)
+    sums = jnp.sum(expo, axis=-1, keepdims=True)
+    probs = expo / sums
+    probs_low = low(probs)
+    attended = dot(probs_low, v_low)
+    attended_low = low(attended)
+    branch = ring_scatter(low(dot(attended_low, o_proj)), 6)
+
+    source = hidden_in.astype(jnp.float32)
+    extra = layer_input.astype(jnp.float32)
+    normed = norm_rows(source, gain_anorm)
+    normed_low = low(normed)
+    left_low = low(dot(normed_low, full_left))
+    low_rank = mul_t(left_low, full_right)
+    first_sum = (
+        source + norm_rows(branch, gain_apost) + normed + norm_rows(low_rank, gain_lnorm)
+    ) * HALF_ROOT
+    ffw_low = low(norm_rows(first_sum, gain_fnorm))
+
+    ffw_all = ring_gather(ffw_low, 7)
+    gate_val = mul_t(ffw_all, gate_proj)
+    up_val = mul_t(ffw_all, up_proj)
+    inner_low = low(gelu_mix(gate_val, up_val))
+    ffw_out = ring_scatter(low(dot(inner_low, down_proj)), 8)
+
+    second_sum = first_sum + norm_rows(ffw_out, gain_fpost)
+    second_low = low(second_sum)
+    pl_pre = dot(second_low, full_plgate)
+    pl_mix = low(gelu_mix(pl_pre, extra))
+    pl_out = dot(pl_mix, full_plproj)
+    result = second_sum + norm_rows(pl_out, gain_plpost)
+    seed = out_grad.astype(jnp.float32)
+    d_plout, grad_plpost = norm_back(pl_out, gain_plpost, seed)
+    d_plout_low = low(d_plout)
+    grad_plproj = outer(pl_mix, d_plout_low)
+    d_mix = mul_t(d_plout_low, full_plproj)
+    d_pre, d_extra = mix_back(pl_pre, extra, d_mix)
+    d_pre_low = low(d_pre)
+    grad_plgate = outer(second_low, d_pre_low)
+    d_second = seed + mul_t(d_pre_low, full_plgate)
+    d_ffwout, grad_fpost = norm_back(ffw_out, gain_fpost, d_second)
+
+    d_ffw_all = ring_gather(low(d_ffwout), 9)
+    d_inner = mul_t(d_ffw_all, down_proj)
+    d_gate, d_up = mix_back(gate_val, up_val, d_inner)
+    d_gate_low = low(d_gate)
+    d_up_low = low(d_up)
+    d_ffwin = ring_scatter(low(dot(d_gate_low, gate_proj) + dot(d_up_low, up_proj)), 10)
+    ffw_grads = [
+        low(outer(d_gate_low, ffw_all)),
+        low(outer(d_up_low, ffw_all)),
+        low(outer(inner_low, d_ffw_all)),
+    ]
+    sum_gate, sum_up, sum_down = [lax.psum(item, "rep").astype(jnp.float32) for item in ffw_grads]
+
+    d_first_part, grad_fnorm = norm_back(first_sum, gain_fnorm, d_ffwin)
+    d_scaled = (d_second + d_first_part) * HALF_ROOT
+    d_branch, grad_apost = norm_back(branch, gain_apost, d_scaled)
+    d_lowrank, grad_lnorm = norm_back(low_rank, gain_lnorm, d_scaled)
+    d_lowrank_low = low(d_lowrank)
+    d_branch_all = ring_gather(low(d_branch), 11)
+    grad_right = outer(d_lowrank_low, left_low)
+    d_left_low = low(dot(d_lowrank_low, full_right))
+    grad_left = outer(normed_low, d_left_low)
+
+    d_att_low = low(mul_t(d_branch_all, o_proj))
+    grad_o = outer(attended_low, d_branch_all)
+    delta = jnp.sum(d_att_low.astype(jnp.float32) * attended, axis=-1, keepdims=True)
+    d_probs = mul_t(d_att_low, v_low)
+    d_scores = low(probs * (d_probs - delta) * scale)
+    d_query = dot(d_scores, k_low)
+    d_key = outer(d_scores, q_low)
+    d_value = outer(probs_low, d_att_low)
+    unused_q, q_pull = jax.vjp(head_path, q_raw, gain_qnorm)
+    d_qraw, grad_qnorm = q_pull(d_query)
+    unused_k, k_pull = jax.vjp(head_path, k_raw, gain_knorm)
+    d_kraw, grad_knorm = k_pull(d_key)
+    d_q_low = low(d_qraw)
+    d_k_low = low(d_kraw)
+    d_v_low = low(d_value)
+    d_normed_part = mul_t(d_q_low, q_head) + mul_t(d_k_low, k_head) + mul_t(d_v_low, v_head)
+    d_normed = d_scaled + mul_t(d_left_low, full_left) + ring_scatter(low(d_normed_part), 12)
+    d_source_part, grad_anorm = norm_back(source, gain_anorm, d_normed)
+    d_source = d_scaled + d_source_part
+
+    head_grads = low(outer(normed_all, jnp.concatenate([d_q_low, d_k_low, d_v_low], axis=1)))
+    head_grads = swap_blocks(head_grads, 13).reshape(HEADS, shard, 3 * HEAD_DIM)
+    q_part = head_grads[:, :, :HEAD_DIM].transpose(1, 0, 2).reshape(shard, -1)
+    kv_part = head_grads[:, :, HEAD_DIM:].astype(jnp.float32)
+    kv_part = low(jnp.sum(kv_part.reshape(KV_HEADS, groups, shard, -1), axis=1))
+    k_part = kv_part[:, :, :HEAD_DIM].transpose(1, 0, 2).reshape(shard, -1)
+    v_part = kv_part[:, :, HEAD_DIM:].transpose(1, 0, 2).reshape(shard, -1)
+
+    def scatter(value):
+        return lax.psum_scatter(low(value), "fsdp", scatter_dimension=0, tiled=True)
+
+    def over_trees(value):
+        return lax.psum(low(value), "rep").astype(jnp.float32)
+
+    small_grads = [grad_anorm, grad_apost, grad_lnorm, grad_fnorm, grad_fpost, grad_plpost]
+    small_sums = lax.psum(jnp.concatenate(small_grads + [grad_qnorm, grad_knorm]), ("rep", "fsdp"))
+
+    def own_part(start, size):
+        return lax.dynamic_slice_in_dim(small_sums, start + index * size, size)
+
+    own = [own_part(i * width, shard) for i in range(len(small_grads))]
+    sum_anorm, sum_apost, sum_lnorm, sum_fnorm, sum_fpost, sum_plpost = own
+    sum_qnorm = own_part(len(small_grads) * width, piece)
+    sum_knorm = own_part(len(small_grads) * width + HEAD_DIM, piece)
+    mixed = scatter(jnp.concatenate([grad_plgate, grad_left, grad_right], axis=1))
+    mixed = over_trees(mixed)
+    return (
+        low(result),
+        low(d_source),
+        low(d_extra),
+        sum_anorm,
+        over_trees(q_part),
+        over_trees(k_part),
+        over_trees(v_part),
+        sum_qnorm,
+        sum_knorm,
+        over_trees(grad_o),
+        sum_apost,
+        mixed[:, per_layer : per_layer + rank],
+        mixed[:, per_layer + rank :],
+        sum_lnorm,
+        sum_fnorm,
+        sum_gate,
+        sum_up,
+        sum_down,
+        sum_fpost,
+        mixed[:, :per_layer],
+        over_trees(scatter(grad_plproj)),
+        sum_plpost,
+    )
+
+
+def gather_plan(
     hidden_in,
     layer_input,
     out_grad,
@@ -494,7 +905,7 @@
         P("fsdp"),
     )
     return jax.shard_map(
-        per_device,
+        head_plan if mesh.shape["fsdp"] == HEADS else gather_plan,
         mesh=mesh,
         in_specs=placed,
         out_specs=(

time: 5280 us -> 1030 us (0.20)
  waiting for transfers between devices: 4600 us -> 185 us
  Pallas kernels: 0 us -> 556 us
  blocking collectives: 227 us -> 40.2 us
  matrix products: 238 us -> 139 us
  other arithmetic: 110 us -> 51.9 us
    reduce_scatter x11 -> x2, waiting for transfers between devices: 2170 us -> 0.01 us  [scatter(): return lax.psum_scatter(low(value), 'fsdp', scatter_dimension=0, tiled=True)]
    all_gather x11 -> x0, waiting for transfers between devices: 2130 us -> none  [the longest x1 631 us: per_device(): lax.all_gather(gate_proj, 'fsdp', axis=0, tiled=True)]
    pallas_call x0 -> x14, Pallas kernels: none -> 551 us  [the longest x8 330 us: ring_gather(): pl.pallas_call(functools.partial(gather_kernel, subs), out_shape=jax.Shap...]
    all_gather x8 -> x0, blocking collectives: 168 us -> none  [the longest x1 32.5 us: per_device(): lax.all_gather(laurel_right, 'fsdp', axis=0, tiled=True)]
    psum x2 -> x1, waiting for transfers between devices: 296 us -> 185 us  [over_trees(): return lax.psum(low(value), 'rep').astype(jnp.float32)]
    concatenate x3, other arithmetic: 68 us -> 3.01 us  [the longest x1 1.37 us: head_plan(): jnp.concatenate([grad_plgate, grad_left, grad_right], axis=1)]
    unnamed x2 -> x0, blocking collectives: 58.7 us -> none
  transfers between devices with their start and end apart: 24 -> 3, of which waited for: 19 -> 1; matrix products, arithmetic and copies ran while one was open for 6% -> 10% of each run, Pallas kernels for 0% -> 24%
where the time goes in v1:
time: 1030 us; the launch traced here: 1020 us
  Pallas kernels  556 us (54%)
  waiting for transfers between devices  185 us (18%)
  matrix products  139 us (13%)
  other arithmetic  51.9 us (5%)
  blocking collectives  40.2 us (4%)
  local copies, waits for them, and re-layouts  31.3 us (3%)
  between operations  15.9 us (2%)
    pallas_call x8, Pallas kernels, ring_gather(): pl.pallas_call(functools.partial(gather_kernel, subs), out_shape=jax.Shap...  330 us
    psum x1, waiting for transfers between devices, over_trees(): return lax.psum(low(value), 'rep').astype(jnp.float32)  185 us
    pallas_call x4, Pallas kernels, ring_scatter(): pl.pallas_call(functools.partial(scatter_kernel, subs), out_shape=jax.Sha...  166 us
    pallas_call x2, Pallas kernels, swap_blocks(): pl.pallas_call(swap_kernel, out_shape=jax.ShapeDtypeStruct(own.shape, own...  54.6 us
    dot_general x13, matrix products, mul_t(): lax.dot_general(left, right, (((1,), (1,)), ((), ())), preferred_element_...  52.4 us
    psum x1, blocking collectives, head_plan(): lax.psum(jnp.concatenate(small_grads + [grad_qnorm, grad_knorm]), ('rep',...  40.2 us
    dot_general x12, matrix products, dot(): return jnp.dot(left, right, preferred_element_type=jnp.float32)  35 us
    dot_general x11, matrix products, outer(): lax.dot_general(left, right, (((0,), (0,)), ((), ())), preferred_element_...  33.6 us
  transfers between devices with their start and end apart: 3, of which 1 were waited for; matrix products, arithmetic and copies ran while one was open for 10% of the time, Pallas kernels for 24%

profile of v1, /device:TPU:0, one launch (start us, length us, event | category | flops | bytes accessed | tf_op | source)
XLA Modules:
  0.0 1019.4 jit_solution(1261101577059283935)
XLA Ops:
  7.8 5.4 concatenate.47
  13.9 25.3 %shard_map.400 = bf16[256,128]{1,0:T(8,128)(2,1)} custom-call(bf16[32,128]{1,0:T(8,128)(2,1)} %pad_bitcast_fusion.own_ref), custom_call_target="tpu_custom_call" | custom-call | tf_op jit(solution)/shard_map/pallas_call | solution.py:157
  41.1 11.6 %while.11 = (s32[]{:T(128)}, s32[13,13]{1,0:T(8,128)S(1)}, s32[13]{0:T(128)}, pred[13]{0:T(512)(128)(4,1)S(1)}, s32[]{:T(128)}) while((s32[]{:T(128)}, s32[13,13]{1,0:T(8,128)S(1)}, s32[13]{0:T(128)}, pred[13]{0:T(512)(128)(4,1)S(1)}, s32[]{:T(128)}) %tuple.89), condition=%wide.region_3.4_spmd.clone, body=%wide.region_2.3_spmd.clone.sunk | while | flops 5579 | bytes 2830 | solution.py:56
  53.9 5.2 fusion.40
  59.3 41.0 %shard_map.399 = bf16[1024,2048]{1,0:T(8,128)(2,1)} custom-call(bf16[128,2048]{1,0:T(8,128)(2,1)} %own_ref.2), custom_call_target="tpu_custom_call" | custom-call | tf_op jit(solution)/shard_map/pallas_call | solution.py:157
  104.9 33.2 %shard_map.407 = bf16[256,2048]{1,0:T(8,128)(2,1)} custom-call(bf16[32,2048]{1,0:T(8,128)(2,1)} %own_ref.3), custom_call_target="tpu_custom_call" | custom-call | tf_op jit(solution)/shard_map/pallas_call | solution.py:157
  139.1 14.4 %shard_map.401 = bf16[2048,256]{1,0:T(8,128)(2,1)} custom-call(bf16[2048,256]{1,0:T(8,128)(2,1)} %bitcast.154), custom_call_target="tpu_custom_call" | custom-call | tf_op jit(solution)/shard_map/pallas_call | solution.py:260
  154.4 36.0 %shard_map.404 = bf16[2048,384]{1,0:T(8,128)(2,1)} custom-call(bf16[256,384]{1,0:T(8,128)(2,1)} %pad_maximum_fusion.2.own_ref), custom_call_target="tpu_custom_call" | custom-call | tf_op jit(solution)/shard_map/pallas_call | solution.py:157
  194.8 34.3 %shard_map.402 = bf16[2048,1024]{1,0:T(8,128)(2,1)} custom-call(bf16[256,1024]{1,0:T(8,128)(2,1)} %pad_maximum_fusion.1.own_ref), custom_call_target="tpu_custom_call" | custom-call | tf_op jit(solution)/shard_map/pallas_call | solution.py:157
  232.2 4.9 fusion.66
  248.8 4.9 online-softmax
  256.3 43.4 %shard_map.403 = f32[128,2048]{1,0:T(8,128)S(1)} custom-call(bf16[1024,2048]{1,0:T(8,128)(2,1)S(1)} %convolution_convert_fusion.part_ref), custom_call_target="tpu_custom_call" | custom-call | tf_op jit(solution)/shard_map/pallas_call | solution.py:218
  302.5 38.5 %shard_map.405 = bf16[1024,2048]{1,0:T(8,128)(2,1)} custom-call(bf16[128,2048]{1,0:T(8,128)(2,1)} %multiply_convert_fusion.3.own_ref), custom_call_target="tpu_custom_call" | custom-call | tf_op jit(solution)/shard_map/pallas_call | solution.py:157
  341.0 8.0 fusion.174
  349.1 7.2 multiply_convert_fusion.2
  356.3 4.7 convolution_convert_fusion.4.part_ref
  361.0 41.3 %shard_map.406 = f32[128,2048]{1,0:T(8,128)S(1)} custom-call(bf16[1024,2048]{1,0:T(8,128)(2,1)S(1)} %convolution_convert_fusion.4.part_ref), custom_call_target="tpu_custom_call" | custom-call | tf_op jit(solution)/shard_map/pallas_call | solution.py:218
  417.2 45.3 %shard_map.408 = bf16[1024,2048]{1,0:T(8,128)(2,1)} custom-call(bf16[128,2048]{1,0:T(8,128)(2,1)} %fusion.50.own_ref), custom_call_target="tpu_custom_call" | custom-call | tf_op jit(solution)/shard_map/pallas_call | solution.py:157
  462.5 12.5 %multiply_convert_fusion.1 = (bf16[1024,1024]{1,0:T(8,128)(2,1)S(1)}, bf16[1024,1024]{1,0:T(8,128)(2,1)S(1)}) fusion(f32[1024,1024]{1,0:T(8,128)} %copy-done.121, f32[1024,1024]{1,0:T(8,128)} %get-tuple-element.233, bf16[1024,2048]{1,0:T(8,128)(2,1)} %shard_map.408, bf16[1024,2048]{1,0:T(8,128)(2,1)} %param.45), kind=kOutput, calls=%fused_computation.27 | convolution fusion | flops 4320133120 | bytes 20971520 | tf_op jit(solution)/shard_map/dot_general | solution.py:73
  475.0 6.8 fusion.175
  481.8 7.0 add_convert_fusion.1.part_ref
  488.9 40.6 %shard_map.409 = f32[128,2048]{1,0:T(8,128)S(1)} custom-call(bf16[1024,2048]{1,0:T(8,128)(2,1)S(1)} %add_convert_fusion.1.part_ref), custom_call_target="tpu_custom_call" | custom-call | tf_op jit(solution)/shard_map/pallas_call | solution.py:218
  539.8 76.6 %shard_map.410 = bf16[1024,2048]{1,0:T(8,128)(2,1)} custom-call(bf16[128,2048]{1,0:T(8,128)(2,1)} %get-tuple-element.197.own_ref), custom_call_target="tpu_custom_call" | custom-call | tf_op jit(solution)/shard_map/pallas_call | solution.py:157
  630.2 5.5 convolution_convert_fusion.5.own_ref
  635.8 40.2 %shard_map.412 = bf16[2048,768]{1,0:T(8,128)(2,1)} custom-call(bf16[2048,768]{1,0:T(8,128)(2,1)} %convolution_convert_fusion.5.own_ref), custom_call_target="tpu_custom_call" | custom-call | tf_op jit(solution)/shard_map/pallas_call | solution.py:260
  682.0 4.6 convolution_convert_fusion.8
  686.6 6.2 convolution_convert_fusion.1
  692.9 6.2 convolution_convert_fusion.2
  699.1 6.6 convolution_convert_fusion.3
  713.5 40.7 %shard_map.411 = f32[128,2048]{1,0:T(8,128)S(1)} custom-call(bf16[1024,2048]{1,0:T(8,128)(2,1)S(1)} %add_convert_fusion.part_ref), custom_call_target="tpu_custom_call" | custom-call | tf_op jit(solution)/shard_map/pallas_call | solution.py:218
  756.8 40.2 %psum.70 = f32[12800]{0:T(1024)S(1)} all-reduce(f32[12800]{0:T(1024)S(1)} %constant_dynamic-update-slice_fusion), channel_id=1, replica_groups=mesh['rep'=4,'fsdp'=8] {'rep','fsdp'}, use_global_device_ids=true, to_apply=%region_32.33 | all-reduce | flops 12800 | bytes 102400 | tf_op jit(solution)/shard_map/psum | solution.py:458
  800.8 185.3 %all-reduce.8.cloned.1.call-done = (bf16[256,512]{0,1:T(8,128)(2,1)}, bf16[256,512]{0,1:T(8,128)(2,1)}, bf16[256,384]{0,1:T(8,128)(2,1)}, bf16[256,2048]{1,0:T(8...) async-done(((bf16[256,512]{0,1:T(8,128)(2,1)}, ...) | async-done | bytes 15532048 | tf_op jit(solution)/shard_map/psum | solution.py:455
  (394 shorter events, 131.1 us)
Async XLA Ops:
  7.2 246.5 %copy-start = (bf16[256,2048]{1,0:T(8,128)(2,1)S(1)}, bf16[256,2048]{1,0:T(8,128)(2,1)}, u32[]{:S(2)}) copy-start(bf16[256,2048]{1,0:T(8,128)(2,1)} %param.37) | copy-start | bytes 3145732
  7.2 51.9 %copy-start.13 = (bf16[128,2048]{1,0:T(8,128)(2,1)S(1)}, bf16[128,2048]{1,0:T(8,128)(2,1)}, u32[]{:S(2)}) copy-start(bf16[128,2048]{1,0:T(8,128)(2,1)} %own_ref.2) | copy-start | bytes 1572868
  7.2 698.5 %reduce-scatter.5.cloned.1.call-start = ((), (), s32[]{:S(2)}) async-start(), calls=%async_computation.3 | async-start | bytes 1179648 | tf_op jit(solution)/shard_map/reduce_scatter | solution.py:452
  53.9 50.8 %copy-start.74 = (bf16[256,64]{0,1:T(8,128)(2,1)S(1)}, bf16[256,64]{0,1:T(8,128)(2,1)}, u32[]{:S(2)}) copy-start(bf16[256,64]{0,1:T(8,128)(2,1)} %param.39) | copy-start | bytes 98308
  53.9 50.9 %copy-start.75 = (bf16[256,64]{0,1:T(8,128)(2,1)S(1)}, bf16[256,64]{0,1:T(8,128)(2,1)}, u32[]{:S(2)}) copy-start(bf16[256,64]{0,1:T(8,128)(2,1)} %param.40) | copy-start | bytes 98308
  59.1 79.0 %copy-start.44 = (bf16[256,2048]{1,0:T(8,128)(2,1)S(1)}, bf16[256,2048]{1,0:T(8,128)(2,1)}, u32[]{:S(2)}) copy-start(bf16[256,2048]{1,0:T(8,128)(2,1)} %param.32) | copy-start | bytes 3145732
  59.3 45.4 %copy-start.100 = (f32[128]{0:T(128)}, f32[128]{0:T(128)S(1)}, u32[]{:S(2)}) copy-start(f32[128]{0:T(128)S(1)} %fusion.58) | copy-start | bytes 1540
  59.3 94.3 %copy-start.59 = (bf16[256,256]{1,0:T(8,128)(2,1)S(1)}, bf16[256,256]{1,0:T(8,128)(2,1)}, u32[]{:S(2)}) copy-start(bf16[256,256]{1,0:T(8,128)(2,1)} %param.47) | copy-start | bytes 393220
  100.3 90.0 %copy-start.14 = (bf16[128,2048]{1,0:T(8,128)(2,1)S(1)}, bf16[128,2048]{1,0:T(8,128)(2,1)}, u32[]{:S(2)}) copy-start(bf16[128,2048]{1,0:T(8,128)(2,1)} %own_ref.2) | copy-start | bytes 1572868
  100.4 90.0 %copy-start.84 = (f32[128]{0:T(128)}, f32[128]{0:T(128)S(1)}, u32[]{:S(2)}) copy-start(f32[128]{0:T(128)S(1)} %fusion.146) | copy-start | bytes 1540
  138.1 55.9 %copy-start.51 = (bf16[256,512]{1,0:T(8,128)(2,1)S(1)}, bf16[256,512]{1,0:T(8,128)(2,1)}, u32[]{:S(2)}) copy-start(bf16[256,512]{1,0:T(8,128)(2,1)} %param.34) | copy-start | bytes 786436
  139.1 54.8 %copy-start.52 = (bf16[256,512]{1,0:T(8,128)(2,1)S(1)}, bf16[256,512]{1,0:T(8,128)(2,1)}, u32[]{:S(2)}) copy-start(bf16[256,512]{1,0:T(8,128)(2,1)} %param.33) | copy-start | bytes 786436
  193.4 106.5 %copy-start.8 = (f32[128,2048]{1,0:T(8,128)}, f32[128,2048]{1,0:T(8,128)S(1)}, u32[]{:S(2)}) copy-start(f32[128,2048]{1,0:T(8,128)S(1)} %get-tuple-element.227) | copy-start | bytes 3145732
  256.2 43.6 %copy-start.15 = (bf16[128,2048]{1,0:T(8,128)(2,1)S(1)}, bf16[128,2048]{1,0:T(8,128)(2,1)}, u32[]{:S(2)}) copy-start(bf16[128,2048]{1,0:T(8,128)(2,1)} %own_ref.2) | copy-start | bytes 1572868
  256.2 43.6 %copy-start.63 = (f32[1,2,8,128]{3,1,2,0:T(2,128)S(1)}, f32[1,2,8,128]{3,1,2,0:T(2,128)}, u32[]{:S(2)}) copy-start(f32[1,2,8,128]{3,1,2,0:T(2,128)} %copy.93) | copy-start | bytes 24580
  256.2 43.6 %copy-start.64 = (f32[1,2,8,128]{3,1,2,0:T(2,128)S(1)}, f32[1,2,8,128]{3,1,2,0:T(2,128)}, u32[]{:S(2)}) copy-start(f32[1,2,8,128]{3,1,2,0:T(2,128)} %copy.92) | copy-start | bytes 24580
  256.2 43.6 %copy-start.85 = (f32[128]{0:T(128)S(1)}, f32[128]{0:T(128)}, u32[]{:S(2)}) copy-start(f32[128]{0:T(128)} %copy-done.84) | copy-start | bytes 1540
  256.3 43.6 %copy-start.89 = (f32[128]{0:T(128)S(1)}, f32[128]{0:T(128)}, u32[]{:S(2)}) copy-start(f32[128]{0:T(128)} %fusion.147) | copy-start | bytes 1540
  300.5 48.5 %copy-start.107 = (f32[128]{0:T(128)}, f32[128]{0:T(128)S(1)}, u32[]{:S(2)}) copy-start(f32[128]{0:T(128)S(1)} %get-tuple-element.182) | copy-start | bytes 1540
  301.1 47.9 %copy-start.98 = (f32[128]{0:T(128)}, f32[128]{0:T(128)S(1)}, u32[]{:S(2)}) copy-start(f32[128]{0:T(128)S(1)} %get-tuple-element.225) | copy-start | bytes 1540
  361.0 42.1 %copy-start.3 = (f32[128,2048]{1,0:T(8,128)S(1)}, f32[128,2048]{1,0:T(8,128)}, u32[]{:S(2)}) copy-start(f32[128,2048]{1,0:T(8,128)} %copy-done.2) | copy-start | bytes 3145732
  361.0 42.0 %copy-start.57 = (f32[1,2,8,128]{3,1,2,0:T(2,128)S(1)}, f32[1,2,8,128]{3,1,2,0:T(2,128)}, u32[]{:S(2)}) copy-start(f32[1,2,8,128]{3,1,2,0:T(2,128)} %copy.95) | copy-start | bytes 24580
  361.0 42.2 %copy-start.5 = (bf16[2048,384]{1,0:T(8,128)(2,1)S(1)}, bf16[2048,384]{1,0:T(8,128)(2,1)}, u32[]{:S(2)}) copy-start(bf16[2048,384]{1,0:T(8,128)(2,1)} %shard_map.404) | copy-start | bytes 4718596
  408.6 297.1 %reduce-scatter.3.cloned.1.call-start = ((), (), s32[]{:S(2)}) async-start(), calls=%async_computation.2 | async-start | bytes 1769472 | tf_op jit(solution)/shard_map/reduce_scatter | solution.py:452
  488.8 41.1 %copy-start.9 = (f32[128,2048]{1,0:T(8,128)S(1)}, f32[128,2048]{1,0:T(8,128)}, u32[]{:S(2)}) copy-start(f32[128,2048]{1,0:T(8,128)} %copy-done.8) | copy-start | bytes 3145732
  488.8 41.1 %copy-start.23 = (f32[128,2048]{1,0:T(8,128)S(1)}, f32[128,2048]{1,0:T(8,128)}, u32[]{:S(2)}) copy-start(f32[128,2048]{1,0:T(8,128)} %copy-done.22) | copy-start | bytes 3145732
  488.8 41.1 %copy-start.61 = (f32[2048]{0:T(1024)S(1)}, f32[2048]{0:T(1024)}, u32[]{:S(2)}) copy-start(f32[2048]{0:T(1024)} %get-tuple-element.244) | copy-start | bytes 24580
  488.9 41.1 %copy-start.62 = (f32[2048]{0:T(1024)S(1)}, f32[2048]{0:T(1024)}, u32[]{:S(2)}) copy-start(f32[2048]{0:T(1024)} %get-tuple-element.245) | copy-start | bytes 24580
  536.5 449.5 %all-reduce.8.cloned.1.call-start = ((), (), s32[]{:S(2)}) async-start(), calls=%async_computation.4 | async-start | bytes 31064064 | tf_op jit(solution)/shard_map/psum | solution.py:455
  536.6 79.8 %copy-start.24 = (f32[1024,256]{1,0:T(8,128)S(1)}, f32[1024,256]{1,0:T(8,128)}, u32[]{:S(2)}) copy-start(f32[1024,256]{1,0:T(8,128)} %online-softmax) | copy-start | bytes 3145732
  713.5 43.3 %copy-start.73 = (f32[2048]{0:T(1024)S(1)}, f32[2048]{0:T(1024)}, u32[]{:S(2)}) copy-start(f32[2048]{0:T(1024)} %get-tuple-element.158) | copy-start | bytes 24580
  713.5 84.8 %copy-start.101 = (f32[128]{0:T(128)S(1)}, f32[128]{0:T(128)}, u32[]{:S(2)}) copy-start(f32[128]{0:T(128)} %copy-done.100) | copy-start | bytes 1540
  (93 other events, 675.4 us)
Sparse Core Ops, SparseCore 0:
  408.7 64.2 reduce-scatter.4
  536.7 79.7 reduce-scatter.2
  705.9 280.1 all-reduce.7

commit v2 on v1

--- a/solution.py
+++ b/solution.py
@@ -115,160 +115,1062 @@
     return pl.ds(pl.multiple_of(start, size), size)
 
 
-def gather_kernel(subs, own_ref, all_ref, local_sem, send_sem, recv_sem):
+def neighbours():
+    rep = lax.axis_index("rep")
+    chip = rep // 2
+    core = lax.rem(rep, 2)
+    return (chip, core, {"rep": 2 * chip + 1 - core}, {"rep": 2 * (1 - chip) + core})
+
+
+def remote(source, target, sems, number, device):
+    copy = pltpu.make_async_remote_copy(
+        source,
+        target,
+        sems[0].at[number],
+        sems[1].at[number],
+        device_id=device,
+        device_id_type=MESH,
+    )
+    copy.start()
+    return copy
+
+
+class Ring:
+    def __init__(self, place, ends, lanes, sems, own, there):
+        self.place, self.ends, self.lanes, self.sems = place, ends, lanes, sems
+        self.own, self.there = own, there
+        self.copies = []
+
+    def owner(self, step, lane):
+        ahead = step if lane % 2 else HEADS - step
+        return ring_index(lax.rem(self.place + ahead, HEADS))
+
+    def send(self, step):
+        for lane in range(self.lanes):
+            number = step * self.lanes + lane
+            target = self.there(self.owner(step, lane), lane)
+            if step:
+                self.copies[number - self.lanes].wait_recv()
+            source = target if step else self.own(lane)
+            self.copies.append(remote(source, target, self.sems, number, self.ends[lane % 2]))
+
+    def arrive(self, step):
+        for lane in range(self.lanes):
+            self.copies[(step - 1) * self.lanes + lane].wait_recv()
+
+    def sent(self):
+        for copy in self.copies:
+            copy.wait_send()
+
+
+class Mirror:
+    def __init__(self, count, sems):
+        unused_chip, unused_core, self.sibling, self.across = neighbours()
+        self.count, self.sems = count, sems
+        self.copies = [None] * (3 * count)
+
+    def give(self, number, ref):
+        self.copies[number] = remote(ref, ref, self.sems, number, self.sibling)
+        self.copies[self.count + number] = remote(
+            ref, ref, self.sems, self.count + number, self.across
+        )
+
+    def relay(self, number, ref):
+        self.copies[self.count + number].wait_recv()
+        self.copies[2 * self.count + number] = remote(
+            ref, ref, self.sems, 2 * self.count + number, self.sibling
+        )
+
+    def finish(self):
+        for number, copy in enumerate(self.copies):
+            if number // self.count != 1:
+                copy.wait_recv()
+            copy.wait_send()
+
+
+RING_STEPS = HEADS - 1
+QUARTERS = 4
+
+
+def start_kernel(
+    hidden_ref,
+    gains_ref,
+    q_ref,
+    kv_ref,
+    small_ref,
+    plproj_ref,
+    hidden_all,
+    gains_all,
+    q_head,
+    kv_all,
+    small_all,
+    plproj_all,
+    local_sems,
+    *sems,
+):
+    pairs = [sems[i : i + 2] for i in range(0, len(sems), 2)]
+    hidden_sems, gains_sems, q_sems, kv_sems, small_sems, plproj_sems = pairs[:6]
+    q_mirror_sems, kv_mirror_sems, small_mirror_sems, plproj_mirror_sems = pairs[6:]
+    index = lax.axis_index("fsdp")
+    chip, core, sibling, across = neighbours()
+    quarter = 2 * chip + core
+    other_quarter = 2 * (1 - chip) + core
+    place = ring_place(index)
+    ends = ring_ends(place)
+    others = [lax.rem(index + step, HEADS) for step in range(1, HEADS)]
+    greet([{"fsdp": other} for other in others] + [sibling, across])
+    rows = hidden_ref.shape[0]
+    shard = q_ref.shape[0]
+    deep = plproj_ref.shape[0]
+    q_rows = shard // QUARTERS
+    wide = plproj_ref.shape[1] // QUARTERS
+
+    locals_list = []
+    for source, target in (
+        (hidden_ref, hidden_all.at[span(index * rows, rows)]),
+        (gains_ref, gains_all.at[span(index * gains_ref.shape[0], gains_ref.shape[0])]),
+        (
+            q_ref.at[:, span(index * HEAD_DIM, HEAD_DIM)],
+            q_head.at[span(index * shard, shard)],
+        ),
+        (kv_ref, kv_all.at[span(index * shard, shard)]),
+        (small_ref, small_all.at[span(index * shard, shard)]),
+        (plproj_ref, plproj_all.at[span(index * deep, deep)]),
+    ):
+        copy = pltpu.make_async_copy(source, target, local_sems.at[len(locals_list)])
+        copy.start()
+        locals_list.append(copy)
+
+    hidden_part = rows // 4
+    gains_part = gains_ref.shape[0] // 2
+    shard_part = shard // QUARTERS // 2
+    wide_part = wide // 2
+
+    def shard_at(ref, part_of):
+        return lambda owner, lane: ref.at[
+            span(owner * shard + part_of * 2 * shard_part + lane * shard_part, shard_part)
+        ]
+
+    def plproj_at(part_of):
+        return lambda owner, lane: plproj_all.at[
+            span(owner * deep, deep), span(part_of * wide + lane * wide_part, wide_part)
+        ]
+
+    hidden = Ring(
+        place,
+        ends,
+        4,
+        hidden_sems,
+        lambda lane: hidden_ref.at[pl.ds(lane * hidden_part, hidden_part)],
+        lambda owner, lane: hidden_all.at[span(owner * rows + lane * hidden_part, hidden_part)],
+    )
+    gains = Ring(
+        place,
+        ends,
+        2,
+        gains_sems,
+        lambda lane: gains_ref.at[pl.ds(lane * gains_part, gains_part)],
+        lambda owner, lane: gains_all.at[
+            span(owner * gains_ref.shape[0] + lane * gains_part, gains_part)
+        ],
+    )
+
+    def shard_own(ref):
+        return lambda lane: ref.at[
+            span(quarter * 2 * shard_part + lane * shard_part, shard_part)
+        ]
+
+    kv = Ring(place, ends, 2, kv_sems, shard_own(kv_ref), shard_at(kv_all, quarter))
+    small = Ring(place, ends, 2, small_sems, shard_own(small_ref), shard_at(small_all, quarter))
+    plproj = Ring(
+        place,
+        ends,
+        2,
+        plproj_sems,
+        lambda lane: plproj_ref.at[:, span(quarter * wide + lane * wide_part, wide_part)],
+        plproj_at(quarter),
+    )
+    mirrored = [
+        (kv, Mirror(2 * RING_STEPS, kv_mirror_sems), shard_at(kv_all, other_quarter)),
+        (small, Mirror(2 * RING_STEPS, small_mirror_sems), shard_at(small_all, other_quarter)),
+        (plproj, Mirror(2 * RING_STEPS, plproj_mirror_sems), plproj_at(other_quarter)),
+    ]
+    q_mirror = Mirror(HEADS - 1, q_mirror_sems)
+    q_copies = []
+    q_landing = q_head.at[span(index * shard + quarter * q_rows, q_rows)]
+    for step, other in enumerate(others):
+        source = q_ref.at[span(quarter * q_rows, q_rows), span(other * HEAD_DIM, HEAD_DIM)]
+        q_copies.append(remote(source, q_landing, q_sems, step, {"fsdp": other}))
+
+    def q_at(step, part_of):
+        giver = lax.rem(index + HEADS - 1 - step, HEADS)
+        return q_head.at[span(giver * shard + part_of * q_rows, q_rows)]
+
+    def pass_on(step):
+        for ring, mirror, unused_there in mirrored:
+            for lane in range(2):
+                mirror.give((step - 1) * 2 + lane, ring.there(ring.owner(step, lane), lane))
+
+    def pass_again(step):
+        for ring, mirror, there in mirrored:
+            for lane in range(2):
+                mirror.relay((step - 1) * 2 + lane, there(ring.owner(step, lane), lane))
+
+    for step in range(RING_STEPS):
+        gains.send(step)
+        for ring, unused_mirror, unused_there in mirrored:
+            ring.send(step)
+        hidden.send(step)
+        if step >= 1:
+            pass_on(step)
+        if step >= 2:
+            pass_again(step - 1)
+        if step == 4:
+            for number, copy in enumerate(q_copies):
+                copy.wait_recv()
+                q_mirror.give(number, q_at(number, quarter))
+        if step == 5:
+            for number in range(HEADS - 1):
+                q_mirror.relay(number, q_at(number, other_quarter))
+    for ring, unused_mirror, unused_there in mirrored:
+        ring.arrive(RING_STEPS)
+    pass_on(RING_STEPS)
+    pass_again(RING_STEPS - 1)
+    pass_again(RING_STEPS)
+    gains.arrive(RING_STEPS)
+    hidden.arrive(RING_STEPS)
+    for ring, mirror, unused_there in mirrored:
+        ring.sent()
+        mirror.finish()
+    hidden.sent()
+    gains.sent()
+    for copy in q_copies:
+        copy.wait_send()
+    q_mirror.finish()
+    for copy in locals_list:
+        copy.wait()
+
+
+def start_gather(hidden, gains, q_proj, kv, small, pl_proj, number):
+    shard = q_proj.shape[0]
+    arrays = (hidden, gains, q_proj, kv, small, pl_proj)
+
+    def grown(item, rows=None, columns=None):
+        rows = rows or item.shape[0] * HEADS
+        return jax.ShapeDtypeStruct((rows, columns or item.shape[1]), item.dtype)
+
+    counts = [4 * RING_STEPS, 2 * RING_STEPS, RING_STEPS] + [2 * RING_STEPS] * 3
+    counts += [3 * RING_STEPS] + [6 * RING_STEPS] * 3
+    return pl.pallas_call(
+        start_kernel,
+        out_shape=[
+            grown(hidden),
+            grown(gains),
+            grown(q_proj, shard * HEADS, HEAD_DIM),
+            grown(kv),
+            grown(small),
+            grown(pl_proj),
+        ],
+        in_specs=[pl.BlockSpec(memory_space=pl.ANY)] * len(arrays),
+        out_specs=[pl.BlockSpec(memory_space=pl.ANY)] * len(arrays),
+        scratch_shapes=[pltpu.SemaphoreType.DMA((len(arrays),))]
+        + [pltpu.SemaphoreType.DMA((count,)) for count in counts for unused_side in range(2)],
+        compiler_params=pltpu.CompilerParams(collective_id=number, has_side_effects=True),
+    )(*arrays)
+
+
+def gather_kernel(own_ref, all_ref, local_sem, send_sem, recv_sem):
     rows = own_ref.shape[0]
-    part = rows // (2 * subs)
+    part = rows // 4
     index = lax.axis_index("fsdp")
     place = ring_place(index)
     ends = ring_ends(place)
     greet(ends)
     local = pltpu.make_async_copy(own_ref, all_ref.at[span(index * rows, rows)], local_sem)
     local.start()
-    copies = []
-    lanes = 2 * subs
-    for step in range(HEADS - 1):
-        for lane in range(lanes):
-            way = lane % 2
-            owner = ring_index(lax.rem(place + (step if way else HEADS - step), HEADS))
-            offset = lane * part
-            there = all_ref.at[span(owner * rows + offset, part)]
-            number = step * lanes + lane
-            if step:
-                copies[number - lanes].wait_recv()
-            copy = pltpu.make_async_remote_copy(
-                there if step else own_ref.at[pl.ds(offset, part)],
-                there,
-                send_sem.at[number],
-                recv_sem.at[number],
-                device_id=ends[way],
-                device_id_type=MESH,
-            )
-            copy.start()
-            copies.append(copy)
-    for number, copy in enumerate(copies):
-        if number >= (HEADS - 2) * lanes:
-            copy.wait_recv()
-        copy.wait_send()
+    ring = Ring(
+        place,
+        ends,
+        4,
+        (send_sem, recv_sem),
+        lambda lane: own_ref.at[pl.ds(lane * part, part)],
+        lambda owner, lane: all_ref.at[span(owner * rows + lane * part, part)],
+    )
+    for step in range(RING_STEPS):
+        ring.send(step)
+    ring.arrive(RING_STEPS)
+    ring.sent()
     local.wait()
 
 
-def ring_gather(own, number, subs=2):
-    steps = (HEADS - 1) * 2 * subs
+def ring_gather(own, number):
+    spec = pl.BlockSpec(memory_space=pl.ANY)
     return pl.pallas_call(
-        functools.partial(gather_kernel, subs),
-        out_shape=jax.ShapeDtypeStruct((own.shape[0] * HEADS, own.shape[1]), own.dtype),
-        in_specs=[pl.BlockSpec(memory_space=pl.ANY)],
-        out_specs=pl.BlockSpec(memory_space=pl.ANY),
-        scratch_shapes=[
-            pltpu.SemaphoreType.DMA,
-            pltpu.SemaphoreType.DMA((steps,)),
-            pltpu.SemaphoreType.DMA((steps,)),
-        ],
+        gather_kernel,
+        out_shape=[jax.ShapeDtypeStruct((own.shape[0] * HEADS, own.shape[1]), own.dtype)],
+        in_specs=[spec],
+        out_specs=[spec],
+        scratch_shapes=[pltpu.SemaphoreType.DMA]
+        + [pltpu.SemaphoreType.DMA((4 * RING_STEPS,))] * 2,
         compiler_params=pltpu.CompilerParams(collective_id=number, has_side_effects=True),
     )(own)
 
 
-def scatter_kernel(subs, part_ref, sum_ref, held, send_sem, recv_sem):
+def add_low(left, right):
+    return (left.astype(jnp.float32) + right.astype(jnp.float32)).astype(jnp.bfloat16)
+
+
+class RingSum:
+    def __init__(self, place, ends, lanes, sems, held, own):
+        self.place, self.ends, self.lanes, self.sems = place, ends, lanes, sems
+        self.held, self.own = held, own
+        self.copies = []
+
+    def send(self, step):
+        for lane in range(self.lanes):
+            ahead = step + 1 if lane % 2 else HEADS - 1 - step
+            owner = ring_index(lax.rem(self.place + ahead, HEADS))
+            number = step * self.lanes + lane
+            if step:
+                slot = number - self.lanes
+                self.copies[slot].wait_recv()
+                value = self.held[slot].astype(jnp.float32) + self.own(owner, lane)
+            else:
+                slot = RING_STEPS * self.lanes + lane
+                value = self.own(owner, lane)
+            self.held[slot] = value.astype(jnp.bfloat16)
+            self.copies.append(
+                remote(self.held.at[slot], self.held.at[number], self.sems, number, self.ends[lane % 2])
+            )
+
+    def last(self, index, lane):
+        number = (RING_STEPS - 1) * self.lanes + lane
+        self.copies[number].wait_recv()
+        return self.held[number].astype(jnp.float32) + self.own(index, lane)
+
+    def sent(self):
+        for copy in self.copies:
+            copy.wait_send()
+
+
+def scatter_kernel(part_ref, *refs):
+    if len(refs) > 4:
+        blocks_ref, sum_ref, block_sum, held, send_sem, recv_sem, block_held, block_send, block_recv = refs
+    else:
+        blocks_ref = None
+        sum_ref, held, send_sem, recv_sem = refs
     rows = sum_ref.shape[0]
-    part = rows // (2 * subs)
+    part = rows // 4
     index = lax.axis_index("fsdp")
     place = ring_place(index)
     ends = ring_ends(place)
     greet(ends)
+
+    def own(owner, lane):
+        return part_ref[span(owner * rows + lane * part, part), :].astype(jnp.float32)
+
+    rings = [RingSum(place, ends, 4, (send_sem, recv_sem), held, own)]
+    if blocks_ref is not None:
+        low_rows = block_sum.shape[0] // 2
+
+        def block_own(owner, lane):
+            return blocks_ref[owner, pl.ds(lane * low_rows, low_rows), :].astype(jnp.float32)
+
+        rings.append(RingSum(place, ends, 2, (block_send, block_recv), block_held, block_own))
+    for step in range(RING_STEPS):
+        for ring in rings:
+            ring.send(step)
+    for lane in range(4):
+        sum_ref[pl.ds(lane * part, part), :] = rings[0].last(index, lane)
+    if blocks_ref is not None:
+        for lane in range(2):
+            block_sum[pl.ds(lane * low_rows, low_rows), :] = (
+                rings[1].last(index, lane).astype(jnp.bfloat16)
+            )
+    for ring in rings:
+        ring.sent()
+
+
+def ring_scatter(parts, number, blocks=None):
+    rows = parts.shape[0] // HEADS
+    near = pl.BlockSpec(memory_space=pltpu.VMEM)
+    out_shape = [jax.ShapeDtypeStruct((rows, parts.shape[1]), jnp.float32)]
+    steps = 4 * RING_STEPS
+    scratch = [pltpu.VMEM((steps + 4, rows // 4, parts.shape[1]), jnp.bfloat16)]
+    scratch += [pltpu.SemaphoreType.DMA((steps,))] * 2
+    arrays = [parts]
+    if blocks is not None:
+        arrays.append(blocks)
+        out_shape.append(jax.ShapeDtypeStruct(blocks.shape[1:], jnp.bfloat16))
+        steps = 2 * RING_STEPS
+        shape = (steps + 2, blocks.shape[1] // 2, blocks.shape[2])
+        scratch += [pltpu.VMEM(shape, jnp.bfloat16)] + [pltpu.SemaphoreType.DMA((steps,))] * 2
+    return pl.pallas_call(
+        scatter_kernel,
+        out_shape=out_shape,
+        in_specs=[near] * len(arrays),
+        out_specs=[near] * len(out_shape),
+        scratch_shapes=scratch,
+        compiler_params=pltpu.CompilerParams(
+            collective_id=number, has_side_effects=True, vmem_limit_bytes=VMEM_BYTES
+        ),
+    )(*arrays)
+
+
+def lane_offset(lane, rows):
+    return (lane % 2) * (rows // 2) + (lane // 2) * (rows // 4)
+
+
+def tile_loop(count, size, body):
+    def step(number, carry):
+        body(span(number * size, size))
+        return carry
+
+    lax.fori_loop(0, count, step, 0)
+
+
+class Pair:
+    def __init__(self, place, step, rows):
+        half = rows // 2
+        behind = ring_index(lax.rem(place + HEADS - step, HEADS))
+        ahead = ring_index(lax.rem(place + step, HEADS))
+        self.half = half
+        self.rows = (span(behind * rows, half), span(ahead * rows + half, half))
+
+    def read(self, ref, columns=slice(None)):
+        return jnp.concatenate([ref[rows, columns] for rows in self.rows], axis=0)
+
+    def write(self, ref, columns, value):
+        for side, rows in enumerate(self.rows):
+            ref[rows, columns] = value[side * self.half : (side + 1) * self.half]
+
+
+GELU_ROOT = math.sqrt(2.0 / math.pi)
+GELU_CUBE = 0.044715
+TILE = 256
+
+
+def start_loads(pairs, sems):
     copies = []
-    lanes = 2 * subs
-    for step in range(HEADS - 1):
+    for number, (source, target) in enumerate(pairs):
+        copy = pltpu.make_async_copy(source, target, sems.at[number])
+        copy.start()
+        copies.append(copy)
+    return copies
+
+
+def ffn_kernel(
+    own_ref,
+    gate_any,
+    up_any,
+    down_any,
+    sum_ref,
+    all_ref,
+    act_ref,
+    slope_ref,
+    inner_ref,
+    gate,
+    up,
+    down,
+    block,
+    inner_block,
+    part,
+    held,
+    load_sems,
+    send_sem,
+    recv_sem,
+    sum_send,
+    sum_recv,
+):
+    rows, width = own_ref.shape
+    units = gate.shape[0]
+    piece = rows // 4
+    index = lax.axis_index("fsdp")
+    place = ring_place(index)
+    ends = ring_ends(place)
+    loads = start_loads(((gate_any, gate), (up_any, up), (down_any, down)), load_sems)
+    greet(ends)
+    ring = Ring(
+        place,
+        ends,
+        4,
+        (send_sem, recv_sem),
+        lambda lane: own_ref.at[pl.ds(lane_offset(lane, rows), piece)],
+        lambda owner, lane: all_ref.at[span(owner * rows + lane_offset(lane, rows), piece)],
+    )
+
+    def own(owner, lane):
+        return part[span(owner * rows + lane_offset(lane, rows), piece), :].astype(jnp.float32)
+
+    sums = RingSum(place, ends, 4, (sum_send, sum_recv), held, own)
+
+    def compute(step):
+        pair = Pair(place, step, rows)
+        block[...] = pair.read(all_ref)
+
+        def into(tile):
+            value = mul_t(block[...], gate[tile, :])
+            second = mul_t(block[...], up[tile, :])
+            square = value * value
+            bent = jnp.tanh(GELU_ROOT * value * (1.0 + GELU_CUBE * square))
+            share = 0.5 * (1.0 + bent)
+            act = value * share
+            slope = share + (0.5 * GELU_ROOT) * value * (1.0 - bent * bent) * (
+                1.0 + (3.0 * GELU_CUBE) * square
+            )
+            inner = low(act * second)
+            inner_block[:, tile] = inner
+            pair.write(act_ref, tile, low(act))
+            pair.write(slope_ref, tile, low(slope * second))
+            pair.write(inner_ref, tile, inner)
+
+        tile_loop(units // TILE, TILE, into)
+
+        def out(tile):
+            pair.write(part, tile, low(dot(inner_block[...], down[:, tile])))
+
+        tile_loop(width // (2 * TILE), 2 * TILE, out)
+
+    ring.send(0)
+    all_ref[span(index * rows, rows), :] = own_ref[...]
+    for copy in loads:
+        copy.wait()
+    compute(0)
+    for step in range(1, HEADS):
+        if step < RING_STEPS:
+            ring.send(step)
+        else:
+            ring.arrive(step)
+        compute(step)
+        sums.send(step - 1)
+    for lane in range(4):
+        sum_ref[pl.ds(lane_offset(lane, rows), piece), :] = sums.last(index, lane)
+    ring.sent()
+    sums.sent()
+
+
+def ffn_forward(own, gate, up, down, number):
+    rows, width = own.shape
+    units = gate.shape[0]
+    near, anywhere = pl.BlockSpec(memory_space=pltpu.VMEM), pl.BlockSpec(memory_space=pl.ANY)
+    total = rows * HEADS
+    steps = 4 * RING_STEPS
+    bf16 = jnp.bfloat16
+    inner = jax.ShapeDtypeStruct((total, units), bf16)
+    return pl.pallas_call(
+        ffn_kernel,
+        out_shape=[
+            jax.ShapeDtypeStruct((rows, width), jnp.float32),
+            jax.ShapeDtypeStruct((total, width), bf16),
+            inner,
+            inner,
+            inner,
+        ],
+        in_specs=[near] + [anywhere] * 3,
+        out_specs=[near] * 5,
+        scratch_shapes=[pltpu.VMEM((units, width), bf16)] * 3
+        + [
+            pltpu.VMEM((rows, width), bf16),
+            pltpu.VMEM((rows, units), bf16),
+            pltpu.VMEM((total, width), bf16),
+            pltpu.VMEM((steps + 4, rows // 4, width), bf16),
+            pltpu.SemaphoreType.DMA((3,)),
+        ]
+        + [pltpu.SemaphoreType.DMA((steps,))] * 4,
+        compiler_params=pltpu.CompilerParams(
+            collective_id=number, has_side_effects=True, vmem_limit_bytes=VMEM_BYTES
+        ),
+    )(own, gate, up, down)
+
+
+def ffn_back_kernel(
+    own_ref,
+    all_any,
+    act_any,
+    slope_any,
+    inner_any,
+    gate_any,
+    up_any,
+    down_any,
+    blocks_ref,
+    sum_ref,
+    down_out,
+    gate_out,
+    up_out,
+    far_down,
+    block_sum,
+    d_all,
+    tokens,
+    d_up,
+    d_gate,
+    inner,
+    gate,
+    up,
+    down,
+    block,
+    inner_block,
+    part,
+    held,
+    turned,
+    give,
+    keep,
+    theirs,
+    block_held,
+    load_sems,
+    store_sems,
+    *sems,
+):
+    ring_sems, sum_sems, fold_sems, block_sems, far_sems = [
+        sems[i : i + 2] for i in range(0, 10, 2)
+    ]
+    rows, width = own_ref.shape
+    units = gate.shape[0]
+    piece = rows // 4
+    index = lax.axis_index("fsdp")
+    place = ring_place(index)
+    ends = ring_ends(place)
+    unused_chip, core, sibling, across = neighbours()
+    load_down, load_act, load_slope, load_gate, load_up, load_inner, load_tokens = start_loads(
+        (
+            (down_any, down),
+            (act_any, d_up),
+            (slope_any, d_gate),
+            (gate_any, gate),
+            (up_any, up),
+            (inner_any, inner),
+            (all_any, tokens),
+        ),
+        load_sems,
+    )
+    greet(ends + (sibling, across))
+    ring = Ring(
+        place,
+        ends,
+        4,
+        ring_sems,
+        lambda lane: own_ref.at[pl.ds(lane_offset(lane, rows), piece)],
+        lambda owner, lane: d_all.at[span(owner * rows + lane_offset(lane, rows), piece)],
+    )
+
+    def own(owner, lane):
+        return part[span(owner * rows + lane_offset(lane, rows), piece), :].astype(jnp.float32)
+
+    low_rows = block_sum.shape[0] // 2
+
+    def block_own(owner, lane):
+        return blocks_ref[owner, pl.ds(lane * low_rows, low_rows), :].astype(jnp.float32)
+
+    sums = RingSum(place, ends, 4, sum_sems, held, own)
+    block_sums = RingSum(place, ends, 2, block_sems, block_held, block_own)
+
+    def compute(step):
+        pair = Pair(place, step, rows)
+        block[...] = pair.read(d_all)
+
+        def into(tile):
+            grad = mul_t(block[...], down[tile, :])
+            first = low(grad * pair.read(d_gate, tile).astype(jnp.float32))
+            second = low(grad * pair.read(d_up, tile).astype(jnp.float32))
+            pair.write(d_gate, tile, first)
+            pair.write(d_up, tile, second)
+            inner_block[0, :, tile] = first
+            inner_block[1, :, tile] = second
+
+        tile_loop(units // TILE, TILE, into)
+        if step == 0:
+            load_gate.wait()
+            load_up.wait()
+
+        def out(tile):
+            total = dot(inner_block[0], gate[:, tile]) + dot(inner_block[1], up[:, tile])
+            pair.write(part, tile, low(total))
+
+        tile_loop(width // (2 * TILE), 2 * TILE, out)
+
+    half = units // 2
+    folds, stores, swaps = [], [], []
+    jobs = (
+        (inner, d_all, down_out),
+        (d_gate, tokens, gate_out),
+        (d_up, tokens, up_out),
+    )
+
+    def outer_half(number, side, target):
+        left, right, unused_out = jobs[number]
+        turned[...] = left[:, span(side * half, half)].T
+
+        def tile_step(tile):
+            target[:, tile] = low(dot(turned[...], right[:, tile]))
+
+        tile_loop(width // (2 * TILE), 2 * TILE, tile_step)
+
+    def grads_give(number):
+        if number:
+            folds[number - 1].wait_send()
+        outer_half(number, 1 - core, give)
+        folds.append(remote(give, theirs.at[number], fold_sems, number, sibling))
+
+    def grads_keep(number):
+        if number > 1:
+            stores[number - 1].wait()
+        outer_half(number, core, keep)
+        folds[number].wait_recv()
+
+        def add(tile):
+            keep[tile, :] = add_low(keep[tile, :], theirs[number, tile, :])
+
+        tile_loop(half // 64, 64, add)
+        store = pltpu.make_async_copy(keep, jobs[number][2], store_sems.at[number])
+        store.start()
+        stores.append(store)
+        if not number:
+            store.wait()
+            swaps.append(remote(down_out, far_down, far_sems, 0, across))
+
+    ring.send(0)
+    d_all[span(index * rows, rows), :] = own_ref[...]
+    for copy in (load_down, load_act, load_slope):
+        copy.wait()
+    compute(0)
+    for step in range(1, HEADS):
+        if step < RING_STEPS:
+            ring.send(step)
+        else:
+            ring.arrive(step)
+        if step >= RING_STEPS - 1:
+            sums.send(step - RING_STEPS + 1)
+        compute(step)
+    load_inner.wait()
+    load_tokens.wait()
+    for step in range(RING_STEPS):
+        if step >= 2:
+            sums.send(step)
+        block_sums.send(step)
+        if step < 6:
+            if step % 2:
+                grads_keep(step // 2)
+            else:
+                grads_give(step // 2)
+    for lane in range(4):
+        sum_ref[pl.ds(lane_offset(lane, rows), piece), :] = sums.last(index, lane)
+    for lane in range(2):
+        block_sum[pl.ds(lane * low_rows, low_rows), :] = low(block_sums.last(index, lane))
+    for item in (ring, sums, block_sums):
+        item.sent()
+    folds[-1].wait_send()
+    stores[-1].wait()
+    swaps[0].wait()
+
+
+def ffn_back(own, arrays, weights, blocks, number):
+    rows, width = own.shape
+    units = weights[0].shape[0]
+    near, anywhere = pl.BlockSpec(memory_space=pltpu.VMEM), pl.BlockSpec(memory_space=pl.ANY)
+    total = rows * HEADS
+    steps = 4 * RING_STEPS
+    bf16 = jnp.bfloat16
+    counts = [steps, steps, 3, 2 * RING_STEPS, 1]
+    half = (units // 2, width)
+    low_rows = blocks.shape[1] // 2
+    return pl.pallas_call(
+        ffn_back_kernel,
+        out_shape=[jax.ShapeDtypeStruct((rows, width), jnp.float32)]
+        + [jax.ShapeDtypeStruct(half, bf16)] * 4
+        + [jax.ShapeDtypeStruct(blocks.shape[1:], bf16)],
+        in_specs=[near] + [anywhere] * 7 + [near],
+        out_specs=[near] + [anywhere] * 4 + [near],
+        scratch_shapes=[pltpu.VMEM((total, width), bf16)] * 2
+        + [pltpu.VMEM((total, units), bf16)] * 3
+        + [pltpu.VMEM((units, width), bf16)] * 3
+        + [
+            pltpu.VMEM((rows, width), bf16),
+            pltpu.VMEM((2, rows, units), bf16),
+            pltpu.VMEM((total, width), bf16),
+            pltpu.VMEM((steps + 4, rows // 4, width), bf16),
+            pltpu.VMEM((units // 2, total), bf16),
+            pltpu.VMEM(half, bf16),
+            pltpu.VMEM(half, bf16),
+            pltpu.VMEM((3,) + half, bf16),
+            pltpu.VMEM((2 * RING_STEPS + 2, low_rows, blocks.shape[2]), bf16),
+            pltpu.SemaphoreType.DMA((7,)),
+            pltpu.SemaphoreType.DMA((3,)),
+        ]
+        + [pltpu.SemaphoreType.DMA((count,)) for count in counts for unused_side in range(2)],
+        compiler_params=pltpu.CompilerParams(
+            collective_id=number, has_side_effects=True, vmem_limit_bytes=56 << 20
+        ),
+    )(own, *arrays, *weights, blocks)
+
+
+ACROSS = ((0, 2), (2, 0), (1, 3), (3, 1))
+SIBLING = ((0, 1), (1, 0), (2, 3), (3, 2))
+
+
+def tail_kernel(
+    grads_ref,
+    weights_ref,
+    blocks_ref,
+    early_ref,
+    sum_ref,
+    owned_ref,
+    early_all,
+    held,
+    part,
+    keep,
+    folded,
+    far,
+    near_sum,
+    key_held,
+    *sems,
+):
+    ring_sems, fold_sems, far_sems, swap_sems, key_sems, mirror_sems, early_sems = [
+        sems[i : i + 2] for i in range(0, 14, 2)
+    ]
+    load_sem = sems[14]
+    rows = sum_ref.shape[0]
+    half = rows // 2
+    piece = rows // 4
+    lanes = 4
+    index = lax.axis_index("fsdp")
+    chip, core, sibling, across = neighbours()
+    place = ring_place(index)
+    ends = ring_ends(place)
+    others = [lax.rem(index + step, HEADS) for step in range(1, HEADS)]
+    greet([{"fsdp": other} for other in others] + [sibling, across])
+    quarter_rows = blocks_ref.shape[2]
+    folds, loads = [], []
+    for side in range(2):
+        folds.append(
+            remote(blocks_ref.at[:, 2 * side + 1 - core], folded.at[side], fold_sems, side, sibling)
+        )
+        load = pltpu.make_async_copy(
+            blocks_ref.at[:, 2 * side + core], keep.at[side], load_sem.at[side]
+        )
+        load.start()
+        loads.append(load)
+
+    quarter = 2 * chip + core
+    own_rows = span(quarter * quarter_rows, quarter_rows)
+    other_rows = span((2 * (1 - chip) + core) * quarter_rows, quarter_rows)
+    early_all[own_rows, :] = early_ref[...]
+    early = Mirror(1, early_sems)
+    early.give(0, early_all.at[own_rows])
+
+    def owner_at(step, way):
+        return ring_index(lax.rem(place + (step + 1 if way else HEADS - 1 - step), HEADS))
+
+    def compute(step):
+        tops = [
+            grads_ref[span(owner_at(step, way) * rows + way * half, half), :] for way in range(2)
+        ]
+        part[...] = mul_t(jnp.concatenate(tops, axis=0), weights_ref[...])
+
+    def lane_rows(lane):
+        return pl.ds((lane % 2) * half + (lane // 2) * piece, piece)
+
+    across_sends, swaps, key_swaps = [], [], []
+    mirror = Mirror(1, mirror_sems)
+    rest = blocks_ref.shape[3] - HEAD_DIM
+    q_columns = HEADS * HEAD_DIM
+
+    def fold_step():
+        for side in range(2):
+            folds[side].wait_recv()
+            loads[side].wait()
+        for block in range(HEADS):
+            keep[1 - chip, block] = add_low(keep[1 - chip, block], folded[1 - chip, block])
+        across_sends.append(remote(keep.at[1 - chip], far, far_sems, 0, across))
+        for block in range(HEADS):
+            keep[chip, block] = add_low(keep[chip, block], folded[chip, block])
+
+    def swap_step():
+        across_sends[0].wait_recv()
+        for block in range(HEADS):
+            near_sum[block] = add_low(keep[chip, block], far[block])
+        mine = span(index * HEAD_DIM, HEAD_DIM)
+        for step, other in enumerate(others):
+            swaps.append(
+                remote(
+                    near_sum.at[other, :, pl.ds(0, HEAD_DIM)],
+                    owned_ref.at[own_rows, mine],
+                    swap_sems,
+                    step,
+                    {"fsdp": other},
+                )
+            )
+            key_swaps.append(
+                remote(
+                    near_sum.at[other, :, pl.ds(HEAD_DIM, rest)],
+                    key_held.at[index],
+                    key_sems,
+                    step,
+                    {"fsdp": other},
+                )
+            )
+        owned_ref[own_rows, mine] = near_sum[index, :, :HEAD_DIM]
+        key_held[index] = near_sum[index, :, HEAD_DIM:]
+
+    copies = []
+    for step in range(RING_STEPS):
+        compute(step)
         for lane in range(lanes):
-            way = lane % 2
-            owner = ring_index(lax.rem(place + (step + 1 if way else HEADS - 1 - step), HEADS))
-            mine = span(owner * rows + lane * part, part)
             number = step * lanes + lane
             if step:
                 copies[number - lanes].wait_recv()
+                held[number - lanes] = (
+                    held[number - lanes].astype(jnp.float32) + part[lane_rows(lane), :]
+                ).astype(jnp.bfloat16)
                 source = held.at[number - lanes]
-                source[...] = (
-                    source[...].astype(jnp.float32) + part_ref[mine, :].astype(jnp.float32)
-                ).astype(jnp.bfloat16)
             else:
-                source = part_ref.at[mine]
-            copy = pltpu.make_async_remote_copy(
-                source,
-                held.at[number],
-                send_sem.at[number],
-                recv_sem.at[number],
-                device_id=ends[way],
-                device_id_type=MESH,
-            )
-            copy.start()
-            copies.append(copy)
+                source = held.at[RING_STEPS * lanes + lane]
+                source[...] = part[lane_rows(lane), :].astype(jnp.bfloat16)
+            copies.append(remote(source, held.at[number], ring_sems, number, ends[lane % 2]))
+        if step == 1:
+            fold_step()
+        if step == 3:
+            early.relay(0, early_all.at[other_rows])
+        if step == 4:
+            swap_step()
+    tops = grads_ref[span(index * rows, rows), :]
+    part[...] = mul_t(tops, weights_ref[...])
     for lane in range(lanes):
-        number = (HEADS - 2) * lanes + lane
+        number = (RING_STEPS - 1) * lanes + lane
         copies[number].wait_recv()
-        mine = span(index * rows + lane * part, part)
-        sum_ref[pl.ds(lane * part, part), :] = held[number].astype(jnp.float32) + part_ref[
-            mine, :
-        ].astype(jnp.float32)
-    for copy in copies:
+        sum_ref[lane_rows(lane), :] = held[number].astype(jnp.float32) + part[lane_rows(lane), :]
+    for copy in swaps + key_swaps:
+        copy.wait_recv()
+    groups = HEADS // KV_HEADS
+    for head in range(KV_HEADS):
+        total = key_held[head * groups].astype(jnp.float32)
+        for step in range(1, groups):
+            total = total + key_held[head * groups + step].astype(jnp.float32)
+        total = total.astype(jnp.bfloat16)
+        for side in range(2):
+            base = q_columns + (side * KV_HEADS + head) * HEAD_DIM
+            owned_ref[own_rows, pl.ds(base, HEAD_DIM)] = total[
+                :, side * HEAD_DIM : (side + 1) * HEAD_DIM
+            ]
+    extra = key_held[0, :, 2 * HEAD_DIM :].astype(jnp.float32)
+    for step in range(1, HEADS):
+        extra = extra + key_held[step, :, 2 * HEAD_DIM :].astype(jnp.float32)
+    base = q_columns + 2 * KV_HEADS * HEAD_DIM
+    owned_ref[own_rows, pl.ds(base, rest - 2 * HEAD_DIM)] = extra.astype(jnp.bfloat16)
+    mirror.give(0, owned_ref.at[own_rows])
+    mirror.relay(0, owned_ref.at[other_rows])
+    mirror.finish()
+    early.finish()
+    for copy in copies + folds + across_sends + swaps + key_swaps:
         copy.wait_send()
 
 
-def ring_scatter(parts, number, subs=2):
-    rows = parts.shape[0] // HEADS
-    steps = (HEADS - 1) * 2 * subs
+def tail_scatter(grads, weights, blocks, early, number):
+    rows = grads.shape[0] // HEADS
+    width = weights.shape[0]
+    shard = width // HEADS
+    steps = 4 * RING_STEPS
+    quarter = shard // QUARTERS
+    across = blocks.shape[1]
+    rest = across - HEAD_DIM
+    blocks = blocks.reshape(HEADS, QUARTERS, quarter, across)
+    near = pl.BlockSpec(memory_space=pltpu.VMEM)
+    bf16 = jnp.bfloat16
+    counts = [steps, 2, 1, HEADS - 1, HEADS - 1, 3, 3]
+    owned = (HEADS + 2 * KV_HEADS) * HEAD_DIM + rest - 2 * HEAD_DIM
     return pl.pallas_call(
-        functools.partial(scatter_kernel, subs),
-        out_shape=jax.ShapeDtypeStruct((rows, parts.shape[1]), jnp.float32),
-        in_specs=[pl.BlockSpec(memory_space=pltpu.VMEM)],
-        out_specs=pl.BlockSpec(memory_space=pltpu.VMEM),
+        tail_kernel,
+        out_shape=[
+            jax.ShapeDtypeStruct((rows, width), jnp.float32),
+            jax.ShapeDtypeStruct((shard, owned), bf16),
+            jax.ShapeDtypeStruct((shard, early.shape[1]), bf16),
+        ],
+        in_specs=[near, near, pl.BlockSpec(memory_space=pl.ANY), near],
+        out_specs=[near] * 3,
         scratch_shapes=[
-            pltpu.VMEM((steps, rows // (2 * subs), parts.shape[1]), jnp.bfloat16),
-            pltpu.SemaphoreType.DMA((steps,)),
-            pltpu.SemaphoreType.DMA((steps,)),
-        ],
+            pltpu.VMEM((steps + 4, rows // 4, width), bf16),
+            pltpu.VMEM((rows, width), jnp.float32),
+            pltpu.VMEM((2, HEADS, quarter, across), bf16),
+            pltpu.VMEM((2, HEADS, quarter, across), bf16),
+            pltpu.VMEM((HEADS, quarter, across), bf16),
+            pltpu.VMEM((HEADS, quarter, across), bf16),
+            pltpu.VMEM((HEADS, quarter, rest), bf16),
+        ]
+        + [pltpu.SemaphoreType.DMA((count,)) for count in counts for unused_side in range(2)]
+        + [pltpu.SemaphoreType.DMA((2,))],
         compiler_params=pltpu.CompilerParams(
             collective_id=number, has_side_effects=True, vmem_limit_bytes=VMEM_BYTES
         ),
+    )(grads, weights, blocks, early)
+
+
+def gains_kernel(parts_ref, sum_ref, landed, totals, send_sem, recv_sem, rep_send, rep_recv):
+    index = lax.axis_index("fsdp")
+    rep = lax.axis_index("rep")
+    others = [lax.rem(index + step, HEADS) for step in range(1, HEADS)]
+    twins = [lax.rem(rep + step, QUARTERS) for step in range(1, QUARTERS)]
+    greet([{"fsdp": other} for other in others] + [{"rep": twin} for twin in twins])
+    sends = [
+        remote(parts_ref.at[other], landed.at[index], (send_sem, recv_sem), step, {"fsdp": other})
+        for step, other in enumerate(others)
+    ]
+    landed[index] = parts_ref[index]
+    for copy in sends:
+        copy.wait_recv()
+    total = landed[0]
+    for step in range(1, HEADS):
+        total = total + landed[step]
+    totals[rep] = total
+    twin_sends = [
+        remote(totals.at[rep], totals.at[rep], (rep_send, rep_recv), step, {"rep": twin})
+        for step, twin in enumerate(twins)
+    ]
+    for copy in twin_sends:
+        copy.wait_recv()
+    total = totals[0]
+    for step in range(1, QUARTERS):
+        total = total + totals[step]
+    sum_ref[...] = total
+    for copy in sends + twin_sends:
+        copy.wait_send()
+
+
+def gains_sum(parts, number):
+    near = pl.BlockSpec(memory_space=pltpu.VMEM)
+    return pl.pallas_call(
+        gains_kernel,
+        out_shape=jax.ShapeDtypeStruct(parts.shape[1:], parts.dtype),
+        in_specs=[near],
+        out_specs=near,
+        scratch_shapes=[
+            pltpu.VMEM(parts.shape, parts.dtype),
+            pltpu.VMEM((QUARTERS,) + parts.shape[1:], parts.dtype),
+        ]
+        + [pltpu.SemaphoreType.DMA((HEADS - 1,))] * 2
+        + [pltpu.SemaphoreType.DMA((QUARTERS - 1,))] * 2,
+        compiler_params=pltpu.CompilerParams(collective_id=number, has_side_effects=True),
     )(parts)
 
 
-def swap_kernel(own_ref, all_ref, local_sem, send_sem, recv_sem):
-    rows = own_ref.shape[0] // HEADS
-    index = lax.axis_index("fsdp")
-    others = [lax.rem(index + step, HEADS) for step in range(1, HEADS)]
-    greet([{"fsdp": other} for other in others])
-    mine = span(index * rows, rows)
-    copies = []
-    for step, other in enumerate(others):
-        copy = pltpu.make_async_remote_copy(
-            own_ref.at[span(other * rows, rows)],
-            all_ref.at[mine],
-            send_sem.at[step],
-            recv_sem.at[step],
-            device_id={"fsdp": other},
-            device_id_type=MESH,
-        )
-        copy.start()
-        copies.append(copy)
-    local = pltpu.make_async_copy(own_ref.at[mine], all_ref.at[mine], local_sem)
-    local.start()
-    for copy in copies:
-        copy.wait()
-    local.wait()
-
-
-def swap_blocks(own, number):
-    return pl.pallas_call(
-        swap_kernel,
-        out_shape=jax.ShapeDtypeStruct(own.shape, own.dtype),
-        in_specs=[pl.BlockSpec(memory_space=pl.ANY)],
-        out_specs=pl.BlockSpec(memory_space=pl.ANY),
-        scratch_shapes=[
-            pltpu.SemaphoreType.DMA,
-            pltpu.SemaphoreType.DMA((HEADS - 1,)),
-            pltpu.SemaphoreType.DMA((HEADS - 1,)),
-        ],
-        compiler_params=pltpu.CompilerParams(collective_id=number, has_side_effects=True),
-    )(own)
+def core_fold(value, axis):
+    half = value.shape[axis] // 2
+    core = lax.rem(lax.axis_index("rep"), 2)
+    give = lax.dynamic_slice_in_dim(value, (1 - core) * half, half, axis)
+    keep = lax.dynamic_slice_in_dim(value, core * half, half, axis)
+    return add_low(keep, lax.ppermute(give, "rep", SIBLING))
+
+
+def chip_fold(value, axis):
+    half = value.shape[axis] // 2
+    chip = lax.axis_index("rep") // 2
+    give = lax.dynamic_slice_in_dim(value, (1 - chip) * half, half, axis)
+    keep = lax.dynamic_slice_in_dim(value, chip * half, half, axis)
+    return add_low(keep, lax.ppermute(give, "rep", ACROSS))
+
+
+def quarter_fold(value):
+    value = value.reshape(value.shape[:-3] + (2, 2) + value.shape[-2:])
+    axis = value.ndim - 4
+    value = chip_fold(core_fold(value, axis + 1), axis)
+    return value.reshape(value.shape[:axis] + value.shape[axis + 2 :])
 
 
 def dot(left, right):
@@ -277,6 +1179,25 @@
 
 def low(value):
     return value.astype(jnp.bfloat16)
+
+
+def tree_places(lengths, parents, total):
+    count = lengths.shape[0]
+    labels = jnp.arange(count, dtype=jnp.int32)
+    ends = jnp.sum(jnp.where(labels[:, None] <= labels[None, :], lengths[:, None], 0), axis=0)
+    starts = ends - lengths
+    tokens = jnp.arange(total, dtype=jnp.int32)
+    segment = jnp.sum((ends[None, :] <= tokens[:, None]).astype(jnp.int32), axis=1)
+    parent_hot = (parents[:, None] == labels[None, :]) & (labels[:, None] > 0)
+    identity = labels[:, None] == labels[None, :]
+    reached = parent_hot | identity
+    for unused_step in range((count - 1).bit_length()):
+        reached = jnp.any(reached[:, :, None] & reached[None, :, :], axis=1)
+    offset = jnp.sum(jnp.where(reached & ~identity, lengths[None, :], 0), axis=1) - starts
+    member = segment[:, None] == labels[None, :]
+    reach = jnp.any(member[:, :, None] & reached[None, :, :], axis=1)
+    position = jnp.sum(jnp.where(member, offset[None, :], 0), axis=1) + tokens
+    return (tokens, member.astype(jnp.bfloat16), reach.astype(jnp.bfloat16), position)
 
 
 def head_plan(
@@ -319,7 +1240,16 @@
     packed = jnp.concatenate(gains + (q_norm, k_norm))
     pad = -packed.shape[0] % (32 * 128)
     packed = jnp.pad(packed, (0, pad)).reshape(-1, 128)
-    all_gains = ring_gather(packed, 0, 1).reshape(HEADS, -1).astype(jnp.float32)
+    hidden_all, gains_held, q_head, kv_all, small_all, full_plproj = start_gather(
+        hidden_in,
+        packed,
+        q_proj,
+        jnp.concatenate([k_proj, v_proj], axis=1),
+        jnp.concatenate([pl_gate, laurel_left, laurel_right], axis=1),
+        pl_proj,
+        0,
+    )
+    all_gains = gains_held.reshape(HEADS, -1).astype(jnp.float32)
     wide_gains = [all_gains[:, i * shard : (i + 1) * shard].reshape(-1) for i in range(len(gains))]
     gain_anorm, gain_apost, gain_lnorm, gain_fnorm, gain_fpost, gain_plpost = wide_gains
     at = len(gains) * shard
@@ -327,21 +1257,15 @@
     gain_qnorm = all_gains[:, at : at + piece].reshape(-1)
     gain_knorm = all_gains[:, at + piece : at + 2 * piece].reshape(-1)
 
-    hidden_all = ring_gather(hidden_in, 1)
-    q_blocks = q_proj.reshape(shard, HEADS, HEAD_DIM).transpose(1, 0, 2).reshape(-1, HEAD_DIM)
-    q_head = swap_blocks(q_blocks, 2)
-    kv_all = ring_gather(jnp.concatenate([k_proj, v_proj], axis=1), 3)
-    small_all = ring_gather(jnp.concatenate([pl_gate, laurel_left, laurel_right], axis=1), 4)
-    full_plproj = ring_gather(pl_proj, 5, 1)
     k_head = lax.dynamic_slice_in_dim(kv_all, key_head * HEAD_DIM, HEAD_DIM, 1)
     v_head = lax.dynamic_slice_in_dim(kv_all, (KV_HEADS + key_head) * HEAD_DIM, HEAD_DIM, 1)
     full_plgate = small_all[:, :per_layer]
     full_left = small_all[:, per_layer : per_layer + rank]
     full_right = small_all[:, per_layer + rank :]
 
-    tokens, member, reach, position = tree_tables(seg_lengths[0], seg_parents[0], total)
+    tokens, member, reach, position = tree_places(seg_lengths[0], seg_parents[0], total)
     depth = position.astype(jnp.float32)
-    seen = (jnp.dot(reach, member.T) > 0) & (tokens[None, :] <= tokens[:, None])
+    seen = (mul_t(reach, member) > 0) & (tokens[None, :] <= tokens[:, None])
 
     normed_all = low(norm_rows(hidden_all.astype(jnp.float32), gain_anorm))
     q_raw = dot(normed_all, q_head)
@@ -361,7 +1285,7 @@
     probs_low = low(probs)
     attended = dot(probs_low, v_low)
     attended_low = low(attended)
-    branch = ring_scatter(low(dot(attended_low, o_proj)), 6)
+    (branch,) = ring_scatter(low(dot(attended_low, o_proj)), 6)
 
     source = hidden_in.astype(jnp.float32)
     extra = layer_input.astype(jnp.float32)
@@ -374,12 +1298,9 @@
     ) * HALF_ROOT
     ffw_low = low(norm_rows(first_sum, gain_fnorm))
 
-    ffw_all = ring_gather(ffw_low, 7)
-    gate_val = mul_t(ffw_all, gate_proj)
-    up_val = mul_t(ffw_all, up_proj)
-    inner_low = low(gelu_mix(gate_val, up_val))
-    ffw_out = ring_scatter(low(dot(inner_low, down_proj)), 8)
-
+    ffw_out, ffw_all, act, slope, inner_low = ffn_forward(
+        ffw_low, gate_proj, up_proj, down_proj, 7
+    )
     second_sum = first_sum + norm_rows(ffw_out, gain_fpost)
     second_low = low(second_sum)
     pl_pre = dot(second_low, full_plgate)
@@ -395,33 +1316,43 @@
     d_pre_low = low(d_pre)
     grad_plgate = outer(second_low, d_pre_low)
     d_second = seed + mul_t(d_pre_low, full_plgate)
+    pl_blocks = jnp.concatenate(
+        [
+            low(grad_plgate).reshape(HEADS, shard, per_layer),
+            low(grad_plproj).reshape(HEADS, shard, per_layer),
+        ],
+        axis=-1,
+    )
+    pl_blocks = quarter_fold(pl_blocks.reshape(HEADS, QUARTERS, -1, 2 * per_layer))
     d_ffwout, grad_fpost = norm_back(ffw_out, gain_fpost, d_second)
 
-    d_ffw_all = ring_gather(low(d_ffwout), 9)
-    d_inner = mul_t(d_ffw_all, down_proj)
-    d_gate, d_up = mix_back(gate_val, up_val, d_inner)
-    d_gate_low = low(d_gate)
-    d_up_low = low(d_up)
-    d_ffwin = ring_scatter(low(dot(d_gate_low, gate_proj) + dot(d_up_low, up_proj)), 10)
-    ffw_grads = [
-        low(outer(d_gate_low, ffw_all)),
-        low(outer(d_up_low, ffw_all)),
-        low(outer(inner_low, d_ffw_all)),
+    d_ffwin, *rest = ffn_back(
+        low(d_ffwout),
+        (ffw_all, act, slope, inner_low),
+        (gate_proj, up_proj, down_proj),
+        pl_blocks,
+        9,
+    )
+    chip_grads, far_down, pl_sum = rest[:3], rest[3], rest[4]
+    late = chip_grads[2].shape[0] * 3 // 4
+    far_gate, far_up, far_last = [
+        lax.ppermute(item, "rep", ACROSS)
+        for item in (chip_grads[1], chip_grads[2][:late], chip_grads[2][late:])
     ]
-    sum_gate, sum_up, sum_down = [lax.psum(item, "rep").astype(jnp.float32) for item in ffw_grads]
 
     d_first_part, grad_fnorm = norm_back(first_sum, gain_fnorm, d_ffwin)
     d_scaled = (d_second + d_first_part) * HALF_ROOT
     d_branch, grad_apost = norm_back(branch, gain_apost, d_scaled)
     d_lowrank, grad_lnorm = norm_back(low_rank, gain_lnorm, d_scaled)
     d_lowrank_low = low(d_lowrank)
-    d_branch_all = ring_gather(low(d_branch), 11)
+    (d_branch_all,) = ring_gather(low(d_branch), 11)
     grad_right = outer(d_lowrank_low, left_low)
     d_left_low = low(dot(d_lowrank_low, full_right))
     grad_left = outer(normed_low, d_left_low)
 
     d_att_low = low(mul_t(d_branch_all, o_proj))
     grad_o = outer(attended_low, d_branch_all)
+    o_quarter = quarter_fold(low(grad_o).reshape(QUARTERS, -1, width))
     delta = jnp.sum(d_att_low.astype(jnp.float32) * attended, axis=-1, keepdims=True)
     d_probs = mul_t(d_att_low, v_low)
     d_scores = low(probs * (d_probs - delta) * scale)
@@ -435,59 +1366,65 @@
     d_q_low = low(d_qraw)
     d_k_low = low(d_kraw)
     d_v_low = low(d_value)
-    d_normed_part = mul_t(d_q_low, q_head) + mul_t(d_k_low, k_head) + mul_t(d_v_low, v_head)
-    d_normed = d_scaled + mul_t(d_left_low, full_left) + ring_scatter(low(d_normed_part), 12)
+    d_qkv = jnp.concatenate([d_q_low, d_k_low, d_v_low], axis=1)
+    qkv_head = jnp.concatenate([q_head, k_head, v_head], axis=1)
+    d_qkv, far_gate, far_up = lax.optimization_barrier((d_qkv, far_gate, far_up))
+    blocks = jnp.concatenate(
+        [low(outer(normed_all, d_qkv)), low(grad_left), low(grad_right)], axis=1
+    )
+    d_normed_sum, owned, early = tail_scatter(
+        d_qkv, qkv_head, blocks, jnp.concatenate([o_quarter, pl_sum], axis=1), 12
+    )
+    owned = owned.astype(jnp.float32)
+    early = early.astype(jnp.float32)
+    key_at = width
+    value_at = key_at + KV_HEADS * HEAD_DIM
+    left_at = value_at + KV_HEADS * HEAD_DIM
+    d_normed = d_scaled + mul_t(d_left_low, full_left) + d_normed_sum
     d_source_part, grad_anorm = norm_back(source, gain_anorm, d_normed)
     d_source = d_scaled + d_source_part
 
-    head_grads = low(outer(normed_all, jnp.concatenate([d_q_low, d_k_low, d_v_low], axis=1)))
-    head_grads = swap_blocks(head_grads, 13).reshape(HEADS, shard, 3 * HEAD_DIM)
-    q_part = head_grads[:, :, :HEAD_DIM].transpose(1, 0, 2).reshape(shard, -1)
-    kv_part = head_grads[:, :, HEAD_DIM:].astype(jnp.float32)
-    kv_part = low(jnp.sum(kv_part.reshape(KV_HEADS, groups, shard, -1), axis=1))
-    k_part = kv_part[:, :, :HEAD_DIM].transpose(1, 0, 2).reshape(shard, -1)
-    v_part = kv_part[:, :, HEAD_DIM:].transpose(1, 0, 2).reshape(shard, -1)
-
-    def scatter(value):
-        return lax.psum_scatter(low(value), "fsdp", scatter_dimension=0, tiled=True)
-
-    def over_trees(value):
-        return lax.psum(low(value), "rep").astype(jnp.float32)
-
+    far_grads = [far_down, far_gate, jnp.concatenate([far_up, far_last], axis=0)]
+    sums = []
+    core = lax.rem(lax.axis_index("rep"), 2)
+    for item, far in zip(chip_grads, far_grads):
+        both = add_low(item, far)
+        other = lax.ppermute(both, "rep", SIBLING)
+        halves = [jnp.where(core == 0, both, other), jnp.where(core == 0, other, both)]
+        sums.append(jnp.concatenate(halves, axis=0).astype(jnp.float32))
+    sum_down, sum_gate, sum_up = sums
     small_grads = [grad_anorm, grad_apost, grad_lnorm, grad_fnorm, grad_fpost, grad_plpost]
-    small_sums = lax.psum(jnp.concatenate(small_grads + [grad_qnorm, grad_knorm]), ("rep", "fsdp"))
-
-    def own_part(start, size):
-        return lax.dynamic_slice_in_dim(small_sums, start + index * size, size)
-
-    own = [own_part(i * width, shard) for i in range(len(small_grads))]
+    parts = [item.reshape(HEADS, shard) for item in small_grads]
+    parts += [item.reshape(HEADS, piece) for item in (grad_qnorm, grad_knorm)]
+    parts = jnp.concatenate(parts, axis=1)
+    parts = jnp.pad(parts, ((0, 0), (0, -parts.shape[1] % 1024))).reshape(HEADS, -1, 128)
+    small_sums = gains_sum(parts, 13).reshape(-1)
+    own = [small_sums[i * shard : (i + 1) * shard] for i in range(len(small_grads))]
     sum_anorm, sum_apost, sum_lnorm, sum_fnorm, sum_fpost, sum_plpost = own
-    sum_qnorm = own_part(len(small_grads) * width, piece)
-    sum_knorm = own_part(len(small_grads) * width + HEAD_DIM, piece)
-    mixed = scatter(jnp.concatenate([grad_plgate, grad_left, grad_right], axis=1))
-    mixed = over_trees(mixed)
+    sum_qnorm = small_sums[at : at + piece]
+    sum_knorm = small_sums[at + piece : at + 2 * piece]
     return (
         low(result),
         low(d_source),
         low(d_extra),
         sum_anorm,
-        over_trees(q_part),
-        over_trees(k_part),
-        over_trees(v_part),
+        owned[:, :width],
+        owned[:, key_at:value_at],
+        owned[:, value_at:left_at],
         sum_qnorm,
         sum_knorm,
-        over_trees(grad_o),
+        early[:, :width],
         sum_apost,
-        mixed[:, per_layer : per_layer + rank],
-        mixed[:, per_layer + rank :],
+        owned[:, left_at : left_at + rank],
+        owned[:, left_at + rank :],
         sum_lnorm,
         sum_fnorm,
         sum_gate,
         sum_up,
         sum_down,
         sum_fpost,
-        mixed[:, :per_layer],
-        over_trees(scatter(grad_plproj)),
+        early[:, width : width + per_layer],
+        early[:, width + per_layer :].reshape(pl_proj.shape),
         sum_plpost,
     )
 

time: 1030 us -> 748 us (0.73)
  Pallas kernels: 556 us -> 456 us
  waiting for transfers between devices: 185 us -> 90.9 us
  matrix products: 139 us -> 47.4 us
  blocking collectives: 40.2 us -> 0 us
  other arithmetic: 51.9 us -> 82.6 us
  local copies, waits for them, and re-layouts: 31.3 us -> 53.2 us
  between operations: 15.9 us -> 2.39 us
    psum x1 -> x0, waiting for transfers between devices: 185 us -> none  [over_trees(): return lax.psum(low(value), 'rep').astype(jnp.float32)]
    pallas_call x14 -> x7, Pallas kernels: 551 us -> 451 us  [the longest x1 114 us: ffn_back(): pl.pallas_call(ffn_back_kernel, out_shape=[jax.ShapeDtypeStruct((rows, wi...]
    ppermute x0 -> x10, waiting for transfers between devices: none -> 90.9 us  [the longest x2 90.9 us: chip_fold(): return add_low(keep, lax.ppermute(give, 'rep', ACROSS))]
    psum x1 -> x0, blocking collectives: 40.2 us -> none  [head_plan(): lax.psum(jnp.concatenate(small_grads + [grad_qnorm, grad_knorm]), ('rep',...]
    dot_general x13 -> x8, matrix products: 52.4 us -> 15.8 us  [mul_t(): lax.dot_general(left, right, (((1,), (1,)), ((), ())), preferred_element_...]
    dot_general x11 -> x8, matrix products: 33.6 us -> 13.1 us  [outer(): lax.dot_general(left, right, (((0,), (0,)), ((), ())), preferred_element_...]
    dot_general x15 -> x0, matrix products: 17.6 us -> none  [the longest x13 11.2 us: tree_tables(): jnp.dot(parent_hot, held)]
    dot_general x12 -> x9, matrix products: 35 us -> 18.5 us  [dot(): return jnp.dot(left, right, preferred_element_type=jnp.float32)]
  transfers between devices with their start and end apart: 3 -> 10, of which waited for: 1 -> 2; matrix products, arithmetic and copies ran while one was open for 10% -> 10% of each run, Pallas kernels for 24% -> 12%
where the time goes in v2:
time: 748 us; the launch traced here: 738 us
  Pallas kernels  456 us (61%)
  waiting for transfers between devices  90.9 us (12%)
  other arithmetic  82.6 us (11%)
  local copies, waits for them, and re-layouts  53.2 us (7%)
  matrix products  47.4 us (6%)
    pallas_call x1, Pallas kernels, ffn_back(): pl.pallas_call(ffn_back_kernel, out_shape=[jax.ShapeDtypeStruct((rows, wi...  114 us
    ppermute x2, waiting for transfers between devices, chip_fold(): return add_low(keep, lax.ppermute(give, 'rep', ACROSS))  90.9 us
    pallas_call x1, Pallas kernels, ffn_forward(): pl.pallas_call(ffn_kernel, out_shape=[jax.ShapeDtypeStruct((rows, width),...  88.3 us
    pallas_call x1, Pallas kernels, start_gather(): pl.pallas_call(start_kernel, out_shape=[grown(hidden), grown(gains), grow...  76.6 us
    pallas_call x1, Pallas kernels, tail_scatter(): pl.pallas_call(tail_kernel, out_shape=[jax.ShapeDtypeStruct((rows, width)...  75 us
    pallas_call x1, Pallas kernels, ring_scatter(): pl.pallas_call(scatter_kernel, out_shape=out_shape, in_specs=[near] * len...  43.6 us
    pallas_call x1, Pallas kernels, ring_gather(): pl.pallas_call(gather_kernel, out_shape=[jax.ShapeDtypeStruct((own.shape[...  43 us
    dot_general x9, matrix products, dot(): return jnp.dot(left, right, preferred_element_type=jnp.float32)  18.5 us
  transfers between devices with their start and end apart: 10, of which 2 were waited for; matrix products, arithmetic and copies ran while one was open for 10% of the time, Pallas kernels for 12%

profile of v2, /device:TPU:0, one launch (start us, length us, event | category | flops | bytes accessed | tf_op | source)
XLA Modules:
  0.0 737.8 jit_solution(12499158552908107044)
XLA Ops:
  0.7 5.5 concatenate.72
  13.4 76.6 %shard_map.399 = (bf16[1024,2048]{1,0:T(8,128)(2,1)}, bf16[256,128]{1,0:T(8,128)(2,1)}, bf16[2048,256]{1,0:T(8,128)(2,1)}, bf16[2048,1024]{1,0:T(8,128)(2,1)}, b...) custom-call(bf16[128,2048]{1,0:T(8,128)(2,1)} %hidden_ref.1, bf16[32,128]{1,0:T(8,128)(2,1)} %pad_bitcast_fusion.1.gains_ref, ...), custom_call_target="tpu_custom_call" | custom-call | tf_op jit(solution)/shard_map/pallas_call | solution.py:364
  94.1 3.4 fusion
  97.6 2.8 constant_dynamic-slice_fusion.2
  103.1 2.5 copy.86
  105.8 5.0 multiply_reduce_fusion.17
  114.9 4.1 fusion.124
  121.9 3.7 fusion.137
  125.6 4.9 online-softmax
  133.0 43.6 %shard_map.400 = f32[128,2048]{1,0:T(8,128)S(1)} custom-call(bf16[1024,2048]{1,0:T(8,128)(2,1)S(1)} %convolution_convert_fusion.part_ref), custom_call_target="tpu_custom_call" | custom-call | tf_op jit(solution)/shard_map/pallas_call | solution.py:508
  179.3 88.3 %shard_map.401 = (f32[128,2048]{1,0:T(8,128)S(1)}, bf16[1024,2048]{1,0:T(8,128)(2,1)}, bf16[1024,1024]{1,0:T(8,128)(2,1)S(1)}, bf16[1024,1024]{1,0:T(8,128)(2,1)S(1)}, bf16[1024,1024]{1,0:T(8,128)(2,1)}) custom-call(bf16[128,2048]{1,0:T(8,128)(2,1)S(1)} %multiply_convert_fusion.1.own_ref, bf16[1024,2048]{1,0:T(8,128)(2,1)} %gate_any.3, ...), custom_call_target="tpu_custom_call" | custom-call | tf_op jit(solution)/shard_map/pallas_call | solution.py:660
  276.1 2.7 convolution_convert_fusion.3
  281.2 2.7 fusion.33
  285.0 3.8 fusion.5
  300.4 10.6 %collective-permute-done.1 = bf16[8,1,1,64,512]{4,3,0,2,1:T(8,128)(2,1)} collective-permute-done((bf16[8,1,1,64,512]{4,3,0,2,1:T(8,128)(2,1)}, bf16[8,1,1,64,512]{4,3,0,2,1:T(8,128)(2,1)}, u32[]{:S(2)}, u32[]{:S(2)}) %collective-permute-start.1) | collective-permute-done | bytes 524320 | tf_op jit(solution)/shard_map/ppermute | solution.py:1166
  313.2 113.5 %shard_map.402 = (f32[128,2048]{1,0:T(8,128)}, bf16[512,2048]{1,0:T(8,128)(2,1)}, bf16[512,2048]{1,0:T(8,128)(2,1)}, bf16[512,2048]{1,0:T(8,128)(2,1)}, bf16[512...) custom-call(bf16[128,2048]{1,0:T(8,128)(2,1)} %fusion.22.own_ref, bf16[1024,2048]{1,0:T(8,128)(2,1)} %get-tuple-element.52.all_any, ...), custom_call_target="tpu_custom_call" | custom-call | tf_op jit(solution)/shard_map/pallas_call | solution.py:875
  432.1 43.0 %shard_map.403 = bf16[1024,2048]{1,0:T(8,128)(2,1)} custom-call(bf16[128,2048]{1,0:T(8,128)(2,1)} %get-tuple-element.184.own_ref), custom_call_target="tpu_custom_call" | custom-call | tf_op jit(solution)/shard_map/pallas_call | solution.py:408
  475.2 3.7 multiply_reduce_fusion.6
  489.6 2.9 fusion.63
  503.3 4.5 add_convert_fusion
  511.2 80.3 %collective-permute-done.5 = bf16[1,1,64,2048]{3,2,1,0:T(8,128)(2,1)S(1)} collective-permute-done((bf16[1,1,64,2048]{3,2,1,0:T(8,128)(2,1)S(1)}, bf16[1,1,64,2048]{3,2,1,0:T(8,128)(2,1)S(1)}, u32[]{:S(2)}, u32[]{:S(2)}) %collective-permute-start.5) | collective-permute-done | bytes 262176 | tf_op jit(solution)/shard_map/ppermute | solution.py:1166
  591.6 4.2 convolution_convert_fusion.1
  597.8 6.2 copy.98
  604.1 75.0 %shard_map.404 = (f32[128,2048]{1,0:T(8,128)S(1)}, bf16[256,3200]{1,0:T(8,128)(2,1)S(1)}, bf16[256,2560]{1,0:T(8,128)(2,1)S(1)}) custom-call(bf16[1024,768]{1,0:T(8,128)(2,1)S(1)} %pad_maximum_fusion.2.grads_ref, bf16[2048,768]{1,0:T(8,128)(2,1)} %pad_maximum_fusion.1.weights_ref, bf16[8,4,64,896]{3,2,1,0:T(8,128)(2,1)} %bitcast.118, ...), custom_call_target="tpu_custom_call" | custom-call | tf_op jit(solution)/shard_map/pallas_call | solution.py:1079
  682.7 10.7 %shard_map.405 = f32[16,128]{1,0:T(8,128)} custom-call(f32[8,16,128]{2,1,0:T(8,128)} %bitcast.122), custom_call_target="tpu_custom_call" | custom-call | tf_op jit(solution)/shard_map/pallas_call | solution.py:1138
  693.5 4.6 add_convert_fusion.2
  700.6 3.8 add_convert_fusion.1
  706.0 4.5 broadcast_select_fusion.1
  716.8 6.0 maximum_convert_fusion.2
  724.0 2.5 broadcast_select_fusion.5
  726.5 4.3 maximum_convert_fusion
  733.3 4.3 maximum_convert_fusion.1
  (362 shorter events, 101.0 us)
Async XLA Ops:
  0.7 129.8 %copy-start = (bf16[256,2048]{1,0:T(8,128)(2,1)S(1)}, bf16[256,2048]{1,0:T(8,128)(2,1)}, u32[]{:S(2)}) copy-start(bf16[256,2048]{1,0:T(8,128)(2,1)} %param.35) | copy-start | bytes 3145732
  0.7 90.4 %copy-start.19 = (bf16[128,2048]{1,0:T(8,128)(2,1)S(1)}, bf16[128,2048]{1,0:T(8,128)(2,1)}, u32[]{:S(2)}) copy-start(bf16[128,2048]{1,0:T(8,128)(2,1)} %hidden_ref.1) | copy-start | bytes 1572868
  9.8 87.7 %copy-start.98 = (f32[128]{0:T(128)}, f32[128]{0:T(128)S(1)}, u32[]{:S(2)}) copy-start(f32[128]{0:T(128)S(1)} %fusion.30) | copy-start | bytes 1540
  91.1 86.3 %copy-start.78 = (f32[128]{0:T(128)}, f32[128]{0:T(128)S(1)}, u32[]{:S(2)}) copy-start(f32[128]{0:T(128)S(1)} %fusion.111) | copy-start | bytes 1540
  94.1 83.3 %copy-start.8 = (f32[128,2048]{1,0:T(8,128)}, f32[128,2048]{1,0:T(8,128)S(1)}, u32[]{:S(2)}) copy-start(f32[128,2048]{1,0:T(8,128)S(1)} %get-tuple-element.210) | copy-start | bytes 3145732
  94.1 83.3 %copy-start.86 = (f32[128]{0:T(128)}, f32[128]{0:T(128)S(1)}, u32[]{:S(2)}) copy-start(f32[128]{0:T(128)S(1)} %fusion.112) | copy-start | bytes 1540
  177.3 90.3 %copy-start.88 = (f32[128]{0:T(128)}, f32[128]{0:T(128)S(1)}, u32[]{:S(2)}) copy-start(f32[128]{0:T(128)S(1)} %fusion.110) | copy-start | bytes 1540
  178.0 89.9 %copy-start.6 = (f32[128,2048]{1,0:T(8,128)}, f32[128,2048]{1,0:T(8,128)S(1)}, u32[]{:S(2)}) copy-start(f32[128,2048]{1,0:T(8,128)S(1)} %get-tuple-element.156) | copy-start | bytes 3145732
  284.9 8.1 %collective-permute-start = (bf16[8,2,1,64,512]{4,3,0,2,1:T(8,128)(2,1)}, bf16[8,2,1,64,512]{4,3,0,2,1:T(8,128)(2,1)}, u32[]{:S(2)}, u32[]{:S(2)}) collective-permute-start(bf16[8,2,1,64,512]{4,3,0,2,1:T(8,128)(2,1)} %copy.109), channel_id=1, source_target_pairs={{0,8},{8,0},{16,24},{24,16},{1,9},{9,1},{17,25},{25,17},{2,10},{10... | collective-permute-start | bytes 3145736 | tf_op jit(solution)/shard_map/ppermute | solution.py:1158
  296.4 14.6 %collective-permute-start.1 = (bf16[8,1,1,64,512]{4,3,0,2,1:T(8,128)(2,1)}, bf16[8,1,1,64,512]{4,3,0,2,1:T(8,128)(2,1)}, u32[]{:S(2)}, u32[]{:S(2)}) collective-permute-start(bf16[8,1,1,64,512]{4,3,0,2,1:T(8,128)(2,1)} %constant_dynamic-slice_fusion.1), channel_id=1, source_target_pairs={{0,16},{16,0},{8,24},{24,8},{1,17},{17,1},{9,25},{25,9},{2,18},{18... | collective-permute-start | bytes 1572872 | tf_op jit(solution)/shard_map/ppermute | solution.py:1166
  313.2 113.6 %copy-start.7 = (f32[128,2048]{1,0:T(8,128)S(1)}, f32[128,2048]{1,0:T(8,128)}, u32[]{:S(2)}) copy-start(f32[128,2048]{1,0:T(8,128)} %copy-done.6) | copy-start | bytes 3145732
  313.2 113.6 %copy-start.97 = (f32[128]{0:T(128)S(1)}, f32[128]{0:T(128)}, u32[]{:S(2)}) copy-start(f32[128]{0:T(128)} %copy-done.96) | copy-start | bytes 1540
  313.2 115.1 %copy-start.106 = (f32[128]{0:T(128)S(1)}, f32[128]{0:T(128)}, u32[]{:S(2)}) copy-start(f32[128]{0:T(128)} %copy-done.105) | copy-start | bytes 1540
  313.2 115.1 %copy-start.9 = (f32[128,2048]{1,0:T(8,128)S(1)}, f32[128,2048]{1,0:T(8,128)}, u32[]{:S(2)}) copy-start(f32[128,2048]{1,0:T(8,128)} %copy-done.8) | copy-start | bytes 3145732
  313.2 115.1 %copy-start.24 = (f32[128,2048]{1,0:T(8,128)S(1)}, f32[128,2048]{1,0:T(8,128)}, u32[]{:S(2)}) copy-start(f32[128,2048]{1,0:T(8,128)} %get-tuple-element.217) | copy-start | bytes 3145732
  313.2 115.1 %copy-start.87 = (f32[128]{0:T(128)S(1)}, f32[128]{0:T(128)}, u32[]{:S(2)}) copy-start(f32[128]{0:T(128)} %copy-done.86) | copy-start | bytes 1540
  313.2 115.1 %copy-start.89 = (f32[128]{0:T(128)S(1)}, f32[128]{0:T(128)}, u32[]{:S(2)}) copy-start(f32[128]{0:T(128)} %copy-done.88) | copy-start | bytes 1540
  313.2 115.1 %copy-start.104 = (f32[128]{0:T(128)S(1)}, f32[128]{0:T(128)}, u32[]{:S(2)}) copy-start(f32[128]{0:T(128)} %get-tuple-element.207) | copy-start | bytes 1540
  494.7 97.0 %collective-permute-start.2 = (bf16[512,2048]{1,0:T(8,128)(2,1)}, bf16[512,2048]{1,0:T(8,128)(2,1)}, u32[]{:S(2)}, u32[]{:S(2)}) collective-permute-start(bf16[512,2048]{1,0:T(8,128)(2,1)} %get-tuple-element.57), channel_id=1, source_target_pairs={{0,16},{16,0},{8,24},{24,8},{1,17},{17,1},{9,25},{25,9},{2,18},{18... | collective-permute-start | bytes 6291464 | tf_op jit(solution)/shard_map/ppermute | solution.py:1339
  496.2 95.4 %collective-permute-start.3 = (bf16[384,2048]{1,0:T(8,128)(2,1)}, bf16[384,2048]{1,0:T(8,128)(2,1)}, u32[]{:S(2)}, u32[]{:S(2)}) collective-permute-start(bf16[384,2048]{1,0:T(8,128)(2,1)} %slice.132), channel_id=1, source_target_pairs={{0,16},{16,0},{8,24},{24,8},{1,17},{17,1},{9,25},{25,9},{2,18},{18... | collective-permute-start | bytes 4718600 | tf_op jit(solution)/shard_map/ppermute | solution.py:1339
  499.3 9.5 %collective-permute-start.4 = (bf16[2,1,64,2048]{3,2,1,0:T(8,128)(2,1)}, bf16[2,1,64,2048]{3,2,1,0:T(8,128)(2,1)}, u32[]{:S(2)}, u32[]{:S(2)}) collective-permute-start(bf16[2,1,64,2048]{3,2,1,0:T(8,128)(2,1)} %constant_dynamic-slice_fusion), channel_id=1, source_target_pairs={{0,8},{8,0},{16,24},{24,16},{1,9},{9,1},{17,25},{25,17},{2,10},{10... | collective-permute-start | bytes 1572872 | tf_op jit(solution)/shard_map/ppermute | solution.py:1158
  501.8 198.7 %collective-permute-start.7 = (bf16[128,2048]{1,0:T(8,128)(2,1)}, bf16[128,2048]{1,0:T(8,128)(2,1)}, u32[]{:S(2)}, u32[]{:S(2)}) collective-permute-start(bf16[128,2048]{1,0:T(8,128)(2,1)} %slice.149), channel_id=1, source_target_pairs={{0,16},{16,0},{8,24},{24,8},{1,17},{17,1},{9,25},{25,9},{2,18},{18... | collective-permute-start | bytes 1572872 | tf_op jit(solution)/shard_map/ppermute | solution.py:1339
  507.8 198.2 %collective-permute-start.9 = (bf16[512,2048]{1,0:T(8,128)(2,1)}, bf16[512,2048]{1,0:T(8,128)(2,1)}, u32[]{:S(2)}, u32[]{:S(2)}) collective-permute-start(bf16[512,2048]{1,0:T(8,128)(2,1)} %add_convert_fusion), channel_id=1, source_target_pairs={{0,8},{8,0},{16,24},{24,16},{1,9},{9,1},{17,25},{25,17},{2,10},{10... | collective-permute-start | bytes 6291464 | tf_op jit(solution)/shard_map/ppermute | solution.py:1392
  508.5 83.1 %copy-start.59 = (bf16[64,512]{1,0:T(8,128)(2,1)S(1)}, bf16[64,512]{1,0:T(8,128)(2,1)}, u32[]{:S(2)}) copy-start(bf16[64,512]{1,0:T(8,128)(2,1)} %get-tuple-element.60) | copy-start | bytes 196612
  508.5 83.1 %copy-start.38 = (bf16[1024,2048]{1,0:T(8,128)(2,1)S(1)}, bf16[1024,2048]{1,0:T(8,128)(2,1)}, u32[]{:S(2)}) copy-start(bf16[1024,2048]{1,0:T(8,128)(2,1)} %get-tuple-element.45) | copy-start | bytes 12582916
  508.5 83.1 %copy-start.91 = (f32[1024]{0:T(1024)S(1)}, f32[1024]{0:T(1024)}, u32[]{:S(2)}) copy-start(f32[1024]{0:T(1024)} %copy-done.90) | copy-start | bytes 12292
  510.1 81.4 %collective-permute-start.5 = (bf16[1,1,64,2048]{3,2,1,0:T(8,128)(2,1)S(1)}, bf16[1,1,64,2048]{3,2,1,0:T(8,128)(2,1)S(1)}, u32[]{:S(2)}, u32[]{:S(2)}) collective-permute-start(bf16[1,1,64,2048]{3,2,1,0:T(8,128)(2,1)S(1)} %constant_dynamic-slice_fusion.4), channel_id=1, source_target_pairs={{0,16},{16,0},{8,24},{24,8},{1,17},{17,1},{9,25},{25,9},{2,18},{18... | collective-permute-start | bytes 786440 | tf_op jit(solution)/shard_map/ppermute | solution.py:1166
  604.0 76.2 %copy-start.11 = (f32[128,2048]{1,0:T(8,128)S(1)}, f32[128,2048]{1,0:T(8,128)}, u32[]{:S(2)}) copy-start(f32[128,2048]{1,0:T(8,128)} %copy-done.10) | copy-start | bytes 3145732
  604.1 76.2 %copy-start.22 = (bf16[128,2048]{1,0:T(8,128)(2,1)S(1)}, bf16[128,2048]{1,0:T(8,128)(2,1)}, u32[]{:S(2)}) copy-start(bf16[128,2048]{1,0:T(8,128)(2,1)} %hidden_ref.1) | copy-start | bytes 1572868
  604.1 76.2 %copy-start.58 = (bf16[128,64]{0,1:T(8,128)(2,1)S(1)}, bf16[128,64]{0,1:T(8,128)(2,1)}, u32[]{:S(2)}) copy-start(bf16[128,64]{0,1:T(8,128)(2,1)} %copy-done.57) | copy-start | bytes 49156
  698.7 25.3 %collective-permute-start.6 = (bf16[512,2048]{1,0:T(8,128)(2,1)}, bf16[512,2048]{1,0:T(8,128)(2,1)}, u32[]{:S(2)}, u32[]{:S(2)}) collective-permute-start(bf16[512,2048]{1,0:T(8,128)(2,1)} %add_convert_fusion.2), channel_id=1, source_target_pairs={{0,8},{8,0},{16,24},{24,16},{1,9},{9,1},{17,25},{25,17},{2,10},{10... | collective-permute-start | bytes 6291464 | tf_op jit(solution)/shard_map/ppermute | solution.py:1392
  704.9 25.9 %collective-permute-start.8 = (bf16[512,2048]{1,0:T(8,128)(2,1)}, bf16[512,2048]{1,0:T(8,128)(2,1)}, u32[]{:S(2)}, u32[]{:S(2)}) collective-permute-start(bf16[512,2048]{1,0:T(8,128)(2,1)} %add_convert_fusion.1), channel_id=1, source_target_pairs={{0,8},{8,0},{16,24},{24,16},{1,9},{9,1},{17,25},{25,17},{2,10},{10... | collective-permute-start | bytes 6291464 | tf_op jit(solution)/shard_map/ppermute | solution.py:1392
  (88 other events, 543.4 us)

commit v3 on v2

--- a/solution.py
+++ b/solution.py
@@ -906,93 +906,316 @@
 SIBLING = ((0, 1), (1, 0), (2, 3), (3, 2))
 
 
-def tail_kernel(
-    grads_ref,
-    weights_ref,
-    blocks_ref,
-    early_ref,
+def head_back(grad, raw, gain, cosine, sine):
+    half = raw.shape[1] // 2
+    first, second = grad[:, :half], grad[:, half:]
+    turned = jnp.concatenate(
+        [first * cosine + second * sine, second * cosine - first * sine], axis=1
+    )
+    root = lax.rsqrt(jnp.mean(raw * raw, axis=1, keepdims=True) + EPS)
+    gain_grad = jnp.sum(turned * raw * root, axis=0, keepdims=True)
+    turned = turned * gain
+    along = jnp.mean(turned * raw, axis=1, keepdims=True)
+    return (root * turned - raw * (root * root * root * along), gain_grad)
+
+
+def attention_back_kernel(
+    own_ref,
+    o_any,
+    q_any,
+    k_any,
+    v_any,
+    att_any,
+    probs_any,
+    normed_any,
+    weights_any,
+    q_raw_any,
+    k_raw_any,
+    cosine_any,
+    sine_any,
+    laurel_any,
+    gains_ref,
+    pl_ref,
+    own_down,
+    far_down,
+    own_gate,
+    own_up,
     sum_ref,
     owned_ref,
-    early_all,
+    early_ref,
+    gain_grads,
+    total_down,
+    total_gate,
+    total_up,
+    far_gate,
+    far_up,
+    o_proj,
+    q_low,
+    k_low,
+    v_low,
+    att,
+    probs,
+    normed,
+    weights,
+    q_raw,
+    k_raw,
+    cosine,
+    sine,
+    d_all,
+    block,
+    att_block,
+    q_block,
+    dq_block,
+    d_q,
+    d_k,
+    d_v,
+    d_qkv,
+    turned,
+    part,
     held,
-    part,
-    keep,
+    blocks,
     folded,
     far,
     near_sum,
     key_held,
+    o_grad,
+    o_folded,
+    o_far,
+    sum_own,
+    sum_far,
+    load_sems,
+    final_sems,
     *sems,
 ):
-    ring_sems, fold_sems, far_sems, swap_sems, key_sems, mirror_sems, early_sems = [
-        sems[i : i + 2] for i in range(0, 14, 2)
-    ]
-    load_sem = sems[14]
-    rows = sum_ref.shape[0]
+    pairs = [sems[i : i + 2] for i in range(0, len(sems), 2)]
+    ring_sems, sum_sems, fold_sems, far_sems, swap_sems, key_sems = pairs[:6]
+    mirror_sems, early_sems, o_fold_sems, o_far_sems, cross_sems, total_sems = pairs[6:]
+    rows, width = own_ref.shape
+    total_rows = rows * HEADS
     half = rows // 2
     piece = rows // 4
-    lanes = 4
     index = lax.axis_index("fsdp")
     chip, core, sibling, across = neighbours()
     place = ring_place(index)
     ends = ring_ends(place)
     others = [lax.rem(index + step, HEADS) for step in range(1, HEADS)]
+    quarter = 2 * chip + core
+    quarter_rows = blocks.shape[2]
+    own_rows = span(quarter * quarter_rows, quarter_rows)
+    other_rows = span((2 * (1 - chip) + core) * quarter_rows, quarter_rows)
+    groups = HEADS // KV_HEADS
+    scale = HEAD_DIM ** (-0.5)
+    head_columns = 3 * HEAD_DIM
+    loads = start_loads(
+        (
+            (o_any, o_proj),
+            (q_any, q_low),
+            (k_any, k_low),
+            (v_any, v_low),
+            (att_any, att),
+            (probs_any, probs),
+            (q_raw_any, q_raw),
+            (k_raw_any, k_raw),
+            (cosine_any, cosine),
+            (sine_any, sine),
+            (weights_any, weights),
+            (normed_any, normed),
+            (laurel_any, blocks.at[:, :, :, pl.ds(head_columns, laurel_any.shape[3])]),
+        ),
+        load_sems,
+    )
     greet([{"fsdp": other} for other in others] + [sibling, across])
-    quarter_rows = blocks_ref.shape[2]
-    folds, loads = [], []
+    early_rows = far_up.shape[0] // 4
+    late_rows = far_up.shape[0] - early_rows
+    crossings = [
+        remote(own_gate, far_gate, cross_sems, 0, across),
+        remote(
+            own_up.at[pl.ds(0, early_rows)], far_up.at[pl.ds(0, early_rows)], cross_sems, 1, across
+        ),
+    ]
+    ring = Ring(
+        place,
+        ends,
+        4,
+        ring_sems,
+        lambda lane: own_ref.at[pl.ds(lane_offset(lane, rows), piece)],
+        lambda owner, lane: d_all.at[span(owner * rows + lane_offset(lane, rows), piece)],
+    )
+    sums = RingSum(
+        place,
+        ends,
+        4,
+        sum_sems,
+        held,
+        lambda owner, lane: part[pl.ds(lane_offset(lane, rows), piece), :],
+    )
+    key_tiles = total_rows // TILE
+
+    def compute(step):
+        pair = Pair(place, step, rows)
+        block[...] = pair.read(d_all)
+        d_att = low(mul_t(block[...], o_proj[...]))
+        att_block[...] = d_att
+        q_block[...] = pair.read(q_low)
+        delta = jnp.sum(
+            d_att.astype(jnp.float32) * pair.read(att).astype(jnp.float32), axis=1, keepdims=True
+        )
+        dq_block[...] = jnp.zeros_like(dq_block)
+
+        def keys(tile):
+            chance = pair.read(probs, tile)
+            d_chance = mul_t(att_block[...], v_low[tile, :])
+            d_score = low(chance.astype(jnp.float32) * (d_chance - delta) * scale)
+            dq_block[...] += dot(d_score, k_low[tile, :])
+            d_k[tile, :] += dot(d_score.T, q_block[...])
+            d_v[tile, :] += dot(chance.T, att_block[...])
+
+        tile_loop(key_tiles, TILE, keys)
+        pair.write(d_q, slice(None), dq_block[...])
+
+    finals = (
+        (own_down, far_down, total_down),
+        (own_gate, far_gate, total_gate),
+        (own_up, far_up, total_up),
+    )
+    final_loads, final_sends, final_stores = [], [], []
+    half_units = far_up.shape[0]
+
+    def load_final(number):
+        if number:
+            final_sends[number - 1].wait_send()
+            final_stores[number - 1].wait()
+        for side, (ref, target) in enumerate(zip(finals[number], (sum_own, sum_far))):
+            copy = pltpu.make_async_copy(ref, target, final_sems.at[side])
+            copy.start()
+            final_loads.append(copy)
+
+    def add_final(number):
+        for copy in final_loads[2 * number :]:
+            copy.wait()
+
+        def add(tile):
+            sum_own[tile, :] = add_low(sum_own[tile, :], sum_far[tile, :])
+
+        tile_loop(half_units // 64, 64, add)
+        target = finals[number][2].at[span(core * half_units, half_units)]
+        final_sends.append(remote(sum_own, target, total_sems, number, sibling))
+        store = pltpu.make_async_copy(sum_own, target, final_sems.at[2])
+        store.start()
+        final_stores.append(store)
+
+    d_k[...] = jnp.zeros_like(d_k)
+    d_v[...] = jnp.zeros_like(d_v)
+    gain_grads[...] = jnp.zeros_like(gain_grads)
+    ring.send(0)
+    d_all[span(index * rows, rows), :] = own_ref[...]
+    for copy in loads[:6]:
+        copy.wait()
+    compute(0)
+    for step in range(1, HEADS):
+        if step < RING_STEPS:
+            ring.send(step)
+        else:
+            ring.arrive(step)
+        compute(step)
+        if step == 2:
+            load_final(0)
+        if step == 4:
+            add_final(0)
+    for copy in loads[6:]:
+        copy.wait()
+
+    def raw_tile(tile):
+        for side, (grad, raw) in enumerate(((d_q, q_raw), (d_k, k_raw))):
+            value, gain_grad = head_back(
+                grad[tile, :],
+                raw[tile, :],
+                gains_ref[side : side + 1, :],
+                cosine[tile, :],
+                sine[tile, :],
+            )
+            d_qkv[tile, side * HEAD_DIM : (side + 1) * HEAD_DIM] = low(value)
+            gain_grads[side : side + 1, :] += gain_grad
+        d_qkv[tile, 2 * HEAD_DIM :] = low(d_v[tile, :])
+
+    tile_loop(total_rows // 128, 128, raw_tile)
+
+    def owner_at(step, way):
+        return ring_index(lax.rem(place + (step + 1 if way else HEADS - 1 - step), HEADS))
+
+    def part_of(step):
+        tops = [
+            d_qkv[span(owner_at(step, way) * rows + way * half, half), :] for way in range(2)
+        ]
+        part[...] = mul_t(jnp.concatenate(tops, axis=0), weights[...])
+
+    def head_grads(number, carry):
+        turned[...] = normed[:, span(number * TILE, TILE)].T
+        value = low(dot(turned[...], d_qkv[...]))
+        for step in range(QUARTERS):
+            blocks[number, step, :, :head_columns] = value[
+                step * quarter_rows : (step + 1) * quarter_rows
+            ]
+        return carry
+
+    def o_tile(tile):
+        value = low(dot(turned[...], d_all[:, tile]))
+        for step in range(QUARTERS):
+            o_grad[step, :, tile] = value[step * quarter_rows : (step + 1) * quarter_rows]
+
+    part_of(0)
+    sums.send(0)
+    lax.fori_loop(0, width // TILE, head_grads, 0)
+    folds, o_folds, across_sends, swaps, key_swaps = [], [], [], [], []
     for side in range(2):
         folds.append(
-            remote(blocks_ref.at[:, 2 * side + 1 - core], folded.at[side], fold_sems, side, sibling)
+            remote(blocks.at[:, 2 * side + 1 - core], folded.at[side], fold_sems, side, sibling)
         )
-        load = pltpu.make_async_copy(
-            blocks_ref.at[:, 2 * side + core], keep.at[side], load_sem.at[side]
+    part_of(1)
+    sums.send(1)
+    turned[...] = att[...].T
+    tile_loop(width // (2 * TILE), 2 * TILE, o_tile)
+    for side in range(2):
+        o_folds.append(
+            remote(o_grad.at[2 * side + 1 - core], o_folded.at[side], o_fold_sems, side, sibling)
         )
-        load.start()
-        loads.append(load)
-
-    quarter = 2 * chip + core
-    own_rows = span(quarter * quarter_rows, quarter_rows)
-    other_rows = span((2 * (1 - chip) + core) * quarter_rows, quarter_rows)
-    early_all[own_rows, :] = early_ref[...]
-    early = Mirror(1, early_sems)
-    early.give(0, early_all.at[own_rows])
-
-    def owner_at(step, way):
-        return ring_index(lax.rem(place + (step + 1 if way else HEADS - 1 - step), HEADS))
-
-    def compute(step):
-        tops = [
-            grads_ref[span(owner_at(step, way) * rows + way * half, half), :] for way in range(2)
-        ]
-        part[...] = mul_t(jnp.concatenate(tops, axis=0), weights_ref[...])
-
-    def lane_rows(lane):
-        return pl.ds((lane % 2) * half + (lane // 2) * piece, piece)
-
-    across_sends, swaps, key_swaps = [], [], []
-    mirror = Mirror(1, mirror_sems)
-    rest = blocks_ref.shape[3] - HEAD_DIM
+    mirror, early = Mirror(1, mirror_sems), Mirror(1, early_sems)
+    rest = blocks.shape[3] - HEAD_DIM
     q_columns = HEADS * HEAD_DIM
+    mine, yours = 2 * chip + core, 2 * (1 - chip) + core
 
     def fold_step():
         for side in range(2):
             folds[side].wait_recv()
-            loads[side].wait()
-        for block in range(HEADS):
-            keep[1 - chip, block] = add_low(keep[1 - chip, block], folded[1 - chip, block])
-        across_sends.append(remote(keep.at[1 - chip], far, far_sems, 0, across))
-        for block in range(HEADS):
-            keep[chip, block] = add_low(keep[chip, block], folded[chip, block])
+            o_folds[side].wait_recv()
+        for number in range(HEADS):
+            blocks[number, yours] = add_low(blocks[number, yours], folded[1 - chip, number])
+        across_sends.append(remote(blocks.at[:, yours], far, far_sems, 0, across))
+        o_grad[yours] = add_low(o_grad[yours], o_folded[1 - chip])
+        across_sends.append(remote(o_grad.at[yours], o_far, o_far_sems, 0, across))
+        crossings.append(
+            remote(
+                own_up.at[pl.ds(early_rows, late_rows)],
+                far_up.at[pl.ds(early_rows, late_rows)],
+                cross_sems,
+                2,
+                across,
+            )
+        )
+        for number in range(HEADS):
+            blocks[number, mine] = add_low(blocks[number, mine], folded[chip, number])
+        o_grad[mine] = add_low(o_grad[mine], o_folded[chip])
 
     def swap_step():
         across_sends[0].wait_recv()
-        for block in range(HEADS):
-            near_sum[block] = add_low(keep[chip, block], far[block])
-        mine = span(index * HEAD_DIM, HEAD_DIM)
+        for number in range(HEADS):
+            near_sum[number] = add_low(blocks[number, mine], far[number])
+        here = span(index * HEAD_DIM, HEAD_DIM)
         for step, other in enumerate(others):
             swaps.append(
                 remote(
                     near_sum.at[other, :, pl.ds(0, HEAD_DIM)],
-                    owned_ref.at[own_rows, mine],
+                    owned_ref.at[own_rows, here],
                     swap_sems,
                     step,
                     {"fsdp": other},
@@ -1007,44 +1230,37 @@
                     {"fsdp": other},
                 )
             )
-        owned_ref[own_rows, mine] = near_sum[index, :, :HEAD_DIM]
+        owned_ref[own_rows, here] = near_sum[index, :, :HEAD_DIM]
         key_held[index] = near_sum[index, :, HEAD_DIM:]
-
-    copies = []
-    for step in range(RING_STEPS):
-        compute(step)
-        for lane in range(lanes):
-            number = step * lanes + lane
-            if step:
-                copies[number - lanes].wait_recv()
-                held[number - lanes] = (
-                    held[number - lanes].astype(jnp.float32) + part[lane_rows(lane), :]
-                ).astype(jnp.bfloat16)
-                source = held.at[number - lanes]
-            else:
-                source = held.at[RING_STEPS * lanes + lane]
-                source[...] = part[lane_rows(lane), :].astype(jnp.bfloat16)
-            copies.append(remote(source, held.at[number], ring_sems, number, ends[lane % 2]))
-        if step == 1:
+        across_sends[1].wait_recv()
+        early_ref[own_rows, :width] = add_low(o_grad[mine], o_far[...])
+        early_ref[own_rows, width:] = pl_ref[...]
+        early.give(0, early_ref.at[own_rows])
+
+    for step in range(2, RING_STEPS):
+        part_of(step)
+        sums.send(step)
+        if step == 2:
             fold_step()
         if step == 3:
-            early.relay(0, early_all.at[other_rows])
+            crossings[0].wait_recv()
+            load_final(1)
         if step == 4:
             swap_step()
-    tops = grads_ref[span(index * rows, rows), :]
-    part[...] = mul_t(tops, weights_ref[...])
-    for lane in range(lanes):
-        number = (RING_STEPS - 1) * lanes + lane
-        copies[number].wait_recv()
-        sum_ref[lane_rows(lane), :] = held[number].astype(jnp.float32) + part[lane_rows(lane), :]
+        if step == 5:
+            add_final(1)
+        if step == 6:
+            early.relay(0, early_ref.at[other_rows])
+    part[...] = mul_t(d_qkv[span(index * rows, rows), :], weights[...])
+    for lane in range(4):
+        sum_ref[pl.ds(lane_offset(lane, rows), piece), :] = sums.last(index, lane)
     for copy in swaps + key_swaps:
         copy.wait_recv()
-    groups = HEADS // KV_HEADS
     for head in range(KV_HEADS):
         total = key_held[head * groups].astype(jnp.float32)
         for step in range(1, groups):
             total = total + key_held[head * groups + step].astype(jnp.float32)
-        total = total.astype(jnp.bfloat16)
+        total = low(total)
         for side in range(2):
             base = q_columns + (side * KV_HEADS + head) * HEAD_DIM
             owned_ref[own_rows, pl.ds(base, HEAD_DIM)] = total[
@@ -1054,52 +1270,88 @@
     for step in range(1, HEADS):
         extra = extra + key_held[step, :, 2 * HEAD_DIM :].astype(jnp.float32)
     base = q_columns + 2 * KV_HEADS * HEAD_DIM
-    owned_ref[own_rows, pl.ds(base, rest - 2 * HEAD_DIM)] = extra.astype(jnp.bfloat16)
+    owned_ref[own_rows, pl.ds(base, rest - 2 * HEAD_DIM)] = low(extra)
     mirror.give(0, owned_ref.at[own_rows])
+    crossings[1].wait_recv()
+    crossings[2].wait_recv()
+    load_final(2)
     mirror.relay(0, owned_ref.at[other_rows])
+    add_final(2)
     mirror.finish()
     early.finish()
-    for copy in copies + folds + across_sends + swaps + key_swaps:
+    ring.sent()
+    sums.sent()
+    for copy in folds + o_folds + across_sends + swaps + key_swaps + crossings:
         copy.wait_send()
-
-
-def tail_scatter(grads, weights, blocks, early, number):
-    rows = grads.shape[0] // HEADS
-    width = weights.shape[0]
+    final_sends[2].wait_send()
+    final_stores[2].wait()
+    for copy in final_sends:
+        copy.wait_recv()
+
+
+def attention_back(own, arrays, laurel, gains, pl_sum, chip_grads, far_down, number):
+    rows, width = own.shape
+    total = rows * HEADS
     shard = width // HEADS
+    quarter = shard // QUARTERS
     steps = 4 * RING_STEPS
-    quarter = shard // QUARTERS
-    across = blocks.shape[1]
-    rest = across - HEAD_DIM
-    blocks = blocks.reshape(HEADS, QUARTERS, quarter, across)
-    near = pl.BlockSpec(memory_space=pltpu.VMEM)
-    bf16 = jnp.bfloat16
-    counts = [steps, 2, 1, HEADS - 1, HEADS - 1, 3, 3]
-    owned = (HEADS + 2 * KV_HEADS) * HEAD_DIM + rest - 2 * HEAD_DIM
+    columns = 3 * HEAD_DIM + laurel.shape[1]
+    laurel = laurel.reshape(HEADS, QUARTERS, quarter, -1)
+    half = chip_grads[0].shape
+    near, anywhere = pl.BlockSpec(memory_space=pltpu.VMEM), pl.BlockSpec(memory_space=pl.ANY)
+    bf16, f32 = jnp.bfloat16, jnp.float32
+    owned = (HEADS + 2 * KV_HEADS) * HEAD_DIM + laurel.shape[3]
+    counts = [steps, steps, 2, 1, HEADS - 1, HEADS - 1, 3, 3, 2, 1, 3, 3]
+    down, gate, up = chip_grads
+    whole = jax.ShapeDtypeStruct((2 * half[0], half[1]), bf16)
+    part = jax.ShapeDtypeStruct(half, bf16)
     return pl.pallas_call(
-        tail_kernel,
+        attention_back_kernel,
         out_shape=[
-            jax.ShapeDtypeStruct((rows, width), jnp.float32),
+            jax.ShapeDtypeStruct((rows, width), f32),
             jax.ShapeDtypeStruct((shard, owned), bf16),
-            jax.ShapeDtypeStruct((shard, early.shape[1]), bf16),
+            jax.ShapeDtypeStruct((shard, width + pl_sum.shape[1]), bf16),
+            jax.ShapeDtypeStruct(gains.shape, f32),
+            whole,
+            whole,
+            whole,
+            part,
+            part,
         ],
-        in_specs=[near, near, pl.BlockSpec(memory_space=pl.ANY), near],
-        out_specs=[near] * 3,
-        scratch_shapes=[
+        in_specs=[near] + [anywhere] * (len(arrays) + 1) + [near] * 2 + [anywhere] * 4,
+        out_specs=[near] * 4 + [anywhere] * 5,
+        scratch_shapes=[pltpu.VMEM(item.shape, item.dtype) for item in arrays]
+        + [
+            pltpu.VMEM((total, width), bf16),
+            pltpu.VMEM((rows, width), bf16),
+            pltpu.VMEM((rows, HEAD_DIM), bf16),
+            pltpu.VMEM((rows, HEAD_DIM), bf16),
+            pltpu.VMEM((rows, HEAD_DIM), f32),
+            pltpu.VMEM((total, HEAD_DIM), f32),
+            pltpu.VMEM((total, HEAD_DIM), f32),
+            pltpu.VMEM((total, HEAD_DIM), f32),
+            pltpu.VMEM((total, 3 * HEAD_DIM), bf16),
+            pltpu.VMEM((HEAD_DIM, total), bf16),
+            pltpu.VMEM((rows, width), f32),
             pltpu.VMEM((steps + 4, rows // 4, width), bf16),
-            pltpu.VMEM((rows, width), jnp.float32),
-            pltpu.VMEM((2, HEADS, quarter, across), bf16),
-            pltpu.VMEM((2, HEADS, quarter, across), bf16),
-            pltpu.VMEM((HEADS, quarter, across), bf16),
-            pltpu.VMEM((HEADS, quarter, across), bf16),
-            pltpu.VMEM((HEADS, quarter, rest), bf16),
+            pltpu.VMEM((HEADS, QUARTERS, quarter, columns), bf16),
+            pltpu.VMEM((2, HEADS, quarter, columns), bf16),
+            pltpu.VMEM((HEADS, quarter, columns), bf16),
+            pltpu.VMEM((HEADS, quarter, columns), bf16),
+            pltpu.VMEM((HEADS, quarter, columns - HEAD_DIM), bf16),
+            pltpu.VMEM((QUARTERS, quarter, width), bf16),
+            pltpu.VMEM((2, quarter, width), bf16),
+            pltpu.VMEM((quarter, width), bf16),
+            pltpu.VMEM(half, bf16),
+            pltpu.VMEM(half, bf16),
+            pltpu.SemaphoreType.DMA((len(arrays) + 1,)),
+            pltpu.SemaphoreType.DMA((3,)),
         ]
-        + [pltpu.SemaphoreType.DMA((count,)) for count in counts for unused_side in range(2)]
-        + [pltpu.SemaphoreType.DMA((2,))],
+        + [pltpu.SemaphoreType.DMA((count,)) for count in counts for unused_side in range(2)],
         compiler_params=pltpu.CompilerParams(
-            collective_id=number, has_side_effects=True, vmem_limit_bytes=VMEM_BYTES
+            collective_id=number, has_side_effects=True, vmem_limit_bytes=56 << 20
         ),
-    )(grads, weights, blocks, early)
+    )(own, *arrays, laurel, gains, pl_sum, down, far_down, gate, up)
 
 
 def gains_kernel(parts_ref, sum_ref, landed, totals, send_sem, recv_sem, rep_send, rep_recv):
@@ -1272,8 +1524,19 @@
     k_raw = dot(normed_all, k_head)
     v_low = low(dot(normed_all, v_head))
 
+    half = HEAD_DIM // 2
+    freqs = jnp.exp(
+        jnp.arange(half, dtype=jnp.float32) * (-2.0 * math.log(ROPE_BASE) / HEAD_DIM)
+    )
+    angle = depth[:, None] * freqs[None, :]
+    cosine, sine = jnp.cos(angle), jnp.sin(angle)
+
     def head_path(raw, gain):
-        return rotate(norm_rows(raw, gain)[:, None, :], depth)[:, 0, :]
+        value = norm_rows(raw, gain)
+        first, second = value[:, :half], value[:, half:]
+        return jnp.concatenate(
+            [first * cosine - second * sine, second * cosine + first * sine], axis=1
+        )
 
     q_low = low(head_path(q_raw, gain_qnorm))
     k_low = low(head_path(k_raw, gain_knorm))
@@ -1334,47 +1597,40 @@
         9,
     )
     chip_grads, far_down, pl_sum = rest[:3], rest[3], rest[4]
-    late = chip_grads[2].shape[0] * 3 // 4
-    far_gate, far_up, far_last = [
-        lax.ppermute(item, "rep", ACROSS)
-        for item in (chip_grads[1], chip_grads[2][:late], chip_grads[2][late:])
-    ]
-
     d_first_part, grad_fnorm = norm_back(first_sum, gain_fnorm, d_ffwin)
     d_scaled = (d_second + d_first_part) * HALF_ROOT
     d_branch, grad_apost = norm_back(branch, gain_apost, d_scaled)
     d_lowrank, grad_lnorm = norm_back(low_rank, gain_lnorm, d_scaled)
     d_lowrank_low = low(d_lowrank)
-    (d_branch_all,) = ring_gather(low(d_branch), 11)
     grad_right = outer(d_lowrank_low, left_low)
     d_left_low = low(dot(d_lowrank_low, full_right))
     grad_left = outer(normed_low, d_left_low)
 
-    d_att_low = low(mul_t(d_branch_all, o_proj))
-    grad_o = outer(attended_low, d_branch_all)
-    o_quarter = quarter_fold(low(grad_o).reshape(QUARTERS, -1, width))
-    delta = jnp.sum(d_att_low.astype(jnp.float32) * attended, axis=-1, keepdims=True)
-    d_probs = mul_t(d_att_low, v_low)
-    d_scores = low(probs * (d_probs - delta) * scale)
-    d_query = dot(d_scores, k_low)
-    d_key = outer(d_scores, q_low)
-    d_value = outer(probs_low, d_att_low)
-    unused_q, q_pull = jax.vjp(head_path, q_raw, gain_qnorm)
-    d_qraw, grad_qnorm = q_pull(d_query)
-    unused_k, k_pull = jax.vjp(head_path, k_raw, gain_knorm)
-    d_kraw, grad_knorm = k_pull(d_key)
-    d_q_low = low(d_qraw)
-    d_k_low = low(d_kraw)
-    d_v_low = low(d_value)
-    d_qkv = jnp.concatenate([d_q_low, d_k_low, d_v_low], axis=1)
-    qkv_head = jnp.concatenate([q_head, k_head, v_head], axis=1)
-    d_qkv, far_gate, far_up = lax.optimization_barrier((d_qkv, far_gate, far_up))
-    blocks = jnp.concatenate(
-        [low(outer(normed_all, d_qkv)), low(grad_left), low(grad_right)], axis=1
-    )
-    d_normed_sum, owned, early = tail_scatter(
-        d_qkv, qkv_head, blocks, jnp.concatenate([o_quarter, pl_sum], axis=1), 12
-    )
+    d_normed_sum, owned, early, head_gains, *totals = attention_back(
+        low(d_branch),
+        (
+            o_proj,
+            q_low,
+            k_low,
+            v_low,
+            attended_low,
+            probs_low,
+            normed_all,
+            jnp.concatenate([q_head, k_head, v_head], axis=1),
+            q_raw,
+            k_raw,
+            cosine,
+            sine,
+        ),
+        low(jnp.concatenate([grad_left, grad_right], axis=1)),
+        jnp.stack([gain_qnorm, gain_knorm]),
+        pl_sum,
+        chip_grads,
+        far_down,
+        12,
+    )
+    grad_qnorm, grad_knorm = head_gains
+    sum_down, sum_gate, sum_up = [item.astype(jnp.float32) for item in totals[:3]]
     owned = owned.astype(jnp.float32)
     early = early.astype(jnp.float32)
     key_at = width
@@ -1384,15 +1640,6 @@
     d_source_part, grad_anorm = norm_back(source, gain_anorm, d_normed)
     d_source = d_scaled + d_source_part
 
-    far_grads = [far_down, far_gate, jnp.concatenate([far_up, far_last], axis=0)]
-    sums = []
-    core = lax.rem(lax.axis_index("rep"), 2)
-    for item, far in zip(chip_grads, far_grads):
-        both = add_low(item, far)
-        other = lax.ppermute(both, "rep", SIBLING)
-        halves = [jnp.where(core == 0, both, other), jnp.where(core == 0, other, both)]
-        sums.append(jnp.concatenate(halves, axis=0).astype(jnp.float32))
-    sum_down, sum_gate, sum_up = sums
     small_grads = [grad_anorm, grad_apost, grad_lnorm, grad_fnorm, grad_fpost, grad_plpost]
     parts = [item.reshape(HEADS, shard) for item in small_grads]
     parts += [item.reshape(HEADS, piece) for item in (grad_qnorm, grad_knorm)]

time: 748 us -> 639 us (0.85)
  waiting for transfers between devices: 90.9 us -> 11.2 us
  Pallas kernels: 456 us -> 485 us
  other arithmetic: 82.6 us -> 62.3 us
  matrix products: 47.4 us -> 30.4 us
  local copies, waits for them, and re-layouts: 53.2 us -> 37.8 us
    ppermute x2 -> x1, waiting for transfers between devices: 90.9 us -> 11.2 us  [chip_fold(): return add_low(keep, lax.ppermute(give, 'rep', ACROSS))]
    pallas_call x2 -> x1, Pallas kernels: 118 us -> 147 us  [attention_back(): pl.pallas_call(attention_back_kernel, out_shape=[jax.ShapeDtypeStruct((ro...]
    convert_element_type x5 -> x1, other arithmetic: 15.7 us -> 1.54 us  [add_low(): (left.astype(jnp.float32) + right.astype(jnp.float32)).astype(jnp.bfloat16)]
    select_n x3 -> x0, other arithmetic: 9.5 us -> none  [head_plan(): jnp.where(core == 0, both, other)]
    dot_general x8 -> x4, matrix products: 13.1 us -> 4.81 us  [outer(): lax.dot_general(left, right, (((0,), (0,)), ((), ())), preferred_element_...]
    dot_general x9 -> x8, matrix products: 18.5 us -> 12.5 us  [dot(): return jnp.dot(left, right, preferred_element_type=jnp.float32)]
    unnamed x234 -> x130, local copies, waits for them, and re-layouts: 15.4 us -> 10.5 us
    dot_general x8 -> x6, matrix products: 15.8 us -> 13.1 us  [mul_t(): lax.dot_general(left, right, (((1,), (1,)), ((), ())), preferred_element_...]
  transfers between devices with their start and end apart: 10 -> 2, of which waited for: 2 -> 1; matrix products, arithmetic and copies ran while one was open for 10% -> 3% of each run, Pallas kernels for 12% -> 0%
where the time goes in v3:
time: 639 us; the launch traced here: 629 us
  Pallas kernels  485 us (76%)
  other arithmetic  62.3 us (10%)
  local copies, waits for them, and re-layouts  37.8 us (6%)
  matrix products  30.4 us (5%)
  waiting for transfers between devices  11.2 us (2%)
    pallas_call x1, Pallas kernels, attention_back(): pl.pallas_call(attention_back_kernel, out_shape=[jax.ShapeDtypeStruct((ro...  147 us
    pallas_call x1, Pallas kernels, ffn_back(): pl.pallas_call(ffn_back_kernel, out_shape=[jax.ShapeDtypeStruct((rows, wi...  114 us
    pallas_call x1, Pallas kernels, ffn_forward(): pl.pallas_call(ffn_kernel, out_shape=[jax.ShapeDtypeStruct((rows, width),...  88.3 us
    pallas_call x1, Pallas kernels, start_gather(): pl.pallas_call(start_kernel, out_shape=[grown(hidden), grown(gains), grow...  76.6 us
    pallas_call x1, Pallas kernels, ring_scatter(): pl.pallas_call(scatter_kernel, out_shape=out_shape, in_specs=[near] * len...  43.6 us
    convert_element_type x3, other arithmetic, head_plan(): item.astype(jnp.float32)  15.7 us
    dot_general x6, matrix products, mul_t(): lax.dot_general(left, right, (((1,), (1,)), ((), ())), preferred_element_...  13.1 us
  transfers between devices with their start and end apart: 2, of which 1 were waited for; matrix products, arithmetic and copies ran while one was open for 3% of the time, Pallas kernels for 0%

profile of v3, /device:TPU:0, one launch (start us, length us, event | category | flops | bytes accessed | tf_op | source)
XLA Modules:
  0.0 629.4 jit_solution(18305875272366222914)
XLA Ops:
  2.0 5.4 concatenate.40
  13.3 76.6 %shard_map.399 = (bf16[1024,2048]{1,0:T(8,128)(2,1)}, bf16[256,128]{1,0:T(8,128)(2,1)}, bf16[2048,256]{1,0:T(8,128)(2,1)}, bf16[2048,1024]{1,0:T(8,128)(2,1)}, b...) custom-call(bf16[128,2048]{1,0:T(8,128)(2,1)} %hidden_ref.1, bf16[32,128]{1,0:T(8,128)(2,1)} %pad_bitcast_fusion.1.gains_ref, ...), custom_call_target="tpu_custom_call" | custom-call | tf_op jit(solution)/shard_map/pallas_call | solution.py:364
  92.0 2.8 fusion.64
  95.9 3.3 fusion.2.normed_any
  101.6 2.1 constant_dynamic-slice_fusion
  105.2 2.3 multiply_reduce_fusion.13
  109.1 5.0 fusion.88
  114.5 3.5 fusion.39
  117.9 3.7 fusion.89
  121.6 4.9 online-softmax
  130.0 43.6 %shard_map.400 = f32[128,2048]{1,0:T(8,128)S(1)} custom-call(bf16[1024,2048]{1,0:T(8,128)(2,1)S(1)} %convolution_convert_fusion.part_ref), custom_call_target="tpu_custom_call" | custom-call | tf_op jit(solution)/shard_map/pallas_call | solution.py:508
  176.0 88.3 %shard_map.401 = (f32[128,2048]{1,0:T(8,128)S(1)}, bf16[1024,2048]{1,0:T(8,128)(2,1)}, bf16[1024,1024]{1,0:T(8,128)(2,1)S(1)}, bf16[1024,1024]{1,0:T(8,128)(2,1)S(1)}, bf16[1024,1024]{1,0:T(8,128)(2,1)}) custom-call(bf16[128,2048]{1,0:T(8,128)(2,1)S(1)} %multiply_convert_fusion.own_ref, bf16[1024,2048]{1,0:T(8,128)(2,1)} %gate_any.3, ...), custom_call_target="tpu_custom_call" | custom-call | tf_op jit(solution)/shard_map/pallas_call | solution.py:660
  271.3 2.7 convolution_convert_fusion.2
  274.0 2.3 concatenate.46
  276.3 2.8 fusion.26
  281.5 2.9 multiply_reduce_fusion
  284.4 3.1 fusion.4
  288.2 2.4 pad_maximum_fusion.2
  290.5 3.1 pad_maximum_fusion.weights_any
  293.7 2.0 divide_convert_fusion.probs_any
  300.4 2.3 fusion.17.own_ref
  302.6 11.2 %collective-permute-done.1 = bf16[8,1,1,64,512]{4,3,0,2,1:T(8,128)(2,1)} collective-permute-done((bf16[8,1,1,64,512]{4,3,0,2,1:T(8,128)(2,1)}, bf16[8,1,1,64,512]{4,3,0,2,1:T(8,128)(2,1)}, u32[]{:S(2)}, u32[]{:S(2)}) %collective-permute-start.1) | collective-permute-done | bytes 524320 | tf_op jit(solution)/shard_map/ppermute | solution.py:1418
  313.8 2.2 fusion.46.blocks_ref
  316.1 114.0 %shard_map.402 = (f32[128,2048]{1,0:T(8,128)}, bf16[512,2048]{1,0:T(8,128)(2,1)}, bf16[512,2048]{1,0:T(8,128)(2,1)}, bf16[512,2048]{1,0:T(8,128)(2,1)}, bf16[512...) custom-call(bf16[128,2048]{1,0:T(8,128)(2,1)} %fusion.17.own_ref, bf16[1024,2048]{1,0:T(8,128)(2,1)} %get-tuple-element.53.all_any, ...), custom_call_target="tpu_custom_call" | custom-call | tf_op jit(solution)/shard_map/pallas_call | solution.py:875
  431.6 2.3 multiply_reduce_fusion.2
  439.1 146.8 %shard_map.403 = (f32[128,2048]{1,0:T(8,128)}, bf16[256,3200]{1,0:T(8,128)(2,1)}, bf16[256,2560]{1,0:T(8,128)(2,1)}, f32[2,256]{1,0:T(2,128)}, bf16[1024,2048]{1...) custom-call(bf16[128,2048]{1,0:T(8,128)(2,1)} %get-tuple-element.174, ...), custom_call_target="tpu_custom_call" | custom-call | tf_op jit(solution)/shard_map/pallas_call | solution.py:1308
  587.8 2.8 slice.165
  593.3 2.0 fusion.13
  596.3 10.8 %shard_map.404 = f32[16,128]{1,0:T(8,128)} custom-call(f32[8,16,128]{2,1,0:T(8,128)} %bitcast.79), custom_call_target="tpu_custom_call" | custom-call | tf_op jit(solution)/shard_map/pallas_call | solution.py:1390
  612.1 6.8 %convert_element_type.171 = f32[1024,2048]{1,0:T(8,128)} convert(bf16[1024,2048]{1,0:T(8,128)(2,1)} %get-tuple-element.67) | non-fusion elementwise | flops 2097152 | bytes 12582912 | tf_op jit(solution)/shard_map/convert_element_type | solution.py:1633
  618.9 4.4 convert_element_type.172
  623.3 4.4 convert_element_type.173
  (222 shorter events, 54.5 us)
Async XLA Ops:
  0.7 90.2 %copy-start.57 = (s32[1,13]{1,0:T(1,128)S(1)}, s32[1,13]{1,0:T(1,128)}, u32[]{:S(2)}) copy-start(s32[1,13]{1,0:T(1,128)} %param.28) | copy-start | bytes 160
  0.7 90.8 %copy-start.37 = (s32[1,13]{1,0:T(1,128)S(1)}, s32[1,13]{1,0:T(1,128)}, u32[]{:S(2)}) copy-start(s32[1,13]{1,0:T(1,128)} %param.27) | copy-start | bytes 160
  2.0 171.7 %copy-start.44 = (f32[128]{0:T(128)}, f32[128]{0:T(128)S(1)}, u32[]{:S(2)}) copy-start(f32[128]{0:T(128)S(1)} %fusion.23) | copy-start | bytes 1540
  90.8 3.9 copy-start.7
  101.6 12.5 %copy-start.11 = (f32[1024,256]{1,0:T(8,128)}, f32[1024,256]{1,0:T(8,128)S(1)}, u32[]{:S(2)}) copy-start(f32[1024,256]{1,0:T(8,128)S(1)} %copy.75.q_raw_any) | copy-start | bytes 3145732
  103.7 5.4 copy-start.23
  109.0 5.2 copy-start.12
  121.6 7.0 %copy-start.25 = (bf16[256,2048]{1,0:T(8,128)(2,1)S(1)}, bf16[256,2048]{1,0:T(8,128)(2,1)}, u32[]{:S(2)}) copy-start(bf16[256,2048]{1,0:T(8,128)(2,1)} %o_any.1) | copy-start | bytes 3145732
  129.9 43.8 %copy-start.9 = (bf16[128,2048]{1,0:T(8,128)(2,1)S(1)}, bf16[128,2048]{1,0:T(8,128)(2,1)}, u32[]{:S(2)}) copy-start(bf16[128,2048]{1,0:T(8,128)(2,1)} %hidden_ref.1) | copy-start | bytes 1572868
  129.9 43.8 %copy-start.14 = (bf16[2048,384]{1,0:T(8,128)(2,1)S(1)}, bf16[2048,384]{1,0:T(8,128)(2,1)}, u32[]{:S(2)}) copy-start(bf16[2048,384]{1,0:T(8,128)(2,1)} %get-tuple-element.50) | copy-start | bytes 4718596
  173.7 90.6 %copy-start.33 = (f32[128]{0:T(128)}, f32[128]{0:T(128)S(1)}, u32[]{:S(2)}) copy-start(f32[128]{0:T(128)S(1)} %get-tuple-element.218) | copy-start | bytes 1540
  173.7 90.6 %copy-start.35 = (f32[128]{0:T(128)}, f32[128]{0:T(128)S(1)}, u32[]{:S(2)}) copy-start(f32[128]{0:T(128)S(1)} %get-tuple-element.217) | copy-start | bytes 1540
  174.7 89.7 %copy-start.40 = (f32[128]{0:T(128)}, f32[128]{0:T(128)S(1)}, u32[]{:S(2)}) copy-start(f32[128]{0:T(128)S(1)} %fusion.74) | copy-start | bytes 1540
  175.3 89.0 %copy-start.54 = (f32[128]{0:T(128)}, f32[128]{0:T(128)S(1)}, u32[]{:S(2)}) copy-start(f32[128]{0:T(128)S(1)} %get-tuple-element.155) | copy-start | bytes 1540
  175.9 88.5 %copy-start.49 = (f32[128]{0:T(128)}, f32[128]{0:T(128)S(1)}, u32[]{:S(2)}) copy-start(f32[128]{0:T(128)S(1)} %get-tuple-element.200) | copy-start | bytes 1540
  280.2 15.6 %collective-permute-start = (bf16[8,2,1,64,512]{4,3,0,2,1:T(8,128)(2,1)}, bf16[8,2,1,64,512]{4,3,0,2,1:T(8,128)(2,1)}, u32[]{:S(2)}, u32[]{:S(2)}) collective-permute-start(bf16[8,2,1,64,512]{4,3,0,2,1:T(8,128)(2,1)} %copy.90), channel_id=1, source_target_pairs={{0,8},{8,0},{16,24},{24,16},{1,9},{9,1},{17,25},{25,17},{2,10},{10... | collective-permute-start | bytes 3145736 | tf_op jit(solution)/shard_map/ppermute | solution.py:1410
  288.2 5.5 copy-start.2
  288.2 5.5 copy-start.32
  293.7 6.1 copy-start.42
  293.7 6.1 copy-start.43
  293.7 6.7 %copy-start.39 = (f32[128]{0:T(128)S(1)}, f32[128]{0:T(128)}, u32[]{:S(2)}) copy-start(f32[128]{0:T(128)} %copy-done.38) | copy-start | bytes 1540
  299.2 14.7 %collective-permute-start.1 = (bf16[8,1,1,64,512]{4,3,0,2,1:T(8,128)(2,1)}, bf16[8,1,1,64,512]{4,3,0,2,1:T(8,128)(2,1)}, u32[]{:S(2)}, u32[]{:S(2)}) collective-permute-start(bf16[8,1,1,64,512]{4,3,0,2,1:T(8,128)(2,1)} %constant_dynamic-slice_fusion.2), channel_id=1, source_target_pairs={{0,16},{16,0},{8,24},{24,8},{1,17},{17,1},{9,25},{25,9},{2,18},{18... | collective-permute-start | bytes 1572872 | tf_op jit(solution)/shard_map/ppermute | solution.py:1418
  316.0 114.0 %copy-start.50 = (f32[128]{0:T(128)S(1)}, f32[128]{0:T(128)}, u32[]{:S(2)}) copy-start(f32[128]{0:T(128)} %copy-done.49) | copy-start | bytes 1540
  316.0 115.6 %copy-start.55 = (f32[128]{0:T(128)S(1)}, f32[128]{0:T(128)}, u32[]{:S(2)}) copy-start(f32[128]{0:T(128)} %copy-done.54) | copy-start | bytes 1540
  316.0 115.6 %copy-start.6 = (f32[128,2048]{1,0:T(8,128)S(1)}, f32[128,2048]{1,0:T(8,128)}, u32[]{:S(2)}) copy-start(f32[128,2048]{1,0:T(8,128)} %copy-done.5) | copy-start | bytes 3145732
  316.0 115.6 %copy-start.13 = (f32[128,2048]{1,0:T(8,128)S(1)}, f32[128,2048]{1,0:T(8,128)}, u32[]{:S(2)}) copy-start(f32[128,2048]{1,0:T(8,128)} %get-tuple-element.209) | copy-start | bytes 3145732
  316.0 115.6 %copy-start.36 = (f32[128]{0:T(128)S(1)}, f32[128]{0:T(128)}, u32[]{:S(2)}) copy-start(f32[128]{0:T(128)} %copy-done.35) | copy-start | bytes 1540
  316.0 115.6 %copy-start.41 = (f32[128]{0:T(128)S(1)}, f32[128]{0:T(128)}, u32[]{:S(2)}) copy-start(f32[128]{0:T(128)} %copy-done.40) | copy-start | bytes 1540
  316.0 115.6 %copy-start.53 = (f32[128]{0:T(128)S(1)}, f32[128]{0:T(128)}, u32[]{:S(2)}) copy-start(f32[128]{0:T(128)} %get-tuple-element.199) | copy-start | bytes 1540
  585.9 4.6 copy-start.15
  612.1 6.8 %copy-start.19 = (bf16[1024,2048]{1,0:T(8,128)(2,1)S(1)}, bf16[1024,2048]{1,0:T(8,128)(2,1)}, u32[]{:S(2)}) copy-start(bf16[1024,2048]{1,0:T(8,128)(2,1)} %get-tuple-element.68) | copy-start | bytes 12582916
  618.9 4.5 copy-start.18
  (28 other events, 77.0 us)

commit v4 on v3

--- a/solution.py
+++ b/solution.py
@@ -379,43 +379,6 @@
     )(*arrays)
 
 
-def gather_kernel(own_ref, all_ref, local_sem, send_sem, recv_sem):
-    rows = own_ref.shape[0]
-    part = rows // 4
-    index = lax.axis_index("fsdp")
-    place = ring_place(index)
-    ends = ring_ends(place)
-    greet(ends)
-    local = pltpu.make_async_copy(own_ref, all_ref.at[span(index * rows, rows)], local_sem)
-    local.start()
-    ring = Ring(
-        place,
-        ends,
-        4,
-        (send_sem, recv_sem),
-        lambda lane: own_ref.at[pl.ds(lane * part, part)],
-        lambda owner, lane: all_ref.at[span(owner * rows + lane * part, part)],
-    )
-    for step in range(RING_STEPS):
-        ring.send(step)
-    ring.arrive(RING_STEPS)
-    ring.sent()
-    local.wait()
-
-
-def ring_gather(own, number):
-    spec = pl.BlockSpec(memory_space=pl.ANY)
-    return pl.pallas_call(
-        gather_kernel,
-        out_shape=[jax.ShapeDtypeStruct((own.shape[0] * HEADS, own.shape[1]), own.dtype)],
-        in_specs=[spec],
-        out_specs=[spec],
-        scratch_shapes=[pltpu.SemaphoreType.DMA]
-        + [pltpu.SemaphoreType.DMA((4 * RING_STEPS,))] * 2,
-        compiler_params=pltpu.CompilerParams(collective_id=number, has_side_effects=True),
-    )(own)
-
-
 def add_low(left, right):
     return (left.astype(jnp.float32) + right.astype(jnp.float32)).astype(jnp.bfloat16)
 
@@ -453,70 +416,6 @@
             copy.wait_send()
 
 
-def scatter_kernel(part_ref, *refs):
-    if len(refs) > 4:
-        blocks_ref, sum_ref, block_sum, held, send_sem, recv_sem, block_held, block_send, block_recv = refs
-    else:
-        blocks_ref = None
-        sum_ref, held, send_sem, recv_sem = refs
-    rows = sum_ref.shape[0]
-    part = rows // 4
-    index = lax.axis_index("fsdp")
-    place = ring_place(index)
-    ends = ring_ends(place)
-    greet(ends)
-
-    def own(owner, lane):
-        return part_ref[span(owner * rows + lane * part, part), :].astype(jnp.float32)
-
-    rings = [RingSum(place, ends, 4, (send_sem, recv_sem), held, own)]
-    if blocks_ref is not None:
-        low_rows = block_sum.shape[0] // 2
-
-        def block_own(owner, lane):
-            return blocks_ref[owner, pl.ds(lane * low_rows, low_rows), :].astype(jnp.float32)
-
-        rings.append(RingSum(place, ends, 2, (block_send, block_recv), block_held, block_own))
-    for step in range(RING_STEPS):
-        for ring in rings:
-            ring.send(step)
-    for lane in range(4):
-        sum_ref[pl.ds(lane * part, part), :] = rings[0].last(index, lane)
-    if blocks_ref is not None:
-        for lane in range(2):
-            block_sum[pl.ds(lane * low_rows, low_rows), :] = (
-                rings[1].last(index, lane).astype(jnp.bfloat16)
-            )
-    for ring in rings:
-        ring.sent()
-
-
-def ring_scatter(parts, number, blocks=None):
-    rows = parts.shape[0] // HEADS
-    near = pl.BlockSpec(memory_space=pltpu.VMEM)
-    out_shape = [jax.ShapeDtypeStruct((rows, parts.shape[1]), jnp.float32)]
-    steps = 4 * RING_STEPS
-    scratch = [pltpu.VMEM((steps + 4, rows // 4, parts.shape[1]), jnp.bfloat16)]
-    scratch += [pltpu.SemaphoreType.DMA((steps,))] * 2
-    arrays = [parts]
-    if blocks is not None:
-        arrays.append(blocks)
-        out_shape.append(jax.ShapeDtypeStruct(blocks.shape[1:], jnp.bfloat16))
-        steps = 2 * RING_STEPS
-        shape = (steps + 2, blocks.shape[1] // 2, blocks.shape[2])
-        scratch += [pltpu.VMEM(shape, jnp.bfloat16)] + [pltpu.SemaphoreType.DMA((steps,))] * 2
-    return pl.pallas_call(
-        scatter_kernel,
-        out_shape=out_shape,
-        in_specs=[near] * len(arrays),
-        out_specs=[near] * len(out_shape),
-        scratch_shapes=scratch,
-        compiler_params=pltpu.CompilerParams(
-            collective_id=number, has_side_effects=True, vmem_limit_bytes=VMEM_BYTES
-        ),
-    )(*arrays)
-
-
 def lane_offset(lane, rows):
     return (lane % 2) * (rows // 2) + (lane // 2) * (rows // 4)
 
@@ -557,6 +456,209 @@
         copy.start()
         copies.append(copy)
     return copies
+
+
+def root_of(value):
+    return lax.rsqrt(jnp.mean(value * value, axis=1, keepdims=True) + EPS)
+
+
+def norm_pull(value, gain, grad):
+    root = root_of(value)
+    gain_grad = jnp.sum(grad * value * root, axis=0, keepdims=True)
+    grad = grad * gain
+    along = jnp.mean(grad * value, axis=1, keepdims=True)
+    return (root * grad - value * (root * root * root * along), gain_grad)
+
+
+def gelu_parts(value):
+    square = value * value
+    bent = jnp.tanh(GELU_ROOT * value * (1.0 + GELU_CUBE * square))
+    share = 0.5 * (1.0 + bent)
+    slope = share + (0.5 * GELU_ROOT) * value * (1.0 - bent * bent) * (
+        1.0 + (3.0 * GELU_CUBE) * square
+    )
+    return (value * share, slope)
+
+
+def attention_kernel(
+    hidden_any,
+    q_any,
+    kv_any,
+    o_any,
+    norm_ref,
+    gains_ref,
+    cosine_ref,
+    sine_ref,
+    reach_ref,
+    member_ref,
+    sum_ref,
+    normed_any,
+    weights_any,
+    q_raw_any,
+    k_raw_any,
+    q_low_any,
+    k_low_any,
+    v_low_any,
+    att_any,
+    probs_any,
+    hidden,
+    o_proj,
+    normed,
+    weights,
+    q_raw,
+    k_raw,
+    q_low,
+    k_low,
+    v_low,
+    att,
+    probs,
+    part,
+    held,
+    load_sems,
+    store_sems,
+    send_sem,
+    recv_sem,
+):
+    rows, width = sum_ref.shape
+    total_rows = rows * HEADS
+    half = rows // 2
+    index = lax.axis_index("fsdp")
+    place = ring_place(index)
+    ends = ring_ends(place)
+    key_at = (index // (HEADS // KV_HEADS)) * HEAD_DIM
+    loads = start_loads(
+        (
+            (q_any, weights.at[:, pl.ds(0, HEAD_DIM)]),
+            (kv_any.at[:, span(key_at, HEAD_DIM)], weights.at[:, pl.ds(HEAD_DIM, HEAD_DIM)]),
+            (
+                kv_any.at[:, span(key_at + KV_HEADS * HEAD_DIM, HEAD_DIM)],
+                weights.at[:, pl.ds(2 * HEAD_DIM, HEAD_DIM)],
+            ),
+            (hidden_any, hidden),
+            (o_any, o_proj),
+        ),
+        load_sems,
+    )
+    greet(ends)
+    for copy in loads:
+        copy.wait()
+
+    def project(tile):
+        source = hidden[tile, :].astype(jnp.float32)
+        value = low(source * root_of(source) * norm_ref[...])
+        normed[tile, :] = value
+        raw = dot(value, weights[...])
+        cosine, sine = cosine_ref[tile, :], sine_ref[tile, :]
+        for side, (raw_ref, low_ref) in enumerate(((q_raw, q_low), (k_raw, k_low))):
+            item = raw[:, side * HEAD_DIM : (side + 1) * HEAD_DIM]
+            raw_ref[tile, :] = item
+            item = item * root_of(item) * gains_ref[side : side + 1, :]
+            first, second = item[:, : HEAD_DIM // 2], item[:, HEAD_DIM // 2 :]
+            low_ref[tile, :] = low(
+                jnp.concatenate(
+                    [first * cosine - second * sine, second * cosine + first * sine], axis=1
+                )
+            )
+        v_low[tile, :] = low(raw[:, 2 * HEAD_DIM :])
+
+    tile_loop(total_rows // 128, 128, project)
+    stores = start_loads(
+        (
+            (normed, normed_any),
+            (weights, weights_any),
+            (q_raw, q_raw_any),
+            (k_raw, k_raw_any),
+            (q_low, q_low_any),
+            (k_low, k_low_any),
+            (v_low, v_low_any),
+        ),
+        store_sems,
+    )
+    scale = HEAD_DIM ** (-0.5)
+
+    def attend(first_owner, second_owner):
+        starts = (first_owner * rows, second_owner * rows + half)
+        spans = [span(start, half) for start in starts]
+
+        def read(ref):
+            return jnp.concatenate([ref[rows_of, :] for rows_of in spans], axis=0)
+
+        query = lax.broadcasted_iota(jnp.int32, (half, total_rows), 0)
+        query = jnp.concatenate([query + start for start in starts], axis=0)
+        key = lax.broadcasted_iota(jnp.int32, (rows, total_rows), 1)
+        scores = mul_t(read(q_low), k_low[...]) * scale
+        seen = (mul_t(read(reach_ref), member_ref[...]) > 0.5) & (key <= query)
+        scores = jnp.where(seen, scores, MASKED)
+        expo = jnp.exp(scores - jnp.max(scores, axis=1, keepdims=True))
+        chance = low(expo / jnp.sum(expo, axis=1, keepdims=True))
+        mixed = low(dot(chance, v_low[...]))
+        for side, rows_of in enumerate(spans):
+            probs[rows_of, :] = chance[side * half : (side + 1) * half]
+            att[rows_of, :] = mixed[side * half : (side + 1) * half]
+        part[...] = dot(mixed, o_proj[...])
+
+    piece = rows // 4
+    sums = RingSum(
+        place,
+        ends,
+        4,
+        (send_sem, recv_sem),
+        held,
+        lambda owner, lane: part[pl.ds(lane_offset(lane, rows), piece), :],
+    )
+    for step in range(RING_STEPS):
+        attend(
+            ring_index(lax.rem(place + HEADS - 1 - step, HEADS)),
+            ring_index(lax.rem(place + step + 1, HEADS)),
+        )
+        sums.send(step)
+    attend(index, index)
+    stores += start_loads(((att, att_any), (probs, probs_any)), store_sems.at[pl.ds(7, 2)])
+    for lane in range(4):
+        sum_ref[pl.ds(lane_offset(lane, rows), piece), :] = sums.last(index, lane)
+    sums.sent()
+    for copy in stores:
+        copy.wait()
+
+
+def attention_forward(hidden, q_head, kv_all, o_proj, norm, gains, cosine, sine, reach, member, number):
+    total, width = hidden.shape
+    rows = total // HEADS
+    steps = 4 * RING_STEPS
+    near, anywhere = pl.BlockSpec(memory_space=pltpu.VMEM), pl.BlockSpec(memory_space=pl.ANY)
+    bf16, f32 = jnp.bfloat16, jnp.float32
+    head = (total, HEAD_DIM)
+    kept = [
+        ((total, width), bf16),
+        ((width, 3 * HEAD_DIM), bf16),
+        (head, f32),
+        (head, f32),
+        (head, bf16),
+        (head, bf16),
+        (head, bf16),
+        (head, bf16),
+        ((total, total), bf16),
+    ]
+    return pl.pallas_call(
+        attention_kernel,
+        out_shape=[jax.ShapeDtypeStruct((rows, width), f32)]
+        + [jax.ShapeDtypeStruct(shape, dtype) for shape, dtype in kept],
+        in_specs=[anywhere] * 4 + [near] * 6,
+        out_specs=[near] + [anywhere] * len(kept),
+        scratch_shapes=[pltpu.VMEM((total, width), bf16), pltpu.VMEM(o_proj.shape, bf16)]
+        + [pltpu.VMEM(shape, dtype) for shape, dtype in kept]
+        + [
+            pltpu.VMEM((rows, width), f32),
+            pltpu.VMEM((steps + 4, rows // 4, width), bf16),
+            pltpu.SemaphoreType.DMA((5,)),
+            pltpu.SemaphoreType.DMA((9,)),
+            pltpu.SemaphoreType.DMA((steps,)),
+            pltpu.SemaphoreType.DMA((steps,)),
+        ],
+        compiler_params=pltpu.CompilerParams(
+            collective_id=number, has_side_effects=True, vmem_limit_bytes=VMEM_BYTES
+        ),
+    )(hidden, q_head, kv_all, o_proj, norm, gains, cosine, sine, reach, member)
 
 
 def ffn_kernel(
@@ -611,13 +713,7 @@
         def into(tile):
             value = mul_t(block[...], gate[tile, :])
             second = mul_t(block[...], up[tile, :])
-            square = value * value
-            bent = jnp.tanh(GELU_ROOT * value * (1.0 + GELU_CUBE * square))
-            share = 0.5 * (1.0 + bent)
-            act = value * share
-            slope = share + (0.5 * GELU_ROOT) * value * (1.0 - bent * bent) * (
-                1.0 + (3.0 * GELU_CUBE) * square
-            )
+            act, slope = gelu_parts(value)
             inner = low(act * second)
             inner_block[:, tile] = inner
             pair.write(act_ref, tile, low(act))
@@ -684,7 +780,13 @@
 
 
 def ffn_back_kernel(
-    own_ref,
+    first_ref,
+    ffw_ref,
+    extra_ref,
+    seed_ref,
+    gains_ref,
+    small_any,
+    pl_proj_any,
     all_any,
     act_any,
     slope_any,
@@ -692,13 +794,18 @@
     gate_any,
     up_any,
     down_any,
-    blocks_ref,
     sum_ref,
+    result_ref,
+    d_extra_ref,
+    d_second_ref,
+    gain_grads,
     down_out,
     gate_out,
     up_out,
     far_down,
-    block_sum,
+    theirs_any,
+    gate_sum,
+    proj_sum,
     d_all,
     tokens,
     d_up,
@@ -715,23 +822,46 @@
     give,
     keep,
     theirs,
-    block_held,
+    own_ref,
+    pl_gate,
+    pl_proj,
+    gate_blocks,
+    gate_folded,
+    gate_far,
+    gate_held,
+    proj_blocks,
+    proj_folded,
+    proj_far,
+    proj_held,
     load_sems,
     store_sems,
     *sems,
 ):
-    ring_sems, sum_sems, fold_sems, block_sems, far_sems = [
-        sems[i : i + 2] for i in range(0, 10, 2)
+    ring_sems, sum_sems, fold_sems, far_sems, gate_sems, proj_sems, pl_fold_sems, pl_far_sems = [
+        sems[i : i + 2] for i in range(0, 16, 2)
     ]
-    rows, width = own_ref.shape
+    rows, width = first_ref.shape
     units = gate.shape[0]
     piece = rows // 4
     index = lax.axis_index("fsdp")
     place = ring_place(index)
     ends = ring_ends(place)
     unused_chip, core, sibling, across = neighbours()
-    load_down, load_act, load_slope, load_gate, load_up, load_inner, load_tokens = start_loads(
+    per_layer = pl_gate.shape[1]
+    (
+        load_pl_gate,
+        load_pl_proj,
+        load_down,
+        load_act,
+        load_slope,
+        load_gate,
+        load_up,
+        load_inner,
+        load_tokens,
+    ) = start_loads(
         (
+            (small_any.at[:, pl.ds(0, per_layer)], pl_gate),
+            (pl_proj_any, pl_proj),
             (down_any, down),
             (act_any, d_up),
             (slope_any, d_gate),
@@ -755,13 +885,101 @@
     def own(owner, lane):
         return part[span(owner * rows + lane_offset(lane, rows), piece), :].astype(jnp.float32)
 
-    low_rows = block_sum.shape[0] // 2
-
-    def block_own(owner, lane):
-        return blocks_ref[owner, pl.ds(lane * low_rows, low_rows), :].astype(jnp.float32)
+    chip = neighbours()[0]
+    mine, yours = 2 * chip + core, 2 * (1 - chip) + core
+
+    def block_ring(block_sems, block_held, blocks):
+        low_rows = blocks.shape[2] // 2
+        return RingSum(
+            place,
+            ends,
+            2,
+            block_sems,
+            block_held,
+            lambda owner, lane: blocks[owner, mine, pl.ds(lane * low_rows, low_rows), :].astype(
+                jnp.float32
+            ),
+        )
 
     sums = RingSum(place, ends, 4, sum_sems, held, own)
-    block_sums = RingSum(place, ends, 2, block_sems, block_held, block_own)
+    pl_rings = (
+        block_ring(gate_sems, gate_held, gate_blocks),
+        block_ring(proj_sems, proj_held, proj_blocks),
+    )
+    pl_arrays = (
+        (gate_blocks, gate_folded, gate_far),
+        (proj_blocks, proj_folded, proj_far),
+    )
+    pl_folds, pl_sends = [], []
+
+    def per_layer_branch():
+        def after_ffw(tile):
+            value = ffw_ref[tile, :]
+            total = first_ref[tile, :] + value * root_of(value) * gains_ref[0:1, :]
+            sum_ref[tile, :] = total
+            block[tile, :] = low(total)
+
+        tile_loop(rows // 32, 32, after_ffw)
+        load_pl_gate.wait()
+        load_pl_proj.wait()
+        extra = extra_ref[...].astype(jnp.float32)
+        act, slope = gelu_parts(dot(block[...], pl_gate[...]))
+        mix = low(act * extra)
+        d_second_ref[...] = dot(mix, pl_proj[...])
+
+        def back_out(tile):
+            value = d_second_ref[tile, :]
+            result_ref[tile, :] = low(sum_ref[tile, :] + value * root_of(value) * gains_ref[1:2, :])
+            grad, gain_grad = norm_pull(
+                value, gains_ref[1:2, :], seed_ref[tile, :].astype(jnp.float32)
+            )
+            own_ref[tile, :] = low(grad)
+            gain_grads[1:2, :] += gain_grad
+
+        tile_loop(rows // 32, 32, back_out)
+        d_mix = mul_t(own_ref[...], pl_proj[...])
+        d_extra_ref[...] = low(d_mix * act)
+        d_pre = low(d_mix * extra * slope)
+        turned_mix = mix.T
+        deep = proj_blocks.shape[2]
+        for step in range(QUARTERS):
+            wide = proj_blocks.shape[3]
+            value = low(dot(turned_mix, own_ref[:, step * wide : (step + 1) * wide]))
+            for owner in range(HEADS):
+                proj_blocks[owner, step] = value[owner * deep : (owner + 1) * deep]
+        shard = width // HEADS
+        for owner in range(HEADS):
+            value = low(dot(block[:, owner * shard : (owner + 1) * shard].T, d_pre))
+            for step in range(QUARTERS):
+                gate_blocks[owner, step] = value[
+                    step * (shard // QUARTERS) : (step + 1) * (shard // QUARTERS)
+                ]
+        d_second_ref[...] = mul_t(d_pre, pl_gate[...])
+
+        def back_ffw(tile):
+            grad = seed_ref[tile, :].astype(jnp.float32) + d_second_ref[tile, :]
+            d_second_ref[tile, :] = grad
+            grad, gain_grad = norm_pull(ffw_ref[tile, :], gains_ref[0:1, :], grad)
+            own_ref[tile, :] = low(grad)
+            gain_grads[0:1, :] += gain_grad
+
+        tile_loop(rows // 32, 32, back_ffw)
+
+    def pl_fold():
+        for number, (blocks, folded, far) in enumerate(pl_arrays):
+            for side in range(2):
+                pl_folds[2 * number + side].wait_recv()
+            for owner in range(HEADS):
+                blocks[owner, yours] = add_low(blocks[owner, yours], folded[1 - chip, owner])
+            pl_sends.append(remote(blocks.at[:, yours], far, pl_far_sems, number, across))
+            for owner in range(HEADS):
+                blocks[owner, mine] = add_low(blocks[owner, mine], folded[chip, owner])
+
+    def pl_join():
+        for number, (blocks, folded, far) in enumerate(pl_arrays):
+            pl_sends[number].wait_recv()
+            for owner in range(HEADS):
+                blocks[owner, mine] = add_low(blocks[owner, mine], far[owner])
 
     def compute(step):
         pair = Pair(place, step, rows)
@@ -808,16 +1026,19 @@
         if number:
             folds[number - 1].wait_send()
         outer_half(number, 1 - core, give)
-        folds.append(remote(give, theirs.at[number], fold_sems, number, sibling))
+        folds.append(remote(give, theirs_any.at[number], fold_sems, number, sibling))
 
     def grads_keep(number):
         if number > 1:
             stores[number - 1].wait()
         outer_half(number, core, keep)
         folds[number].wait_recv()
+        load = pltpu.make_async_copy(theirs_any.at[number], theirs, load_sems.at[9])
+        load.start()
+        load.wait()
 
         def add(tile):
-            keep[tile, :] = add_low(keep[tile, :], theirs[number, tile, :])
+            keep[tile, :] = add_low(keep[tile, :], theirs[tile, :])
 
         tile_loop(half // 64, 64, add)
         store = pltpu.make_async_copy(keep, jobs[number][2], store_sems.at[number])
@@ -827,7 +1048,20 @@
             store.wait()
             swaps.append(remote(down_out, far_down, far_sems, 0, across))
 
+    gain_grads[...] = jnp.zeros_like(gain_grads)
+    per_layer_branch()
     ring.send(0)
+    for number, (blocks, folded, unused_far) in enumerate(pl_arrays):
+        for side in range(2):
+            pl_folds.append(
+                remote(
+                    blocks.at[:, 2 * side + 1 - core],
+                    folded.at[side],
+                    pl_fold_sems,
+                    2 * number + side,
+                    sibling,
+                )
+            )
     d_all[span(index * rows, rows), :] = own_ref[...]
     for copy in (load_down, load_act, load_slope):
         copy.wait()
@@ -840,12 +1074,17 @@
         if step >= RING_STEPS - 1:
             sums.send(step - RING_STEPS + 1)
         compute(step)
+        if step == 2:
+            pl_fold()
+        if step == 4:
+            pl_join()
     load_inner.wait()
     load_tokens.wait()
     for step in range(RING_STEPS):
         if step >= 2:
             sums.send(step)
-        block_sums.send(step)
+        for item in pl_rings:
+            item.send(step)
         if step < 6:
             if step % 2:
                 grads_keep(step // 2)
@@ -853,32 +1092,55 @@
                 grads_give(step // 2)
     for lane in range(4):
         sum_ref[pl.ds(lane_offset(lane, rows), piece), :] = sums.last(index, lane)
-    for lane in range(2):
-        block_sum[pl.ds(lane * low_rows, low_rows), :] = low(block_sums.last(index, lane))
-    for item in (ring, sums, block_sums):
+    for item, target in zip(pl_rings, (gate_sum, proj_sum)):
+        low_rows = target.shape[0] // 2
+        for lane in range(2):
+            target[pl.ds(lane * low_rows, low_rows), :] = low(item.last(index, lane))
+    for item in (ring, sums) + pl_rings:
         item.sent()
+    for copy in pl_folds + pl_sends:
+        copy.wait_send()
     folds[-1].wait_send()
     stores[-1].wait()
     swaps[0].wait()
 
 
-def ffn_back(own, arrays, weights, blocks, number):
-    rows, width = own.shape
+def ffn_back(local, gains, small, pl_proj, arrays, weights, number):
+    rows, width = local[0].shape
     units = weights[0].shape[0]
     near, anywhere = pl.BlockSpec(memory_space=pltpu.VMEM), pl.BlockSpec(memory_space=pl.ANY)
     total = rows * HEADS
     steps = 4 * RING_STEPS
-    bf16 = jnp.bfloat16
-    counts = [steps, steps, 3, 2 * RING_STEPS, 1]
+    bf16, f32 = jnp.bfloat16, jnp.float32
+    low_steps = 2 * RING_STEPS
+    counts = [steps, steps, 3, 1, low_steps, low_steps, 4, 2]
     half = (units // 2, width)
-    low_rows = blocks.shape[1] // 2
+    deep, per_layer = pl_proj.shape[0] // HEADS, local[2].shape[1]
+    gate_block = (width // HEADS // QUARTERS, per_layer)
+    proj_block = (deep, width // QUARTERS)
+
+    def block_scratch(shape):
+        return [
+            pltpu.VMEM((HEADS, QUARTERS) + shape, bf16),
+            pltpu.VMEM((2, HEADS) + shape, bf16),
+            pltpu.VMEM((HEADS,) + shape, bf16),
+            pltpu.VMEM((low_steps + 2, shape[0] // 2, shape[1]), bf16),
+        ]
+
     return pl.pallas_call(
         ffn_back_kernel,
-        out_shape=[jax.ShapeDtypeStruct((rows, width), jnp.float32)]
+        out_shape=[
+            jax.ShapeDtypeStruct((rows, width), f32),
+            jax.ShapeDtypeStruct((rows, width), bf16),
+            jax.ShapeDtypeStruct((rows, per_layer), bf16),
+            jax.ShapeDtypeStruct((rows, width), f32),
+            jax.ShapeDtypeStruct(gains.shape, f32),
+        ]
         + [jax.ShapeDtypeStruct(half, bf16)] * 4
-        + [jax.ShapeDtypeStruct(blocks.shape[1:], bf16)],
-        in_specs=[near] + [anywhere] * 7 + [near],
-        out_specs=[near] + [anywhere] * 4 + [near],
+        + [jax.ShapeDtypeStruct((3,) + half, bf16)]
+        + [jax.ShapeDtypeStruct(gate_block, bf16), jax.ShapeDtypeStruct(proj_block, bf16)],
+        in_specs=[near] * 5 + [anywhere] * 9,
+        out_specs=[near] * 5 + [anywhere] * 5 + [near] * 2,
         scratch_shapes=[pltpu.VMEM((total, width), bf16)] * 2
         + [pltpu.VMEM((total, units), bf16)] * 3
         + [pltpu.VMEM((units, width), bf16)] * 3
@@ -890,20 +1152,19 @@
             pltpu.VMEM((units // 2, total), bf16),
             pltpu.VMEM(half, bf16),
             pltpu.VMEM(half, bf16),
-            pltpu.VMEM((3,) + half, bf16),
-            pltpu.VMEM((2 * RING_STEPS + 2, low_rows, blocks.shape[2]), bf16),
-            pltpu.SemaphoreType.DMA((7,)),
-            pltpu.SemaphoreType.DMA((3,)),
+            pltpu.VMEM(half, bf16),
+            pltpu.VMEM((rows, width), bf16),
+            pltpu.VMEM((width, per_layer), bf16),
+            pltpu.VMEM(pl_proj.shape, bf16),
         ]
+        + block_scratch(gate_block)
+        + block_scratch(proj_block)
+        + [pltpu.SemaphoreType.DMA((10,)), pltpu.SemaphoreType.DMA((3,))]
         + [pltpu.SemaphoreType.DMA((count,)) for count in counts for unused_side in range(2)],
         compiler_params=pltpu.CompilerParams(
-            collective_id=number, has_side_effects=True, vmem_limit_bytes=56 << 20
+            collective_id=number, has_side_effects=True, vmem_limit_bytes=58 << 20
         ),
-    )(own, *arrays, *weights, blocks)
-
-
-ACROSS = ((0, 2), (2, 0), (1, 3), (3, 1))
-SIBLING = ((0, 1), (1, 0), (2, 3), (3, 2))
+    )(*local, gains, small, pl_proj, *arrays, *weights)
 
 
 def head_back(grad, raw, gain, cosine, sine):
@@ -935,7 +1196,8 @@
     sine_any,
     laurel_any,
     gains_ref,
-    pl_ref,
+    pl_gate_ref,
+    pl_proj_ref,
     own_down,
     far_down,
     own_gate,
@@ -943,6 +1205,7 @@
     sum_ref,
     owned_ref,
     early_ref,
+    pl_proj_all,
     gain_grads,
     total_down,
     total_gate,
@@ -989,7 +1252,7 @@
 ):
     pairs = [sems[i : i + 2] for i in range(0, len(sems), 2)]
     ring_sems, sum_sems, fold_sems, far_sems, swap_sems, key_sems = pairs[:6]
-    mirror_sems, early_sems, o_fold_sems, o_far_sems, cross_sems, total_sems = pairs[6:]
+    mirror_sems, early_sems, o_fold_sems, o_far_sems, cross_sems, total_sems, proj_sems = pairs[6:]
     rows, width = own_ref.shape
     total_rows = rows * HEADS
     half = rows // 2
@@ -1179,7 +1442,10 @@
         o_folds.append(
             remote(o_grad.at[2 * side + 1 - core], o_folded.at[side], o_fold_sems, side, sibling)
         )
-    mirror, early = Mirror(1, mirror_sems), Mirror(1, early_sems)
+    mirror, early, pl_mirror = Mirror(1, mirror_sems), Mirror(1, early_sems), Mirror(1, proj_sems)
+    wide = pl_proj_ref.shape[1]
+    own_columns = span(quarter * wide, wide)
+    other_columns = span((2 * (1 - chip) + core) * wide, wide)
     rest = blocks.shape[3] - HEAD_DIM
     q_columns = HEADS * HEAD_DIM
     mine, yours = 2 * chip + core, 2 * (1 - chip) + core
@@ -1234,8 +1500,10 @@
         key_held[index] = near_sum[index, :, HEAD_DIM:]
         across_sends[1].wait_recv()
         early_ref[own_rows, :width] = add_low(o_grad[mine], o_far[...])
-        early_ref[own_rows, width:] = pl_ref[...]
+        early_ref[own_rows, width:] = pl_gate_ref[...]
         early.give(0, early_ref.at[own_rows])
+        pl_proj_all[:, own_columns] = pl_proj_ref[...]
+        pl_mirror.give(0, pl_proj_all.at[:, own_columns])
 
     for step in range(2, RING_STEPS):
         part_of(step)
@@ -1251,6 +1519,7 @@
             add_final(1)
         if step == 6:
             early.relay(0, early_ref.at[other_rows])
+            pl_mirror.relay(0, pl_proj_all.at[:, other_columns])
     part[...] = mul_t(d_qkv[span(index * rows, rows), :], weights[...])
     for lane in range(4):
         sum_ref[pl.ds(lane_offset(lane, rows), piece), :] = sums.last(index, lane)
@@ -1279,6 +1548,7 @@
     add_final(2)
     mirror.finish()
     early.finish()
+    pl_mirror.finish()
     ring.sent()
     sums.sent()
     for copy in folds + o_folds + across_sends + swaps + key_swaps + crossings:
@@ -1289,7 +1559,7 @@
         copy.wait_recv()
 
 
-def attention_back(own, arrays, laurel, gains, pl_sum, chip_grads, far_down, number):
+def attention_back(own, arrays, laurel, gains, pl_sums, chip_grads, far_down, number):
     rows, width = own.shape
     total = rows * HEADS
     shard = width // HEADS
@@ -1301,7 +1571,8 @@
     near, anywhere = pl.BlockSpec(memory_space=pltpu.VMEM), pl.BlockSpec(memory_space=pl.ANY)
     bf16, f32 = jnp.bfloat16, jnp.float32
     owned = (HEADS + 2 * KV_HEADS) * HEAD_DIM + laurel.shape[3]
-    counts = [steps, steps, 2, 1, HEADS - 1, HEADS - 1, 3, 3, 2, 1, 3, 3]
+    counts = [steps, steps, 2, 1, HEADS - 1, HEADS - 1, 3, 3, 2, 1, 3, 3, 3]
+    pl_gate, pl_proj = pl_sums
     down, gate, up = chip_grads
     whole = jax.ShapeDtypeStruct((2 * half[0], half[1]), bf16)
     part = jax.ShapeDtypeStruct(half, bf16)
@@ -1310,7 +1581,8 @@
         out_shape=[
             jax.ShapeDtypeStruct((rows, width), f32),
             jax.ShapeDtypeStruct((shard, owned), bf16),
-            jax.ShapeDtypeStruct((shard, width + pl_sum.shape[1]), bf16),
+            jax.ShapeDtypeStruct((shard, width + pl_gate.shape[1]), bf16),
+            jax.ShapeDtypeStruct((pl_proj.shape[0], width), bf16),
             jax.ShapeDtypeStruct(gains.shape, f32),
             whole,
             whole,
@@ -1318,8 +1590,8 @@
             part,
             part,
         ],
-        in_specs=[near] + [anywhere] * (len(arrays) + 1) + [near] * 2 + [anywhere] * 4,
-        out_specs=[near] * 4 + [anywhere] * 5,
+        in_specs=[near] + [anywhere] * (len(arrays) + 1) + [near] * 3 + [anywhere] * 4,
+        out_specs=[near] * 5 + [anywhere] * 5,
         scratch_shapes=[pltpu.VMEM(item.shape, item.dtype) for item in arrays]
         + [
             pltpu.VMEM((total, width), bf16),
@@ -1351,7 +1623,7 @@
         compiler_params=pltpu.CompilerParams(
             collective_id=number, has_side_effects=True, vmem_limit_bytes=56 << 20
         ),
-    )(own, *arrays, laurel, gains, pl_sum, down, far_down, gate, up)
+    )(own, *arrays, laurel, gains, pl_gate, pl_proj, down, far_down, gate, up)
 
 
 def gains_kernel(parts_ref, sum_ref, landed, totals, send_sem, recv_sem, rep_send, rep_recv):
@@ -1400,29 +1672,6 @@
         + [pltpu.SemaphoreType.DMA((QUARTERS - 1,))] * 2,
         compiler_params=pltpu.CompilerParams(collective_id=number, has_side_effects=True),
     )(parts)
-
-
-def core_fold(value, axis):
-    half = value.shape[axis] // 2
-    core = lax.rem(lax.axis_index("rep"), 2)
-    give = lax.dynamic_slice_in_dim(value, (1 - core) * half, half, axis)
-    keep = lax.dynamic_slice_in_dim(value, core * half, half, axis)
-    return add_low(keep, lax.ppermute(give, "rep", SIBLING))
-
-
-def chip_fold(value, axis):
-    half = value.shape[axis] // 2
-    chip = lax.axis_index("rep") // 2
-    give = lax.dynamic_slice_in_dim(value, (1 - chip) * half, half, axis)
-    keep = lax.dynamic_slice_in_dim(value, chip * half, half, axis)
-    return add_low(keep, lax.ppermute(give, "rep", ACROSS))
-
-
-def quarter_fold(value):
-    value = value.reshape(value.shape[:-3] + (2, 2) + value.shape[-2:])
-    axis = value.ndim - 4
-    value = chip_fold(core_fold(value, axis + 1), axis)
-    return value.reshape(value.shape[:axis] + value.shape[axis + 2 :])
 
 
 def dot(left, right):
@@ -1482,11 +1731,8 @@
     rows, width = hidden_in.shape
     shard = width // HEADS
     total = rows * HEADS
-    groups = HEADS // KV_HEADS
-    scale = HEAD_DIM ** (-0.5)
     rank = laurel_left.shape[1]
     per_layer = pl_gate.shape[1]
-    key_head = index // groups
 
     gains = (attn_norm, attn_post_norm, laurel_norm, ffw_norm, ffw_post_norm, pl_post_norm)
     packed = jnp.concatenate(gains + (q_norm, k_norm))
@@ -1509,21 +1755,11 @@
     gain_qnorm = all_gains[:, at : at + piece].reshape(-1)
     gain_knorm = all_gains[:, at + piece : at + 2 * piece].reshape(-1)
 
-    k_head = lax.dynamic_slice_in_dim(kv_all, key_head * HEAD_DIM, HEAD_DIM, 1)
-    v_head = lax.dynamic_slice_in_dim(kv_all, (KV_HEADS + key_head) * HEAD_DIM, HEAD_DIM, 1)
-    full_plgate = small_all[:, :per_layer]
     full_left = small_all[:, per_layer : per_layer + rank]
     full_right = small_all[:, per_layer + rank :]
 
     tokens, member, reach, position = tree_places(seg_lengths[0], seg_parents[0], total)
     depth = position.astype(jnp.float32)
-    seen = (mul_t(reach, member) > 0) & (tokens[None, :] <= tokens[:, None])
-
-    normed_all = low(norm_rows(hidden_all.astype(jnp.float32), gain_anorm))
-    q_raw = dot(normed_all, q_head)
-    k_raw = dot(normed_all, k_head)
-    v_low = low(dot(normed_all, v_head))
-
     half = HEAD_DIM // 2
     freqs = jnp.exp(
         jnp.arange(half, dtype=jnp.float32) * (-2.0 * math.log(ROPE_BASE) / HEAD_DIM)
@@ -1531,27 +1767,36 @@
     angle = depth[:, None] * freqs[None, :]
     cosine, sine = jnp.cos(angle), jnp.sin(angle)
 
-    def head_path(raw, gain):
-        value = norm_rows(raw, gain)
-        first, second = value[:, :half], value[:, half:]
-        return jnp.concatenate(
-            [first * cosine - second * sine, second * cosine + first * sine], axis=1
-        )
-
-    q_low = low(head_path(q_raw, gain_qnorm))
-    k_low = low(head_path(k_raw, gain_knorm))
-    scores = jnp.where(seen, mul_t(q_low, k_low) * scale, MASKED)
-    top = jnp.max(scores, axis=-1, keepdims=True)
-    expo = jnp.exp(scores - top)
-    sums = jnp.sum(expo, axis=-1, keepdims=True)
-    probs = expo / sums
-    probs_low = low(probs)
-    attended = dot(probs_low, v_low)
-    attended_low = low(attended)
-    (branch,) = ring_scatter(low(dot(attended_low, o_proj)), 6)
+    def padded(item):
+        return jnp.pad(item, ((0, 0), (0, 128 - item.shape[1])))
+
+    head_gain = jnp.stack([gain_qnorm, gain_knorm])
+    (
+        branch,
+        normed_all,
+        qkv_head,
+        q_raw,
+        k_raw,
+        q_low,
+        k_low,
+        v_low,
+        attended_low,
+        probs_low,
+    ) = attention_forward(
+        hidden_all,
+        q_head,
+        kv_all,
+        o_proj,
+        gain_anorm[None, :],
+        head_gain,
+        cosine,
+        sine,
+        padded(reach),
+        padded(member),
+        6,
+    )
 
     source = hidden_in.astype(jnp.float32)
-    extra = layer_input.astype(jnp.float32)
     normed = norm_rows(source, gain_anorm)
     normed_low = low(normed)
     left_low = low(dot(normed_low, full_left))
@@ -1564,39 +1809,18 @@
     ffw_out, ffw_all, act, slope, inner_low = ffn_forward(
         ffw_low, gate_proj, up_proj, down_proj, 7
     )
-    second_sum = first_sum + norm_rows(ffw_out, gain_fpost)
-    second_low = low(second_sum)
-    pl_pre = dot(second_low, full_plgate)
-    pl_mix = low(gelu_mix(pl_pre, extra))
-    pl_out = dot(pl_mix, full_plproj)
-    result = second_sum + norm_rows(pl_out, gain_plpost)
-    seed = out_grad.astype(jnp.float32)
-    d_plout, grad_plpost = norm_back(pl_out, gain_plpost, seed)
-    d_plout_low = low(d_plout)
-    grad_plproj = outer(pl_mix, d_plout_low)
-    d_mix = mul_t(d_plout_low, full_plproj)
-    d_pre, d_extra = mix_back(pl_pre, extra, d_mix)
-    d_pre_low = low(d_pre)
-    grad_plgate = outer(second_low, d_pre_low)
-    d_second = seed + mul_t(d_pre_low, full_plgate)
-    pl_blocks = jnp.concatenate(
-        [
-            low(grad_plgate).reshape(HEADS, shard, per_layer),
-            low(grad_plproj).reshape(HEADS, shard, per_layer),
-        ],
-        axis=-1,
-    )
-    pl_blocks = quarter_fold(pl_blocks.reshape(HEADS, QUARTERS, -1, 2 * per_layer))
-    d_ffwout, grad_fpost = norm_back(ffw_out, gain_fpost, d_second)
-
-    d_ffwin, *rest = ffn_back(
-        low(d_ffwout),
+    d_ffwin, result, d_extra, d_second, ffw_gains, *rest = ffn_back(
+        (first_sum, ffw_out, layer_input, out_grad),
+        jnp.stack([gain_fpost, gain_plpost]),
+        small_all,
+        full_plproj,
         (ffw_all, act, slope, inner_low),
         (gate_proj, up_proj, down_proj),
-        pl_blocks,
         9,
     )
-    chip_grads, far_down, pl_sum = rest[:3], rest[3], rest[4]
+    grad_fpost, grad_plpost = ffw_gains
+    chip_grads, far_down, pl_sums = rest[:3], rest[3], rest[5:]
+
     d_first_part, grad_fnorm = norm_back(first_sum, gain_fnorm, d_ffwin)
     d_scaled = (d_second + d_first_part) * HALF_ROOT
     d_branch, grad_apost = norm_back(branch, gain_apost, d_scaled)
@@ -1606,7 +1830,7 @@
     d_left_low = low(dot(d_lowrank_low, full_right))
     grad_left = outer(normed_low, d_left_low)
 
-    d_normed_sum, owned, early, head_gains, *totals = attention_back(
+    d_normed_sum, owned, early, sum_plproj, head_gains, *totals = attention_back(
         low(d_branch),
         (
             o_proj,
@@ -1616,15 +1840,15 @@
             attended_low,
             probs_low,
             normed_all,
-            jnp.concatenate([q_head, k_head, v_head], axis=1),
+            qkv_head,
             q_raw,
             k_raw,
             cosine,
             sine,
         ),
         low(jnp.concatenate([grad_left, grad_right], axis=1)),
-        jnp.stack([gain_qnorm, gain_knorm]),
-        pl_sum,
+        head_gain,
+        pl_sums,
         chip_grads,
         far_down,
         12,
@@ -1651,9 +1875,9 @@
     sum_qnorm = small_sums[at : at + piece]
     sum_knorm = small_sums[at + piece : at + 2 * piece]
     return (
-        low(result),
+        result,
         low(d_source),
-        low(d_extra),
+        d_extra,
         sum_anorm,
         owned[:, :width],
         owned[:, key_at:value_at],
@@ -1670,8 +1894,8 @@
         sum_up,
         sum_down,
         sum_fpost,
-        early[:, width : width + per_layer],
-        early[:, width + per_layer :].reshape(pl_proj.shape),
+        early[:, width:],
+        sum_plproj.astype(jnp.float32),
         sum_plpost,
     )
 

time: 639 us -> 582 us (0.911)
  other arithmetic: 62.3 us -> 37.2 us
  matrix products: 30.4 us -> 8.15 us
  Pallas kernels: 485 us -> 499 us
  waiting for transfers between devices: 11.2 us -> 0 us
  local copies, waits for them, and re-layouts: 37.8 us -> 28.3 us
    pallas_call x1, Pallas kernels: 43.6 us -> 55.2 us  [attention_forward(): pl.pallas_call(attention_kernel, out_shape=[jax.ShapeDtypeStruct((rows, w...]
    ppermute x2 -> x0, waiting for transfers between devices: 11.2 us -> none  [the longest x1 11.2 us: chip_fold(): return add_low(keep, lax.ppermute(give, 'rep', ACROSS))]
    dot_general x8 -> x2, matrix products: 12.5 us -> 3.11 us  [dot(): return jnp.dot(left, right, preferred_element_type=jnp.float32)]
    dot_general x6 -> x2, matrix products: 13.1 us -> 4.48 us  [mul_t(): lax.dot_general(left, right, (((1,), (1,)), ((), ())), preferred_element_...]
    concatenate x3 -> x0, other arithmetic: 8.29 us -> none  [the longest x1 3.12 us: head_plan(): jnp.concatenate([q_head, k_head, v_head], axis=1)]
    pallas_call x1, Pallas kernels: 114 us -> 121 us  [ffn_back(): pl.pallas_call(ffn_back_kernel, out_shape=[jax.ShapeDtypeStruct((rows, wi...]
    convert_element_type x8 -> x3, other arithmetic: 12.6 us -> 6.14 us  [low(): return value.astype(jnp.bfloat16)]
  transfers between devices with their start and end apart: 2 -> 0, of which waited for: 1 -> 0; matrix products, arithmetic and copies ran while one was open for 3% -> 0% of each run, Pallas kernels for 0% -> 0%
where the time goes in v4:
time: 582 us; the launch traced here: 574 us
  Pallas kernels  499 us (86%)
  other arithmetic  37.2 us (6%)
  local copies, waits for them, and re-layouts  28.3 us (5%)
  matrix products  8.15 us (1%)
    pallas_call x1, Pallas kernels, attention_back(): pl.pallas_call(attention_back_kernel, out_shape=[jax.ShapeDtypeStruct((ro...  147 us
    pallas_call x1, Pallas kernels, ffn_back(): pl.pallas_call(ffn_back_kernel, out_shape=[jax.ShapeDtypeStruct((rows, wi...  121 us
    pallas_call x1, Pallas kernels, ffn_forward(): pl.pallas_call(ffn_kernel, out_shape=[jax.ShapeDtypeStruct((rows, width),...  88.6 us
    pallas_call x1, Pallas kernels, start_gather(): pl.pallas_call(start_kernel, out_shape=[grown(hidden), grown(gains), grow...  76.7 us
    pallas_call x1, Pallas kernels, attention_forward(): pl.pallas_call(attention_kernel, out_shape=[jax.ShapeDtypeStruct((rows, w...  55.2 us
    convert_element_type x3, other arithmetic, head_plan(): item.astype(jnp.float32)  13.3 us

profile of v4, /device:TPU:0, one launch (start us, length us, event | category | flops | bytes accessed | tf_op | source)
XLA Modules:
  0.0 574.3 jit_solution(6036215967241127418)
XLA Ops:
  0.7 1.3 fusion.12
  5.3 5.4 concatenate.21
  13.0 1.7 pad_maximum_fusion.2.small_ref
  16.6 1.9 multiply_sine_fusion
  18.5 76.7 %shard_map.399 = (bf16[1024,2048]{1,0:T(8,128)(2,1)}, bf16[256,128]{1,0:T(8,128)(2,1)}, bf16[2048,256]{1,0:T(8,128)(2,1)}, bf16[2048,1024]{1,0:T(8,128)(2,1)}, b...) custom-call(bf16[128,2048]{1,0:T(8,128)(2,1)} %hidden_ref.1, bf16[32,128]{1,0:T(8,128)(2,1)} %pad_bitcast_fusion.1.gains_ref, ...), custom_call_target="tpu_custom_call" | custom-call | tf_op jit(solution)/shard_map/pallas_call | solution.py:364
  97.1 1.4 convolution_convert_fusion.3
  98.6 1.6 multiply_reduce_fusion.7
  100.2 55.2 %shard_map.400 = (f32[128,2048]{1,0:T(8,128)S(1)}, bf16[1024,2048]{1,0:T(8,128)(2,1)}, bf16[2048,768]{1,0:T(8,128)(2,1)}, f32[1024,256]{1,0:T(8,128)S(1)}, f32[1...) custom-call(bf16[1024,2048]{1,0:T(8,128)(2,1)} %get-tuple-element.62, ...), custom_call_target="tpu_custom_call" | custom-call | tf_op jit(solution)/shard_map/pallas_call | solution.py:642
  157.1 1.1 multiply_convert_fusion
  158.3 88.6 %shard_map.401 = (f32[128,2048]{1,0:T(8,128)S(1)}, bf16[1024,2048]{1,0:T(8,128)(2,1)}, bf16[1024,1024]{1,0:T(8,128)(2,1)S(1)}, bf16[1024,1024]{1,0:T(8,128)(2,1)S(1)}, bf16[1024,1024]{1,0:T(8,128)(2,1)}) custom-call(bf16[128,2048]{1,0:T(8,128)(2,1)S(1)} %get-tuple-element.171.own_ref, bf16[1024,2048]{1,0:T(8,128)(2,1)} %gate_any.3, ...), custom_call_target="tpu_custom_call" | custom-call | tf_op jit(solution)/shard_map/pallas_call | solution.py:756
  246.9 1.3 copy-done.2
  248.2 1.3 copy-done.3
  250.5 120.8 %shard_map.402 = (f32[128,2048]{1,0:T(8,128)}, bf16[128,2048]{1,0:T(8,128)(2,1)}, bf16[128,256]{1,0:T(8,128)(2,1)}, f32[128,2048]{1,0:T(8,128)}, f32[2,2048]{1,0...) custom-call(f32[128,2048]{1,0:T(8,128)} %get-tuple-element.172.first, ...), custom_call_target="tpu_custom_call" | custom-call | tf_op jit(solution)/shard_map/pallas_call | solution.py:1130
  371.3 1.6 multiply_reduce_fusion
  372.9 3.3 multiply_reduce_fusion.1
  376.3 2.5 fusion.8
  378.8 1.7 convolution_convert_fusion.2
  381.7 1.1 pad_maximum_fusion.1.laurel_any
  382.8 146.9 %shard_map.403 = (f32[128,2048]{1,0:T(8,128)}, bf16[256,3200]{1,0:T(8,128)(2,1)}, bf16[256,2304]{1,0:T(8,128)(2,1)}, bf16[32,2048]{1,0:T(8,128)(2,1)}, f32[2,256...) custom-call(bf16[128,2048]{1,0:T(8,128)(2,1)} %get-tuple-element.170, ...), custom_call_target="tpu_custom_call" | custom-call | tf_op jit(solution)/shard_map/pallas_call | solution.py:1579
  529.7 2.9 fusion.6
  532.7 2.5 fusion.11
  536.1 10.7 %shard_map.404 = f32[16,128]{1,0:T(8,128)} custom-call(f32[8,16,128]{2,1,0:T(8,128)} %bitcast.67), custom_call_target="tpu_custom_call" | custom-call | tf_op jit(solution)/shard_map/pallas_call | solution.py:1662
  546.8 1.3 fusion.36
  548.2 1.4 slice_bitcast_fusion.7
  550.3 1.6 slice.140
  553.4 1.6 slice.137
  555.0 1.1 fusion.34
  556.1 1.6 slice.132
  557.7 1.4 copy-done.20
  559.1 4.4 convert_element_type.83
  563.5 4.4 convert_element_type.84
  568.0 4.4 convert_element_type.85
  (122 shorter events, 17.8 us)
Async XLA Ops:
  0.7 15.1 %copy-start.22 = (bf16[256,512]{1,0:T(8,128)(2,1)S(1)}, bf16[256,512]{1,0:T(8,128)(2,1)}, u32[]{:S(2)}) copy-start(bf16[256,512]{1,0:T(8,128)(2,1)} %param.32) | copy-start | bytes 786436
  0.7 15.1 %copy-start.23 = (bf16[256,512]{1,0:T(8,128)(2,1)S(1)}, bf16[256,512]{1,0:T(8,128)(2,1)}, u32[]{:S(2)}) copy-start(bf16[256,512]{1,0:T(8,128)(2,1)} %param.31) | copy-start | bytes 786436
  16.6 80.5 %copy-start.14 = (bf16[128,2048]{1,0:T(8,128)(2,1)S(1)}, bf16[128,2048]{1,0:T(8,128)(2,1)}, u32[]{:S(2)}) copy-start(bf16[128,2048]{1,0:T(8,128)(2,1)} %hidden_ref.1) | copy-start | bytes 1572868
  18.5 81.6 %copy-start = (f32[1024,128]{1,0:T(8,128)}, f32[1024,128]{1,0:T(8,128)S(1)}, u32[]{:S(2)}) copy-start(f32[1024,128]{1,0:T(8,128)S(1)} %get-tuple-element.190.sine_ref.sine_any) | copy-start | bytes 1572868
  18.5 81.6 %copy-start.1 = (f32[1024,128]{1,0:T(8,128)}, f32[1024,128]{1,0:T(8,128)S(1)}, u32[]{:S(2)}) copy-start(f32[1024,128]{1,0:T(8,128)S(1)} %get-tuple-element.191.cosine_ref.cosine_any) | copy-start | bytes 1572868
  96.4 59.0 %copy-start.10 = (f32[2,256]{1,0:T(2,128)}, f32[2,256]{1,0:T(2,128)S(1)}, u32[]{:S(2)}) copy-start(f32[2,256]{1,0:T(2,128)S(1)} %pad_maximum_fusion.4.gains_ref) | copy-start | bytes 6148
  100.1 55.5 %copy-start.11 = (f32[128,2048]{1,0:T(8,128)}, f32[128,2048]{1,0:T(8,128)S(1)}, u32[]{:S(2)}) copy-start(f32[128,2048]{1,0:T(8,128)S(1)} %get-tuple-element.195) | copy-start | bytes 3145732
  155.4 1.0 copy-start.4
  155.4 1.1 copy-start.6
  155.5 1.3 copy-start.7
  155.5 1.4 copy-start.8
  155.5 1.6 copy-start.9
  246.9 1.3 copy-start.2
  248.2 1.3 copy-start.3
  249.5 1.0 copy-start.5
  371.3 1.6 copy-start.12
  376.3 4.4 copy-start.26
  378.8 2.3 copy-start.15
  382.8 146.9 %copy-start.13 = (f32[128,2048]{1,0:T(8,128)S(1)}, f32[128,2048]{1,0:T(8,128)}, u32[]{:S(2)}) copy-start(f32[128,2048]{1,0:T(8,128)} %get-tuple-element.162) | copy-start | bytes 3145732
  532.6 2.6 copy-start.27
  532.6 17.0 %copy-start.24 = (bf16[32,2048]{1,0:T(8,128)(2,1)S(1)}, bf16[32,2048]{1,0:T(8,128)(2,1)}, u32[]{:S(2)}) copy-start(bf16[32,2048]{1,0:T(8,128)(2,1)} %get-tuple-element.101) | copy-start | bytes 393220
  532.6 19.3 %copy-start.16 = (bf16[256,3200]{1,0:T(8,128)(2,1)S(1)}, bf16[256,3200]{1,0:T(8,128)(2,1)}, u32[]{:S(2)}) copy-start(bf16[256,3200]{1,0:T(8,128)(2,1)} %get-tuple-element.96) | copy-start | bytes 4915204
  535.2 18.3 %copy-start.17 = (bf16[256,2304]{1,0:T(8,128)(2,1)S(1)}, bf16[256,2304]{1,0:T(8,128)(2,1)}, u32[]{:S(2)}) copy-start(bf16[256,2304]{1,0:T(8,128)(2,1)} %get-tuple-element.97) | copy-start | bytes 3538948
  556.1 2.9 copy-start.20
  559.0 4.5 copy-start.19
  563.5 4.5 copy-start.18
  568.0 4.5 copy-start.21
  568.0 5.2 copy-start.25

commit v5 on v4

--- a/solution.py
+++ b/solution.py
@@ -181,202 +181,30 @@
             ref, ref, self.sems, 2 * self.count + number, self.sibling
         )
 
-    def finish(self):
+    def arrive(self):
         for number, copy in enumerate(self.copies):
             if number // self.count != 1:
                 copy.wait_recv()
+
+    def sent(self):
+        for copy in self.copies:
             copy.wait_send()
+
+    def finish(self):
+        self.arrive()
+        self.sent()
 
 
 RING_STEPS = HEADS - 1
 QUARTERS = 4
 
 
-def start_kernel(
-    hidden_ref,
-    gains_ref,
-    q_ref,
-    kv_ref,
-    small_ref,
-    plproj_ref,
-    hidden_all,
-    gains_all,
-    q_head,
-    kv_all,
-    small_all,
-    plproj_all,
-    local_sems,
-    *sems,
-):
-    pairs = [sems[i : i + 2] for i in range(0, len(sems), 2)]
-    hidden_sems, gains_sems, q_sems, kv_sems, small_sems, plproj_sems = pairs[:6]
-    q_mirror_sems, kv_mirror_sems, small_mirror_sems, plproj_mirror_sems = pairs[6:]
-    index = lax.axis_index("fsdp")
-    chip, core, sibling, across = neighbours()
-    quarter = 2 * chip + core
-    other_quarter = 2 * (1 - chip) + core
-    place = ring_place(index)
-    ends = ring_ends(place)
-    others = [lax.rem(index + step, HEADS) for step in range(1, HEADS)]
-    greet([{"fsdp": other} for other in others] + [sibling, across])
-    rows = hidden_ref.shape[0]
-    shard = q_ref.shape[0]
-    deep = plproj_ref.shape[0]
-    q_rows = shard // QUARTERS
-    wide = plproj_ref.shape[1] // QUARTERS
-
-    locals_list = []
-    for source, target in (
-        (hidden_ref, hidden_all.at[span(index * rows, rows)]),
-        (gains_ref, gains_all.at[span(index * gains_ref.shape[0], gains_ref.shape[0])]),
-        (
-            q_ref.at[:, span(index * HEAD_DIM, HEAD_DIM)],
-            q_head.at[span(index * shard, shard)],
-        ),
-        (kv_ref, kv_all.at[span(index * shard, shard)]),
-        (small_ref, small_all.at[span(index * shard, shard)]),
-        (plproj_ref, plproj_all.at[span(index * deep, deep)]),
-    ):
-        copy = pltpu.make_async_copy(source, target, local_sems.at[len(locals_list)])
-        copy.start()
-        locals_list.append(copy)
-
-    hidden_part = rows // 4
-    gains_part = gains_ref.shape[0] // 2
-    shard_part = shard // QUARTERS // 2
-    wide_part = wide // 2
-
-    def shard_at(ref, part_of):
-        return lambda owner, lane: ref.at[
-            span(owner * shard + part_of * 2 * shard_part + lane * shard_part, shard_part)
-        ]
-
-    def plproj_at(part_of):
-        return lambda owner, lane: plproj_all.at[
-            span(owner * deep, deep), span(part_of * wide + lane * wide_part, wide_part)
-        ]
-
-    hidden = Ring(
-        place,
-        ends,
-        4,
-        hidden_sems,
-        lambda lane: hidden_ref.at[pl.ds(lane * hidden_part, hidden_part)],
-        lambda owner, lane: hidden_all.at[span(owner * rows + lane * hidden_part, hidden_part)],
-    )
-    gains = Ring(
-        place,
-        ends,
-        2,
-        gains_sems,
-        lambda lane: gains_ref.at[pl.ds(lane * gains_part, gains_part)],
-        lambda owner, lane: gains_all.at[
-            span(owner * gains_ref.shape[0] + lane * gains_part, gains_part)
-        ],
-    )
-
-    def shard_own(ref):
-        return lambda lane: ref.at[
-            span(quarter * 2 * shard_part + lane * shard_part, shard_part)
-        ]
-
-    kv = Ring(place, ends, 2, kv_sems, shard_own(kv_ref), shard_at(kv_all, quarter))
-    small = Ring(place, ends, 2, small_sems, shard_own(small_ref), shard_at(small_all, quarter))
-    plproj = Ring(
-        place,
-        ends,
-        2,
-        plproj_sems,
-        lambda lane: plproj_ref.at[:, span(quarter * wide + lane * wide_part, wide_part)],
-        plproj_at(quarter),
-    )
-    mirrored = [
-        (kv, Mirror(2 * RING_STEPS, kv_mirror_sems), shard_at(kv_all, other_quarter)),
-        (small, Mirror(2 * RING_STEPS, small_mirror_sems), shard_at(small_all, other_quarter)),
-        (plproj, Mirror(2 * RING_STEPS, plproj_mirror_sems), plproj_at(other_quarter)),
-    ]
-    q_mirror = Mirror(HEADS - 1, q_mirror_sems)
-    q_copies = []
-    q_landing = q_head.at[span(index * shard + quarter * q_rows, q_rows)]
-    for step, other in enumerate(others):
-        source = q_ref.at[span(quarter * q_rows, q_rows), span(other * HEAD_DIM, HEAD_DIM)]
-        q_copies.append(remote(source, q_landing, q_sems, step, {"fsdp": other}))
-
-    def q_at(step, part_of):
-        giver = lax.rem(index + HEADS - 1 - step, HEADS)
-        return q_head.at[span(giver * shard + part_of * q_rows, q_rows)]
-
-    def pass_on(step):
-        for ring, mirror, unused_there in mirrored:
-            for lane in range(2):
-                mirror.give((step - 1) * 2 + lane, ring.there(ring.owner(step, lane), lane))
-
-    def pass_again(step):
-        for ring, mirror, there in mirrored:
-            for lane in range(2):
-                mirror.relay((step - 1) * 2 + lane, there(ring.owner(step, lane), lane))
-
-    for step in range(RING_STEPS):
-        gains.send(step)
-        for ring, unused_mirror, unused_there in mirrored:
-            ring.send(step)
-        hidden.send(step)
-        if step >= 1:
-            pass_on(step)
-        if step >= 2:
-            pass_again(step - 1)
-        if step == 4:
-            for number, copy in enumerate(q_copies):
-                copy.wait_recv()
-                q_mirror.give(number, q_at(number, quarter))
-        if step == 5:
-            for number in range(HEADS - 1):
-                q_mirror.relay(number, q_at(number, other_quarter))
-    for ring, unused_mirror, unused_there in mirrored:
-        ring.arrive(RING_STEPS)
-    pass_on(RING_STEPS)
-    pass_again(RING_STEPS - 1)
-    pass_again(RING_STEPS)
-    gains.arrive(RING_STEPS)
-    hidden.arrive(RING_STEPS)
-    for ring, mirror, unused_there in mirrored:
-        ring.sent()
-        mirror.finish()
-    hidden.sent()
-    gains.sent()
-    for copy in q_copies:
-        copy.wait_send()
-    q_mirror.finish()
-    for copy in locals_list:
-        copy.wait()
-
-
-def start_gather(hidden, gains, q_proj, kv, small, pl_proj, number):
-    shard = q_proj.shape[0]
-    arrays = (hidden, gains, q_proj, kv, small, pl_proj)
-
-    def grown(item, rows=None, columns=None):
-        rows = rows or item.shape[0] * HEADS
-        return jax.ShapeDtypeStruct((rows, columns or item.shape[1]), item.dtype)
-
-    counts = [4 * RING_STEPS, 2 * RING_STEPS, RING_STEPS] + [2 * RING_STEPS] * 3
-    counts += [3 * RING_STEPS] + [6 * RING_STEPS] * 3
-    return pl.pallas_call(
-        start_kernel,
-        out_shape=[
-            grown(hidden),
-            grown(gains),
-            grown(q_proj, shard * HEADS, HEAD_DIM),
-            grown(kv),
-            grown(small),
-            grown(pl_proj),
-        ],
-        in_specs=[pl.BlockSpec(memory_space=pl.ANY)] * len(arrays),
-        out_specs=[pl.BlockSpec(memory_space=pl.ANY)] * len(arrays),
-        scratch_shapes=[pltpu.SemaphoreType.DMA((len(arrays),))]
-        + [pltpu.SemaphoreType.DMA((count,)) for count in counts for unused_side in range(2)],
-        compiler_params=pltpu.CompilerParams(collective_id=number, has_side_effects=True),
-    )(*arrays)
+def dot(left, right):
+    return jnp.dot(left, right, preferred_element_type=jnp.float32)
+
+
+def low(value):
+    return value.astype(jnp.bfloat16)
 
 
 def add_low(left, right):
@@ -480,18 +308,59 @@
     return (value * share, slope)
 
 
+def tree_tables_near(segments, count, tables):
+    member, reach, cosine, sine = tables
+    lengths, parents = segments[0:1, :], segments[1:2, :]
+    size = lengths.shape[1]
+    row = lax.broadcasted_iota(jnp.int32, (size, size), 0)
+    column = lax.broadcasted_iota(jnp.int32, (size, size), 1)
+    same = row == column
+
+    def upright(value):
+        return jnp.sum(jnp.where(same, value, 0.0), axis=1, keepdims=True)
+
+    parent = upright(parents) == column.astype(jnp.float32)
+    reached = jnp.where(same | (parent & (row > 0)), 1.0, 0.0)
+    for unused_step in range((count - 1).bit_length()):
+        reached = jnp.where(dot(low(reached), low(reached)) > 0.5, 1.0, 0.0)
+    ends = jnp.sum(jnp.where(row <= column, upright(lengths), 0.0), axis=0, keepdims=True)
+    starts = ends - lengths
+    above = jnp.sum(jnp.where(same, 0.0, reached * lengths), axis=1, keepdims=True)
+    offset = jnp.sum(jnp.where(same, above, 0.0), axis=0, keepdims=True) - starts
+    reached = low(reached)
+    half = cosine.shape[1]
+    place = lax.broadcasted_iota(jnp.int32, (1, half), 1).astype(jnp.float32)
+    freqs = jnp.exp(place * (-math.log(ROPE_BASE) / half))
+
+    def token_tile(number, carry):
+        tile = span(number * size, size)
+        token = (row + number * size).astype(jnp.float32)
+        inside = jnp.where((token >= starts) & (token < ends), 1.0, 0.0)
+        position = jnp.sum(inside * offset, axis=1, keepdims=True) + token[:, :1]
+        angle = position * freqs
+        cosine[tile, :] = jnp.cos(angle)
+        sine[tile, :] = jnp.sin(angle)
+        member[tile, :] = low(inside)
+        reach[tile, :] = low(dot(low(inside), reached))
+        return carry
+
+    lax.fori_loop(0, member.shape[0] // size, token_tile, 0)
+
+
 def attention_kernel(
-    hidden_any,
-    q_any,
-    kv_any,
+    count,
+    hidden_ref,
+    packed_ref,
+    segments_ref,
+    q_ref,
+    kv_ref,
+    small_ref,
+    pl_proj_ref,
     o_any,
-    norm_ref,
+    sum_ref,
     gains_ref,
-    cosine_ref,
-    sine_ref,
-    reach_ref,
-    member_ref,
-    sum_ref,
+    small_all,
+    pl_proj_all,
     normed_any,
     weights_any,
     q_raw_any,
@@ -501,8 +370,8 @@
     v_low_any,
     att_any,
     probs_any,
-    hidden,
-    o_proj,
+    cosine_any,
+    sine_any,
     normed,
     weights,
     q_raw,
@@ -512,56 +381,213 @@
     v_low,
     att,
     probs,
+    cosine,
+    sine,
+    hidden_all,
+    kv_all,
+    gains_all,
+    o_proj,
+    member,
+    reach,
     part,
     held,
     load_sems,
     store_sems,
-    send_sem,
-    recv_sem,
+    *sems,
 ):
-    rows, width = sum_ref.shape
+    pairs = [sems[i : i + 2] for i in range(0, len(sems), 2)]
+    hidden_sems, gains_sems, q_sems, kv_sems, small_sems, pl_proj_sems, sum_sems = pairs[:7]
+    q_mirror_sems, kv_mirror_sems, small_mirror_sems, pl_proj_mirror_sems = pairs[7:]
+    rows, width = hidden_ref.shape
     total_rows = rows * HEADS
     half = rows // 2
+    piece = rows // 4
+    shard = q_ref.shape[0]
+    deep = pl_proj_ref.shape[0]
+    q_rows = shard // QUARTERS
+    shard_part = q_rows // 2
+    wide = pl_proj_ref.shape[1] // QUARTERS
+    wide_part = wide // 2
     index = lax.axis_index("fsdp")
+    chip, core, sibling, across = neighbours()
+    quarter, other_quarter = 2 * chip + core, 2 * (1 - chip) + core
     place = ring_place(index)
     ends = ring_ends(place)
-    key_at = (index // (HEADS // KV_HEADS)) * HEAD_DIM
+    others = [lax.rem(index + step, HEADS) for step in range(1, HEADS)]
+    own_shard = span(index * shard, shard)
     loads = start_loads(
         (
-            (q_any, weights.at[:, pl.ds(0, HEAD_DIM)]),
-            (kv_any.at[:, span(key_at, HEAD_DIM)], weights.at[:, pl.ds(HEAD_DIM, HEAD_DIM)]),
-            (
-                kv_any.at[:, span(key_at + KV_HEADS * HEAD_DIM, HEAD_DIM)],
-                weights.at[:, pl.ds(2 * HEAD_DIM, HEAD_DIM)],
-            ),
-            (hidden_any, hidden),
+            (q_ref.at[:, span(index * HEAD_DIM, HEAD_DIM)], weights.at[own_shard, pl.ds(0, HEAD_DIM)]),
+            (kv_ref, kv_all.at[own_shard]),
             (o_any, o_proj),
+            (small_ref, small_all.at[own_shard]),
+            (pl_proj_ref, pl_proj_all.at[span(index * deep, deep)]),
         ),
         load_sems,
     )
-    greet(ends)
-    for copy in loads:
-        copy.wait()
-
-    def project(tile):
-        source = hidden[tile, :].astype(jnp.float32)
-        value = low(source * root_of(source) * norm_ref[...])
-        normed[tile, :] = value
+    greet([{"fsdp": other} for other in others] + [sibling, across])
+    gain_copies = [
+        remote(packed_ref, gains_all.at[index], gains_sems, step, {"fsdp": other})
+        for step, other in enumerate(others)
+    ]
+
+    def shard_at(ref, part_of):
+        return lambda owner, lane: ref.at[
+            span(owner * shard + part_of * q_rows + lane * shard_part, shard_part)
+        ]
+
+    def pl_proj_at(part_of):
+        return lambda owner, lane: pl_proj_all.at[
+            span(owner * deep, deep), span(part_of * wide + lane * wide_part, wide_part)
+        ]
+
+    def shard_own(ref):
+        return lambda lane: ref.at[span(quarter * q_rows + lane * shard_part, shard_part)]
+
+    hidden = Ring(
+        place,
+        ends,
+        4,
+        hidden_sems,
+        lambda lane: hidden_ref.at[pl.ds(lane_offset(lane, rows), piece)],
+        lambda owner, lane: hidden_all.at[span(owner * rows + lane_offset(lane, rows), piece)],
+    )
+    kv = Ring(place, ends, 2, kv_sems, shard_own(kv_ref), shard_at(kv_all, quarter))
+    small = Ring(place, ends, 2, small_sems, shard_own(small_ref), shard_at(small_all, quarter))
+    pl_proj = Ring(
+        place,
+        ends,
+        2,
+        pl_proj_sems,
+        lambda lane: pl_proj_ref.at[:, span(quarter * wide + lane * wide_part, wide_part)],
+        pl_proj_at(quarter),
+    )
+    lanes = 2 * RING_STEPS
+    kv_mirror = Mirror(lanes, kv_mirror_sems)
+    q_mirror = Mirror(HEADS - 1, q_mirror_sems)
+    late = (
+        (small, Mirror(lanes, small_mirror_sems), shard_at(small_all, other_quarter)),
+        (pl_proj, Mirror(lanes, pl_proj_mirror_sems), pl_proj_at(other_quarter)),
+    )
+    kv_other = shard_at(kv_all, other_quarter)
+
+    def pass_on(ring, mirror, step):
+        for lane in range(2):
+            mirror.give((step - 1) * 2 + lane, ring.there(ring.owner(step, lane), lane))
+
+    def pass_again(ring, mirror, there, step):
+        for lane in range(2):
+            mirror.relay((step - 1) * 2 + lane, there(ring.owner(step, lane), lane))
+
+    def late_step(step):
+        for ring, mirror, there in late:
+            if step < RING_STEPS:
+                ring.send(step)
+            elif step == RING_STEPS:
+                ring.arrive(step)
+            if 1 <= step <= RING_STEPS:
+                pass_on(ring, mirror, step)
+            if step >= 2:
+                pass_again(ring, mirror, there, step - 1)
+
+    def q_at(step, part_of):
+        giver = lax.rem(index + HEADS - 1 - step, HEADS)
+        return weights.at[span(giver * shard + part_of * q_rows, q_rows), pl.ds(0, HEAD_DIM)]
+
+    kv.send(0)
+    q_landing = weights.at[span(index * shard + quarter * q_rows, q_rows), pl.ds(0, HEAD_DIM)]
+    q_copies = [
+        remote(
+            q_ref.at[span(quarter * q_rows, q_rows), span(other * HEAD_DIM, HEAD_DIM)],
+            q_landing,
+            q_sems,
+            step,
+            {"fsdp": other},
+        )
+        for step, other in enumerate(others)
+    ]
+    hidden.send(0)
+    hidden_all[span(index * rows, rows), :] = hidden_ref[...]
+    gains_all[index] = packed_ref[...]
+    tree_tables_near(segments_ref, count, (member, reach, cosine, sine))
+
+    def project(step):
+        pair = Pair(place, step, rows)
+        source = pair.read(hidden_all).astype(jnp.float32)
+        value = low(source * root_of(source) * gains_ref[0:1, :])
+        pair.write(normed, slice(None), value)
         raw = dot(value, weights[...])
-        cosine, sine = cosine_ref[tile, :], sine_ref[tile, :]
+        cos_rows, sin_rows = pair.read(cosine), pair.read(sine)
         for side, (raw_ref, low_ref) in enumerate(((q_raw, q_low), (k_raw, k_low))):
             item = raw[:, side * HEAD_DIM : (side + 1) * HEAD_DIM]
-            raw_ref[tile, :] = item
-            item = item * root_of(item) * gains_ref[side : side + 1, :]
+            pair.write(raw_ref, slice(None), item)
+            item = item * root_of(item) * gains_ref[6 + side : 7 + side, :HEAD_DIM]
             first, second = item[:, : HEAD_DIM // 2], item[:, HEAD_DIM // 2 :]
-            low_ref[tile, :] = low(
-                jnp.concatenate(
-                    [first * cosine - second * sine, second * cosine + first * sine], axis=1
-                )
+            turned = jnp.concatenate(
+                [first * cos_rows - second * sin_rows, second * cos_rows + first * sin_rows],
+                axis=1,
             )
-        v_low[tile, :] = low(raw[:, 2 * HEAD_DIM :])
-
-    tile_loop(total_rows // 128, 128, project)
+            pair.write(low_ref, slice(None), low(turned))
+        pair.write(v_low, slice(None), low(raw[:, 2 * HEAD_DIM :]))
+
+    for step in range(1, RING_STEPS):
+        if step <= 3:
+            for kv_step in (2 * step - 1, 2 * step):
+                kv.send(kv_step)
+                pass_on(kv, kv_mirror, kv_step)
+        hidden.send(step)
+        if step in (2, 3):
+            for kv_step in (2 * step - 3, 2 * step - 2):
+                pass_again(kv, kv_mirror, kv_other, kv_step)
+        if step == 2:
+            for number, copy in enumerate(q_copies):
+                copy.wait_recv()
+                q_mirror.give(number, q_at(number, quarter))
+        if step == 3:
+            for number in range(HEADS - 1):
+                q_mirror.relay(number, q_at(number, other_quarter))
+        if step == 4:
+            kv.arrive(RING_STEPS)
+            pass_on(kv, kv_mirror, RING_STEPS)
+            for kv_step in (5, 6, 7):
+                pass_again(kv, kv_mirror, kv_other, kv_step)
+            for copy in gain_copies:
+                copy.wait_recv()
+            for owner in range(HEADS):
+                gains_ref[:, owner * shard : (owner + 1) * shard] = gains_all[owner]
+            total = gains_all[0, 6:, :]
+            for owner in range(1, HEADS):
+                total = total + gains_all[owner, 6:, :]
+            gains_ref[6:, :shard] = total
+        if step == 5:
+            late_step(0)
+            kv_mirror.arrive()
+            q_mirror.arrive()
+            loads[0].wait()
+            loads[1].wait()
+            key_at = (index // (HEADS // KV_HEADS)) * HEAD_DIM
+            turns = start_loads(
+                [
+                    (
+                        kv_all.at[:, span(key_at + side * KV_HEADS * HEAD_DIM, HEAD_DIM)],
+                        weights.at[:, pl.ds((1 + side) * HEAD_DIM, HEAD_DIM)],
+                    )
+                    for side in range(2)
+                ],
+                load_sems.at[pl.ds(5, 2)],
+            )
+            for copy in turns:
+                copy.wait()
+            for number in range(3):
+                project(number)
+        if step == 6:
+            late_step(1)
+            for number in range(3, 6):
+                project(number)
+    late_step(2)
+    project(6)
+    hidden.arrive(RING_STEPS)
+    project(7)
     stores = start_loads(
         (
             (normed, normed_any),
@@ -571,9 +597,12 @@
             (q_low, q_low_any),
             (k_low, k_low_any),
             (v_low, v_low_any),
+            (cosine, cosine_any),
+            (sine, sine_any),
         ),
         store_sems,
     )
+    loads[2].wait()
     scale = HEAD_DIM ** (-0.5)
 
     def attend(first_owner, second_owner):
@@ -587,7 +616,7 @@
         query = jnp.concatenate([query + start for start in starts], axis=0)
         key = lax.broadcasted_iota(jnp.int32, (rows, total_rows), 1)
         scores = mul_t(read(q_low), k_low[...]) * scale
-        seen = (mul_t(read(reach_ref), member_ref[...]) > 0.5) & (key <= query)
+        seen = (mul_t(read(reach), member[...]) > 0.5) & (key <= query)
         scores = jnp.where(seen, scores, MASKED)
         expo = jnp.exp(scores - jnp.max(scores, axis=1, keepdims=True))
         chance = low(expo / jnp.sum(expo, axis=1, keepdims=True))
@@ -597,12 +626,11 @@
             att[rows_of, :] = mixed[side * half : (side + 1) * half]
         part[...] = dot(mixed, o_proj[...])
 
-    piece = rows // 4
     sums = RingSum(
         place,
         ends,
         4,
-        (send_sem, recv_sem),
+        sum_sems,
         held,
         lambda owner, lane: part[pl.ds(lane_offset(lane, rows), piece), :],
     )
@@ -612,22 +640,31 @@
             ring_index(lax.rem(place + step + 1, HEADS)),
         )
         sums.send(step)
+        if step + 3 <= HEADS:
+            late_step(step + 3)
     attend(index, index)
-    stores += start_loads(((att, att_any), (probs, probs_any)), store_sems.at[pl.ds(7, 2)])
+    stores += start_loads(((att, att_any), (probs, probs_any)), store_sems.at[pl.ds(9, 2)])
     for lane in range(4):
         sum_ref[pl.ds(lane_offset(lane, rows), piece), :] = sums.last(index, lane)
-    sums.sent()
-    for copy in stores:
+    for item in (hidden, kv, small, pl_proj, sums, kv_mirror, q_mirror):
+        item.sent()
+    for unused_ring, mirror, unused_there in late:
+        mirror.finish()
+    for copy in q_copies + gain_copies:
+        copy.wait_send()
+    for copy in loads[3:] + stores:
         copy.wait()
 
 
-def attention_forward(hidden, q_head, kv_all, o_proj, norm, gains, cosine, sine, reach, member, number):
-    total, width = hidden.shape
-    rows = total // HEADS
+def attention_forward(hidden, packed, segments, count, q_proj, kv, small, pl_proj, o_proj, number):
+    rows, width = hidden.shape
+    total = rows * HEADS
+    shard = q_proj.shape[0]
     steps = 4 * RING_STEPS
     near, anywhere = pl.BlockSpec(memory_space=pltpu.VMEM), pl.BlockSpec(memory_space=pl.ANY)
     bf16, f32 = jnp.bfloat16, jnp.float32
     head = (total, HEAD_DIM)
+    table = (total, HEAD_DIM // 2)
     kept = [
         ((total, width), bf16),
         ((width, 3 * HEAD_DIM), bf16),
@@ -638,27 +675,40 @@
         (head, bf16),
         (head, bf16),
         ((total, total), bf16),
+        (table, f32),
+        (table, f32),
     ]
+    grown = [((shard * HEADS, small.shape[1]), bf16), ((pl_proj.shape[0] * HEADS, width), bf16)]
+    low_steps = 2 * RING_STEPS
+    counts = [steps, HEADS - 1, HEADS - 1] + [low_steps] * 3 + [steps]
+    counts += [3 * (HEADS - 1)] + [3 * low_steps] * 3
     return pl.pallas_call(
-        attention_kernel,
-        out_shape=[jax.ShapeDtypeStruct((rows, width), f32)]
-        + [jax.ShapeDtypeStruct(shape, dtype) for shape, dtype in kept],
-        in_specs=[anywhere] * 4 + [near] * 6,
-        out_specs=[near] + [anywhere] * len(kept),
-        scratch_shapes=[pltpu.VMEM((total, width), bf16), pltpu.VMEM(o_proj.shape, bf16)]
-        + [pltpu.VMEM(shape, dtype) for shape, dtype in kept]
+        functools.partial(attention_kernel, count),
+        out_shape=[
+            jax.ShapeDtypeStruct((rows, width), f32),
+            jax.ShapeDtypeStruct((8, width), f32),
+        ]
+        + [jax.ShapeDtypeStruct(shape, dtype) for shape, dtype in grown + kept],
+        in_specs=[near] * 3 + [anywhere] * 5,
+        out_specs=[near] * 2 + [anywhere] * (len(grown) + len(kept)),
+        scratch_shapes=[pltpu.VMEM(shape, dtype) for shape, dtype in kept]
         + [
+            pltpu.VMEM((total, width), bf16),
+            pltpu.VMEM((width, kv.shape[1]), bf16),
+            pltpu.VMEM((HEADS,) + packed.shape, f32),
+            pltpu.VMEM(o_proj.shape, bf16),
+            pltpu.VMEM((total, segments.shape[1]), bf16),
+            pltpu.VMEM((total, segments.shape[1]), bf16),
             pltpu.VMEM((rows, width), f32),
             pltpu.VMEM((steps + 4, rows // 4, width), bf16),
-            pltpu.SemaphoreType.DMA((5,)),
-            pltpu.SemaphoreType.DMA((9,)),
-            pltpu.SemaphoreType.DMA((steps,)),
-            pltpu.SemaphoreType.DMA((steps,)),
-        ],
+            pltpu.SemaphoreType.DMA((7,)),
+            pltpu.SemaphoreType.DMA((11,)),
+        ]
+        + [pltpu.SemaphoreType.DMA((item,)) for item in counts for unused_side in range(2)],
         compiler_params=pltpu.CompilerParams(
             collective_id=number, has_side_effects=True, vmem_limit_bytes=VMEM_BYTES
         ),
-    )(hidden, q_head, kv_all, o_proj, norm, gains, cosine, sine, reach, member)
+    )(hidden, packed, segments, q_proj, kv, small, pl_proj, o_proj)
 
 
 def ffn_kernel(
@@ -1181,7 +1231,15 @@
 
 
 def attention_back_kernel(
-    own_ref,
+    hidden_ref,
+    first_ref,
+    d_ffwin_ref,
+    d_second_ref,
+    branch_ref,
+    low_rank_ref,
+    left_low_ref,
+    gains_ref,
+    ffw_gains_ref,
     o_any,
     q_any,
     k_any,
@@ -1194,19 +1252,18 @@
     k_raw_any,
     cosine_any,
     sine_any,
-    laurel_any,
-    gains_ref,
+    small_any,
     pl_gate_ref,
     pl_proj_ref,
     own_down,
     far_down,
     own_gate,
     own_up,
-    sum_ref,
+    source_ref,
     owned_ref,
     early_ref,
     pl_proj_all,
-    gain_grads,
+    gain_sums,
     total_down,
     total_gate,
     total_up,
@@ -1246,13 +1303,23 @@
     o_far,
     sum_own,
     sum_far,
+    own_ref,
+    laurel,
+    d_low_rank,
+    d_scaled,
+    sum_ref,
+    gain_rows,
+    gain_parts,
+    gain_landed,
+    gain_totals,
     load_sems,
     final_sems,
     *sems,
 ):
     pairs = [sems[i : i + 2] for i in range(0, len(sems), 2)]
     ring_sems, sum_sems, fold_sems, far_sems, swap_sems, key_sems = pairs[:6]
-    mirror_sems, early_sems, o_fold_sems, o_far_sems, cross_sems, total_sems, proj_sems = pairs[6:]
+    mirror_sems, early_sems, o_fold_sems, o_far_sems, cross_sems, total_sems, proj_sems = pairs[6:13]
+    gain_sems, twin_sems = pairs[13:]
     rows, width = own_ref.shape
     total_rows = rows * HEADS
     half = rows // 2
@@ -1283,11 +1350,13 @@
             (sine_any, sine),
             (weights_any, weights),
             (normed_any, normed),
-            (laurel_any, blocks.at[:, :, :, pl.ds(head_columns, laurel_any.shape[3])]),
+            (small_any.at[:, span(small_any.shape[1] - laurel.shape[1], laurel.shape[1])], laurel),
         ),
         load_sems,
     )
-    greet([{"fsdp": other} for other in others] + [sibling, across])
+    rep = lax.axis_index("rep")
+    twins = [lax.rem(rep + step, QUARTERS) for step in range(1, QUARTERS)]
+    greet([{"fsdp": other} for other in others] + [{"rep": twin} for twin in twins])
     early_rows = far_up.shape[0] // 4
     late_rows = far_up.shape[0] - early_rows
     crossings = [
@@ -1313,6 +1382,48 @@
         lambda owner, lane: part[pl.ds(lane_offset(lane, rows), piece), :],
     )
     key_tiles = total_rows // TILE
+    rank = laurel.shape[1] // 2
+
+    def before(tile):
+        grad, part_sum = norm_pull(first_ref[tile, :], gains_ref[3:4, :], d_ffwin_ref[tile, :])
+        gain_rows[3:4, :] += part_sum
+        scaled = (d_second_ref[tile, :] + grad) * HALF_ROOT
+        d_scaled[tile, :] = scaled
+        grad, part_sum = norm_pull(branch_ref[tile, :], gains_ref[1:2, :], scaled)
+        gain_rows[1:2, :] += part_sum
+        own_ref[tile, :] = low(grad)
+        grad, part_sum = norm_pull(low_rank_ref[tile, :], gains_ref[2:3, :], scaled)
+        gain_rows[2:3, :] += part_sum
+        d_low_rank[tile, :] = low(grad)
+
+    def low_rank_grads():
+        d_left = low(dot(d_low_rank[...], laurel[...])[:, rank:])
+        source = hidden_ref[...].astype(jnp.float32)
+        block[...] = low(source * root_of(source) * gains_ref[0:1, :])
+        shard = width // HEADS
+        for owner in range(HEADS):
+            columns = slice(owner * shard, (owner + 1) * shard)
+            value = jnp.concatenate(
+                [
+                    dot(block[:, columns].T, d_left),
+                    dot(d_low_rank[:, columns].T, left_low_ref[...]),
+                ],
+                axis=1,
+            )
+            value = low(value)
+            for step in range(QUARTERS):
+                blocks[owner, step, :, head_columns:] = value[
+                    step * quarter_rows : (step + 1) * quarter_rows
+                ]
+        return d_left
+
+    def after(tile):
+        grad = d_scaled[tile, :] + sum_ref[tile, :]
+        grad, part_sum = norm_pull(
+            hidden_ref[tile, :].astype(jnp.float32), gains_ref[0:1, :], grad
+        )
+        gain_rows[0:1, :] += part_sum
+        source_ref[tile, :] = low(d_scaled[tile, :] + grad)
 
     def compute(step):
         pair = Pair(place, step, rows)
@@ -1369,9 +1480,12 @@
 
     d_k[...] = jnp.zeros_like(d_k)
     d_v[...] = jnp.zeros_like(d_v)
-    gain_grads[...] = jnp.zeros_like(gain_grads)
+    gain_rows[...] = jnp.zeros_like(gain_rows)
+    tile_loop(rows // 32, 32, before)
     ring.send(0)
     d_all[span(index * rows, rows), :] = own_ref[...]
+    loads[12].wait()
+    d_left = low_rank_grads()
     for copy in loads[:6]:
         copy.wait()
     compute(0)
@@ -1385,7 +1499,7 @@
             load_final(0)
         if step == 4:
             add_final(0)
-    for copy in loads[6:]:
+    for copy in loads[6:12]:
         copy.wait()
 
     def raw_tile(tile):
@@ -1393,12 +1507,12 @@
             value, gain_grad = head_back(
                 grad[tile, :],
                 raw[tile, :],
-                gains_ref[side : side + 1, :],
+                gains_ref[6 + side : 7 + side, :HEAD_DIM],
                 cosine[tile, :],
                 sine[tile, :],
             )
             d_qkv[tile, side * HEAD_DIM : (side + 1) * HEAD_DIM] = low(value)
-            gain_grads[side : side + 1, :] += gain_grad
+            gain_rows[6 + side : 7 + side, :HEAD_DIM] += gain_grad
         d_qkv[tile, 2 * HEAD_DIM :] = low(d_v[tile, :])
 
     tile_loop(total_rows // 128, 128, raw_tile)
@@ -1541,17 +1655,47 @@
     base = q_columns + 2 * KV_HEADS * HEAD_DIM
     owned_ref[own_rows, pl.ds(base, rest - 2 * HEAD_DIM)] = low(extra)
     mirror.give(0, owned_ref.at[own_rows])
+    sum_ref[...] += mul_t(d_left, laurel[:, :rank])
+    tile_loop(rows // 32, 32, after)
+    gain_rows[4:6, :] = ffw_gains_ref[...]
+    shard = width // HEADS
+    for owner in range(HEADS):
+        gain_parts[owner, :6] = gain_rows[:6, owner * shard : (owner + 1) * shard]
+        gain_parts[owner, 6:] = gain_rows[6:, :HEAD_DIM]
+    gain_sends = [
+        remote(gain_parts.at[other], gain_landed.at[index], gain_sems, step, {"fsdp": other})
+        for step, other in enumerate(others)
+    ]
+    gain_landed[index] = gain_parts[index]
+    for copy in gain_sends:
+        copy.wait_recv()
+    total = gain_landed[0]
+    for step in range(1, HEADS):
+        total = total + gain_landed[step]
+    gain_totals[rep] = total
+    twin_sends = [
+        remote(gain_totals.at[rep], gain_totals.at[rep], twin_sems, step, {"rep": twin})
+        for step, twin in enumerate(twins)
+    ]
     crossings[1].wait_recv()
     crossings[2].wait_recv()
     load_final(2)
     mirror.relay(0, owned_ref.at[other_rows])
+    for copy in twin_sends:
+        copy.wait_recv()
+    total = gain_totals[0]
+    for step in range(1, QUARTERS):
+        total = total + gain_totals[step]
+    gain_sums[...] = total
     add_final(2)
     mirror.finish()
     early.finish()
     pl_mirror.finish()
     ring.sent()
     sums.sent()
-    for copy in folds + o_folds + across_sends + swaps + key_swaps + crossings:
+    for copy in (
+        folds + o_folds + across_sends + swaps + key_swaps + crossings + gain_sends + twin_sends
+    ):
         copy.wait_send()
     final_sends[2].wait_send()
     final_stores[2].wait()
@@ -1559,38 +1703,39 @@
         copy.wait_recv()
 
 
-def attention_back(own, arrays, laurel, gains, pl_sums, chip_grads, far_down, number):
-    rows, width = own.shape
+def attention_back(local, arrays, small, pl_sums, chip_grads, far_down, number):
+    rows, width = local[0].shape
     total = rows * HEADS
     shard = width // HEADS
     quarter = shard // QUARTERS
     steps = 4 * RING_STEPS
-    columns = 3 * HEAD_DIM + laurel.shape[1]
-    laurel = laurel.reshape(HEADS, QUARTERS, quarter, -1)
+    pl_gate, pl_proj = pl_sums
+    laurel = 2 * local[6].shape[1]
+    columns = 3 * HEAD_DIM + laurel
     half = chip_grads[0].shape
     near, anywhere = pl.BlockSpec(memory_space=pltpu.VMEM), pl.BlockSpec(memory_space=pl.ANY)
     bf16, f32 = jnp.bfloat16, jnp.float32
-    owned = (HEADS + 2 * KV_HEADS) * HEAD_DIM + laurel.shape[3]
+    owned = (HEADS + 2 * KV_HEADS) * HEAD_DIM + laurel
     counts = [steps, steps, 2, 1, HEADS - 1, HEADS - 1, 3, 3, 2, 1, 3, 3, 3]
-    pl_gate, pl_proj = pl_sums
+    counts += [HEADS - 1, QUARTERS - 1]
     down, gate, up = chip_grads
     whole = jax.ShapeDtypeStruct((2 * half[0], half[1]), bf16)
     part = jax.ShapeDtypeStruct(half, bf16)
     return pl.pallas_call(
         attention_back_kernel,
         out_shape=[
-            jax.ShapeDtypeStruct((rows, width), f32),
+            jax.ShapeDtypeStruct((rows, width), bf16),
             jax.ShapeDtypeStruct((shard, owned), bf16),
             jax.ShapeDtypeStruct((shard, width + pl_gate.shape[1]), bf16),
             jax.ShapeDtypeStruct((pl_proj.shape[0], width), bf16),
-            jax.ShapeDtypeStruct(gains.shape, f32),
+            jax.ShapeDtypeStruct((8, shard), f32),
             whole,
             whole,
             whole,
             part,
             part,
         ],
-        in_specs=[near] + [anywhere] * (len(arrays) + 1) + [near] * 3 + [anywhere] * 4,
+        in_specs=[near] * len(local) + [anywhere] * (len(arrays) + 1) + [near] * 2 + [anywhere] * 4,
         out_specs=[near] * 5 + [anywhere] * 5,
         scratch_shapes=[pltpu.VMEM(item.shape, item.dtype) for item in arrays]
         + [
@@ -1616,89 +1761,23 @@
             pltpu.VMEM((quarter, width), bf16),
             pltpu.VMEM(half, bf16),
             pltpu.VMEM(half, bf16),
+            pltpu.VMEM((rows, width), bf16),
+            pltpu.VMEM((width, laurel), bf16),
+            pltpu.VMEM((rows, width), bf16),
+            pltpu.VMEM((rows, width), f32),
+            pltpu.VMEM((rows, width), f32),
+            pltpu.VMEM((8, width), f32),
+            pltpu.VMEM((HEADS, 8, shard), f32),
+            pltpu.VMEM((HEADS, 8, shard), f32),
+            pltpu.VMEM((QUARTERS, 8, shard), f32),
             pltpu.SemaphoreType.DMA((len(arrays) + 1,)),
             pltpu.SemaphoreType.DMA((3,)),
         ]
         + [pltpu.SemaphoreType.DMA((count,)) for count in counts for unused_side in range(2)],
         compiler_params=pltpu.CompilerParams(
-            collective_id=number, has_side_effects=True, vmem_limit_bytes=56 << 20
+            collective_id=number, has_side_effects=True, vmem_limit_bytes=58 << 20
         ),
-    )(own, *arrays, laurel, gains, pl_gate, pl_proj, down, far_down, gate, up)
-
-
-def gains_kernel(parts_ref, sum_ref, landed, totals, send_sem, recv_sem, rep_send, rep_recv):
-    index = lax.axis_index("fsdp")
-    rep = lax.axis_index("rep")
-    others = [lax.rem(index + step, HEADS) for step in range(1, HEADS)]
-    twins = [lax.rem(rep + step, QUARTERS) for step in range(1, QUARTERS)]
-    greet([{"fsdp": other} for other in others] + [{"rep": twin} for twin in twins])
-    sends = [
-        remote(parts_ref.at[other], landed.at[index], (send_sem, recv_sem), step, {"fsdp": other})
-        for step, other in enumerate(others)
-    ]
-    landed[index] = parts_ref[index]
-    for copy in sends:
-        copy.wait_recv()
-    total = landed[0]
-    for step in range(1, HEADS):
-        total = total + landed[step]
-    totals[rep] = total
-    twin_sends = [
-        remote(totals.at[rep], totals.at[rep], (rep_send, rep_recv), step, {"rep": twin})
-        for step, twin in enumerate(twins)
-    ]
-    for copy in twin_sends:
-        copy.wait_recv()
-    total = totals[0]
-    for step in range(1, QUARTERS):
-        total = total + totals[step]
-    sum_ref[...] = total
-    for copy in sends + twin_sends:
-        copy.wait_send()
-
-
-def gains_sum(parts, number):
-    near = pl.BlockSpec(memory_space=pltpu.VMEM)
-    return pl.pallas_call(
-        gains_kernel,
-        out_shape=jax.ShapeDtypeStruct(parts.shape[1:], parts.dtype),
-        in_specs=[near],
-        out_specs=near,
-        scratch_shapes=[
-            pltpu.VMEM(parts.shape, parts.dtype),
-            pltpu.VMEM((QUARTERS,) + parts.shape[1:], parts.dtype),
-        ]
-        + [pltpu.SemaphoreType.DMA((HEADS - 1,))] * 2
-        + [pltpu.SemaphoreType.DMA((QUARTERS - 1,))] * 2,
-        compiler_params=pltpu.CompilerParams(collective_id=number, has_side_effects=True),
-    )(parts)
-
-
-def dot(left, right):
-    return jnp.dot(left, right, preferred_element_type=jnp.float32)
-
-
-def low(value):
-    return value.astype(jnp.bfloat16)
-
-
-def tree_places(lengths, parents, total):
-    count = lengths.shape[0]
-    labels = jnp.arange(count, dtype=jnp.int32)
-    ends = jnp.sum(jnp.where(labels[:, None] <= labels[None, :], lengths[:, None], 0), axis=0)
-    starts = ends - lengths
-    tokens = jnp.arange(total, dtype=jnp.int32)
-    segment = jnp.sum((ends[None, :] <= tokens[:, None]).astype(jnp.int32), axis=1)
-    parent_hot = (parents[:, None] == labels[None, :]) & (labels[:, None] > 0)
-    identity = labels[:, None] == labels[None, :]
-    reached = parent_hot | identity
-    for unused_step in range((count - 1).bit_length()):
-        reached = jnp.any(reached[:, :, None] & reached[None, :, :], axis=1)
-    offset = jnp.sum(jnp.where(reached & ~identity, lengths[None, :], 0), axis=1) - starts
-    member = segment[:, None] == labels[None, :]
-    reach = jnp.any(member[:, :, None] & reached[None, :, :], axis=1)
-    position = jnp.sum(jnp.where(member, offset[None, :], 0), axis=1) + tokens
-    return (tokens, member.astype(jnp.bfloat16), reach.astype(jnp.bfloat16), position)
+    )(*local, *arrays, small, pl_gate, pl_proj, down, far_down, gate, up)
 
 
 def head_plan(
@@ -1734,45 +1813,18 @@
     rank = laurel_left.shape[1]
     per_layer = pl_gate.shape[1]
 
+    piece = HEAD_DIM // HEADS
     gains = (attn_norm, attn_post_norm, laurel_norm, ffw_norm, ffw_post_norm, pl_post_norm)
-    packed = jnp.concatenate(gains + (q_norm, k_norm))
-    pad = -packed.shape[0] % (32 * 128)
-    packed = jnp.pad(packed, (0, pad)).reshape(-1, 128)
-    hidden_all, gains_held, q_head, kv_all, small_all, full_plproj = start_gather(
-        hidden_in,
-        packed,
-        q_proj,
-        jnp.concatenate([k_proj, v_proj], axis=1),
-        jnp.concatenate([pl_gate, laurel_left, laurel_right], axis=1),
-        pl_proj,
-        0,
-    )
-    all_gains = gains_held.reshape(HEADS, -1).astype(jnp.float32)
-    wide_gains = [all_gains[:, i * shard : (i + 1) * shard].reshape(-1) for i in range(len(gains))]
-    gain_anorm, gain_apost, gain_lnorm, gain_fnorm, gain_fpost, gain_plpost = wide_gains
-    at = len(gains) * shard
-    piece = HEAD_DIM // HEADS
-    gain_qnorm = all_gains[:, at : at + piece].reshape(-1)
-    gain_knorm = all_gains[:, at + piece : at + 2 * piece].reshape(-1)
-
-    full_left = small_all[:, per_layer : per_layer + rank]
-    full_right = small_all[:, per_layer + rank :]
-
-    tokens, member, reach, position = tree_places(seg_lengths[0], seg_parents[0], total)
-    depth = position.astype(jnp.float32)
-    half = HEAD_DIM // 2
-    freqs = jnp.exp(
-        jnp.arange(half, dtype=jnp.float32) * (-2.0 * math.log(ROPE_BASE) / HEAD_DIM)
-    )
-    angle = depth[:, None] * freqs[None, :]
-    cosine, sine = jnp.cos(angle), jnp.sin(angle)
-
-    def padded(item):
-        return jnp.pad(item, ((0, 0), (0, 128 - item.shape[1])))
-
-    head_gain = jnp.stack([gain_qnorm, gain_knorm])
+    lanes = jnp.arange(HEAD_DIM, dtype=jnp.int32) // piece == index
+    gains += tuple(jnp.where(lanes, jnp.tile(item, HEADS), 0) for item in (q_norm, k_norm))
+    packed = jnp.concatenate([item.astype(jnp.float32) for item in gains]).reshape(8, shard)
+    segments = jnp.stack([seg_lengths[0], seg_parents[0]]).astype(jnp.float32)
+    segments = jnp.pad(segments, ((0, 6), (0, 128 - segments.shape[1])))
     (
         branch,
+        wide_gains,
+        small_all,
+        full_plproj,
         normed_all,
         qkv_head,
         q_raw,
@@ -1782,19 +1834,23 @@
         v_low,
         attended_low,
         probs_low,
-    ) = attention_forward(
-        hidden_all,
-        q_head,
-        kv_all,
-        o_proj,
-        gain_anorm[None, :],
-        head_gain,
         cosine,
         sine,
-        padded(reach),
-        padded(member),
-        6,
-    )
+    ) = attention_forward(
+        hidden_in,
+        packed,
+        segments,
+        seg_lengths.shape[1],
+        q_proj,
+        jnp.concatenate([k_proj, v_proj], axis=1),
+        jnp.concatenate([pl_gate, laurel_left, laurel_right], axis=1),
+        pl_proj,
+        o_proj,
+        0,
+    )
+    gain_anorm, gain_apost, gain_lnorm, gain_fnorm = wide_gains[:4]
+    full_left = small_all[:, per_layer : per_layer + rank]
+    full_right = small_all[:, per_layer + rank :]
 
     source = hidden_in.astype(jnp.float32)
     normed = norm_rows(source, gain_anorm)
@@ -1811,27 +1867,27 @@
     )
     d_ffwin, result, d_extra, d_second, ffw_gains, *rest = ffn_back(
         (first_sum, ffw_out, layer_input, out_grad),
-        jnp.stack([gain_fpost, gain_plpost]),
+        wide_gains[4:6],
         small_all,
         full_plproj,
         (ffw_all, act, slope, inner_low),
         (gate_proj, up_proj, down_proj),
         9,
     )
-    grad_fpost, grad_plpost = ffw_gains
     chip_grads, far_down, pl_sums = rest[:3], rest[3], rest[5:]
 
-    d_first_part, grad_fnorm = norm_back(first_sum, gain_fnorm, d_ffwin)
-    d_scaled = (d_second + d_first_part) * HALF_ROOT
-    d_branch, grad_apost = norm_back(branch, gain_apost, d_scaled)
-    d_lowrank, grad_lnorm = norm_back(low_rank, gain_lnorm, d_scaled)
-    d_lowrank_low = low(d_lowrank)
-    grad_right = outer(d_lowrank_low, left_low)
-    d_left_low = low(dot(d_lowrank_low, full_right))
-    grad_left = outer(normed_low, d_left_low)
-
-    d_normed_sum, owned, early, sum_plproj, head_gains, *totals = attention_back(
-        low(d_branch),
+    d_source, owned, early, sum_plproj, gain_sums, *totals = attention_back(
+        (
+            hidden_in,
+            first_sum,
+            d_ffwin,
+            d_second,
+            branch,
+            low_rank,
+            left_low,
+            wide_gains,
+            ffw_gains,
+        ),
         (
             o_proj,
             q_low,
@@ -1846,55 +1902,45 @@
             cosine,
             sine,
         ),
-        low(jnp.concatenate([grad_left, grad_right], axis=1)),
-        head_gain,
+        small_all,
         pl_sums,
         chip_grads,
         far_down,
         12,
     )
-    grad_qnorm, grad_knorm = head_gains
     sum_down, sum_gate, sum_up = [item.astype(jnp.float32) for item in totals[:3]]
-    owned = owned.astype(jnp.float32)
-    early = early.astype(jnp.float32)
-    key_at = width
-    value_at = key_at + KV_HEADS * HEAD_DIM
-    left_at = value_at + KV_HEADS * HEAD_DIM
-    d_normed = d_scaled + mul_t(d_left_low, full_left) + d_normed_sum
-    d_source_part, grad_anorm = norm_back(source, gain_anorm, d_normed)
-    d_source = d_scaled + d_source_part
-
-    small_grads = [grad_anorm, grad_apost, grad_lnorm, grad_fnorm, grad_fpost, grad_plpost]
-    parts = [item.reshape(HEADS, shard) for item in small_grads]
-    parts += [item.reshape(HEADS, piece) for item in (grad_qnorm, grad_knorm)]
-    parts = jnp.concatenate(parts, axis=1)
-    parts = jnp.pad(parts, ((0, 0), (0, -parts.shape[1] % 1024))).reshape(HEADS, -1, 128)
-    small_sums = gains_sum(parts, 13).reshape(-1)
-    own = [small_sums[i * shard : (i + 1) * shard] for i in range(len(small_grads))]
-    sum_anorm, sum_apost, sum_lnorm, sum_fnorm, sum_fpost, sum_plpost = own
-    sum_qnorm = small_sums[at : at + piece]
-    sum_knorm = small_sums[at + piece : at + 2 * piece]
+    sum_anorm, sum_apost, sum_lnorm, sum_fnorm, sum_fpost, sum_plpost = gain_sums[:6]
+    sum_qnorm, sum_knorm = [
+        lax.dynamic_slice_in_dim(item, index * piece, piece) for item in gain_sums[6:]
+    ]
+
+    def owned_part(start, size):
+        return owned[:, start : start + size].astype(jnp.float32)
+
+    keys = KV_HEADS * HEAD_DIM
+    value_at = width + keys
+    left_at = value_at + keys
     return (
         result,
-        low(d_source),
+        d_source,
         d_extra,
         sum_anorm,
-        owned[:, :width],
-        owned[:, key_at:value_at],
-        owned[:, value_at:left_at],
+        owned_part(0, width),
+        owned_part(width, keys),
+        owned_part(value_at, keys),
         sum_qnorm,
         sum_knorm,
-        early[:, :width],
+        early[:, :width].astype(jnp.float32),
         sum_apost,
-        owned[:, left_at : left_at + rank],
-        owned[:, left_at + rank :],
+        owned_part(left_at, rank),
+        owned_part(left_at + rank, rank),
         sum_lnorm,
         sum_fnorm,
         sum_gate,
         sum_up,
         sum_down,
         sum_fpost,
-        early[:, width:],
+        early[:, width:].astype(jnp.float32),
         sum_plproj.astype(jnp.float32),
         sum_plpost,
     )

time: 582 us -> 541 us (0.930)
  Pallas kernels: 499 us -> 481 us
  other arithmetic: 37.2 us -> 28 us
  local copies, waits for them, and re-layouts: 28.3 us -> 20.2 us
    pallas_call x3 -> x1, Pallas kernels: 143 us -> 121 us  [attention_forward(): pl.pallas_call(functools.partial(attention_kernel, count), out_shape=[jax...]
    slice x8 -> x1, local copies, waits for them, and re-layouts: 8.76 us -> 0.85 us  [head_plan(): wide_gains[4:6]]
    convert_element_type x1 -> x6, other arithmetic: 0.01 us -> 7.66 us  [the longest x3 3.66 us: owned_part(): return owned[:, start:start + size].astype(jnp.float32)]
    reduce_sum x5 -> x0, other arithmetic: 6.29 us -> none  [the longest x2 4.91 us: norm_rows(): value * lax.rsqrt(jnp.mean(value * value, axis=-1, keepdims=True) + EPS)]
    unnamed x72 -> x60, local copies, waits for them, and re-layouts: 11.2 us -> 14.9 us
where the time goes in v5:
time: 541 us; the launch traced here: 534 us
  Pallas kernels  481 us (89%)
  other arithmetic  28 us (5%)
  local copies, waits for them, and re-layouts  20.2 us (4%)
    pallas_call x1, Pallas kernels, attention_back(): pl.pallas_call(attention_back_kernel, out_shape=[jax.ShapeDtypeStruct((ro...  152 us
    pallas_call x1, Pallas kernels, attention_forward(): pl.pallas_call(functools.partial(attention_kernel, count), out_shape=[jax...  121 us
    pallas_call x1, Pallas kernels, ffn_back(): pl.pallas_call(ffn_back_kernel, out_shape=[jax.ShapeDtypeStruct((rows, wi...  121 us
    pallas_call x1, Pallas kernels, ffn_forward(): pl.pallas_call(ffn_kernel, out_shape=[jax.ShapeDtypeStruct((rows, width),...  87.6 us
    unnamed x60, local copies, waits for them, and re-layouts  14.9 us
    convert_element_type x3, other arithmetic, head_plan(): item.astype(jnp.float32)  13.3 us

profile of v5, /device:TPU:0, one launch (start us, length us, event | category | flops | bytes accessed | tf_op | source)
XLA Modules:
  0.0 534.0 jit_solution(1736233312540866346)
XLA Ops:
  0.7 1.3 fusion.2
  4.2 0.9 dynamic-update-slice
  5.0 0.8 dynamic-update-slice.1
  5.9 0.8 dynamic-update-slice.2
  6.7 0.8 dynamic-update-slice.3
  7.5 0.8 dynamic-update-slice.4
  8.4 0.8 dynamic-update-slice.5
  9.6 0.9 copy.46
  10.5 0.9 copy.47
  11.4 1.0 pad_maximum_fusion.1.small_ref
  12.4 1.1 pad_maximum_fusion.kv_ref
  13.5 121.2 %shard_map.399 = (f32[128,2048]{1,0:T(8,128)S(1)}, f32[8,2048]{1,0:T(8,128)S(1)}, bf16[2048,384]{1,0:T(8,128)(2,1)}, bf16[256,2048]{1,0:T(8,128)(2,1)}, bf16[102...) custom-call(bf16[128,2048]{1,0:T(8,128)(2,1)S(1)} %copy-done.1, ...), custom_call_target="tpu_custom_call" | custom-call | tf_op jit(solution)/shard_map/pallas_call | solution.py:685
  134.9 0.9 slice.47.gains_ref
  135.8 1.7 convolution_convert_fusion.left_low_ref
  137.5 1.5 multiply_reduce_fusion.1
  139.8 1.1 multiply_convert_fusion
  140.9 87.6 %shard_map.400 = (f32[128,2048]{1,0:T(8,128)S(1)}, bf16[1024,2048]{1,0:T(8,128)(2,1)}, bf16[1024,1024]{1,0:T(8,128)(2,1)S(1)}, bf16[1024,1024]{1,0:T(8,128)(2,1)S(1)}, bf16[1024,1024]{1,0:T(8,128)(2,1)}) custom-call(bf16[128,2048]{1,0:T(8,128)(2,1)S(1)} %get-tuple-element.128.own_ref, bf16[1024,2048]{1,0:T(8,128)(2,1)} %gate_any.3, ...), custom_call_target="tpu_custom_call" | custom-call | tf_op jit(solution)/shard_map/pallas_call | solution.py:806
  228.6 1.3 copy-done.2
  229.9 1.3 copy-done.3
  231.2 1.0 copy-done.4
  232.2 120.7 %shard_map.401 = (f32[128,2048]{1,0:T(8,128)}, bf16[128,2048]{1,0:T(8,128)(2,1)}, bf16[128,256]{1,0:T(8,128)(2,1)}, f32[128,2048]{1,0:T(8,128)}, f32[2,2048]{1,0...) custom-call(f32[128,2048]{1,0:T(8,128)} %get-tuple-element.129.first, ...), custom_call_target="tpu_custom_call" | custom-call | tf_op jit(solution)/shard_map/pallas_call | solution.py:1180
  352.9 151.7 %shard_map.402 = (bf16[128,2048]{1,0:T(8,128)(2,1)}, bf16[256,3200]{1,0:T(8,128)(2,1)}, bf16[256,2304]{1,0:T(8,128)(2,1)}, bf16[32,2048]{1,0:T(8,128)(2,1)}, f32...) custom-call(bf16[128,2048]{1,0:T(8,128)(2,1)} %hidden_ref.3, ...), custom_call_target="tpu_custom_call" | custom-call | tf_op jit(solution)/shard_map/pallas_call | solution.py:1724
  504.6 1.6 fusion.16
  507.3 1.6 convert_element_type.76
  508.9 1.7 slice_convert_fusion.4
  510.7 1.0 slice_convert_fusion.5
  513.1 1.6 slice_convert_fusion
  514.7 1.1 slice_convert_fusion.2
  515.8 1.6 slice_convert_fusion.1
  518.0 4.4 convert_element_type.72
  522.4 4.4 convert_element_type.73
  526.9 4.4 convert_element_type.74
  (68 shorter events, 8.9 us)
Async XLA Ops:
  0.7 12.8 %copy-start.1 = (bf16[128,2048]{1,0:T(8,128)(2,1)S(1)}, bf16[128,2048]{1,0:T(8,128)(2,1)}, u32[]{:S(2)}) copy-start(bf16[128,2048]{1,0:T(8,128)(2,1)} %hidden_ref.3) | copy-start | bytes 1572868
  0.7 12.8 %copy-start.12 = (bf16[32,2048]{1,0:T(8,128)(2,1)S(1)}, bf16[32,2048]{1,0:T(8,128)(2,1)}, u32[]{:S(2)}) copy-start(bf16[32,2048]{1,0:T(8,128)(2,1)} %pl_proj_ref.1) | copy-start | bytes 393220
  134.7 4.4 copy-start.5
  134.7 4.4 copy-start.6
  134.7 4.4 copy-start.7
  134.7 4.4 copy-start.8
  134.7 4.4 copy-start.9
  134.7 4.4 copy-start.10
  134.7 4.4 copy-start.11
  134.7 4.4 copy-start
  137.5 2.3 copy-start.21
  139.1 1.8 copy-start.13
  228.6 1.3 copy-start.2
  229.9 1.3 copy-start.3
  231.2 1.0 copy-start.4
  504.6 8.6 %copy-start.18 = (bf16[256,2304]{1,0:T(8,128)(2,1)S(1)}, bf16[256,2304]{1,0:T(8,128)(2,1)}, u32[]{:S(2)}) copy-start(bf16[256,2304]{1,0:T(8,128)(2,1)} %get-tuple-element.95) | copy-start | bytes 3538948
  508.9 5.7 %copy-start.17 = (bf16[256,3200]{1,0:T(8,128)(2,1)S(1)}, bf16[256,3200]{1,0:T(8,128)(2,1)}, u32[]{:S(2)}) copy-start(bf16[256,3200]{1,0:T(8,128)(2,1)} %get-tuple-element.94) | copy-start | bytes 4915204
  514.7 3.3 copy-start.16
  518.0 4.5 copy-start.15
  522.4 4.5 copy-start.14
  526.9 4.5 copy-start.19
  526.9 5.3 copy-start.20
  531.3 1.6 copy-start.22
